TPU v7x, 32 devices: a whole 2x2x4 slice. The times are simulated.
32 devices in a mesh: wide: 8 (over y, x, core), narrow: 4 (over z).
Axes of the slice: x: 2, y: 2, z: 4, core: 2. Of those that a mesh axis runs over, the one named last changes fastest.
Arguments:
- token_ids: int32 [2, 32, 384], P(None, ('wide', 'narrow')), may hold values from 0 to 30591
- seq_lengths: int32 [2, 32], P(None, ('wide', 'narrow')), may hold values from 24 to 384, as said below
- mlm_slots: int32 [2, 32, 56], P(None, ('wide', 'narrow')), may hold values from 0 to 383
- mlm_labels: int32 [2, 32, 56], P(None, ('wide', 'narrow')), may hold values from 0 to 30591
- nsp_labels: int32 [2, 32], P(None, ('wide', 'narrow')), may hold values from 0 to 1
- table_master: float32 [30592, 768], P(('wide', 'narrow')), may hold values from -0.375 to 0.375
- table_first: float32 [30592, 768], P(('wide', 'narrow')), may hold values from -2.3841858e-06 to 2.3841858e-06
- table_second: float32 [30592, 768], P(('wide', 'narrow')), may hold values from 6.2315795e-15 to 9.970527e-14
- position_master: float32 [384, 768], P(None, ('wide', 'narrow')), may hold values from -0.375 to 0.375
- position_first: float32 [384, 768], P(None, ('wide', 'narrow')), may hold values from -2.3841858e-06 to 2.3841858e-06
- position_second: float32 [384, 768], P(None, ('wide', 'narrow')), may hold values from 6.2315795e-15 to 9.970527e-14
- pair_master: float32 [2, 768, 2], P(None, ('wide', 'narrow')), may hold values from -0.75 to 0.75
- pair_first: float32 [2, 768, 2], P(None, ('wide', 'narrow')), may hold values from -2.3841858e-06 to 2.3841858e-06
- pair_second: float32 [2, 768, 2], P(None, ('wide', 'narrow')), may hold values from 6.2315795e-15 to 9.970527e-14
- input_master: float32 [768, 2304], P(('wide', 'narrow')), may hold values from -0.21875 to 0.21875
- input_first: float32 [768, 2304], P(('wide', 'narrow')), may hold values from -2.3841858e-06 to 2.3841858e-06
- input_second: float32 [768, 2304], P(('wide', 'narrow')), may hold values from 6.2315795e-15 to 9.970527e-14
- output_master: float32 [768, 768], P(('wide', 'narrow')), may hold values from -0.875 to 0.875
- output_first: float32 [768, 768], P(('wide', 'narrow')), may hold values from -2.3841858e-06 to 2.3841858e-06
- output_second: float32 [768, 768], P(('wide', 'narrow')), may hold values from 6.2315795e-15 to 9.970527e-14
- dense_master: float32 [2, 768, 768], P(None, ('wide', 'narrow')), may hold values from -0.21875 to 0.21875
- dense_first: float32 [2, 768, 768], P(None, ('wide', 'narrow')), may hold values from -2.3841858e-06 to 2.3841858e-06
- dense_second: float32 [2, 768, 768], P(None, ('wide', 'narrow')), may hold values from 6.2315795e-15 to 9.970527e-14
- feed_master: float32 [2, 768, 3072], P(None, ('wide', 'narrow')), may hold values from -0.21875 to 0.21875
- feed_first: float32 [2, 768, 3072], P(None, ('wide', 'narrow')), may hold values from -2.3841858e-06 to 2.3841858e-06
- feed_second: float32 [2, 768, 3072], P(None, ('wide', 'narrow')), may hold values from 6.2315795e-15 to 9.970527e-14
- vector_master: float32 [44416], P(('wide', 'narrow')), may hold values from -1.75 to 2.4
- vector_first: float32 [44416], P(('wide', 'narrow')), may hold values from -9.536743e-06 to 9.536743e-06
- vector_second: float32 [44416], P(('wide', 'narrow')), may hold values from 9.970527e-14 to 1.5952843e-12
Outputs:
- masked_sums: float32 [2], replicated
- pair_sum: float32 [], replicated
- grad_norm: float32 [], replicated
- table_new: float32 [30592, 768], P(('wide', 'narrow'))
- table_first_new: float32 [30592, 768], P(('wide', 'narrow'))
- table_second_new: float32 [30592, 768], P(('wide', 'narrow'))
- position_new: float32 [384, 768], P(None, ('wide', 'narrow'))
- position_first_new: float32 [384, 768], P(None, ('wide', 'narrow'))
- position_second_new: float32 [384, 768], P(None, ('wide', 'narrow'))
- pair_new: float32 [2, 768, 2], P(None, ('wide', 'narrow'))
- pair_first_new: float32 [2, 768, 2], P(None, ('wide', 'narrow'))
- pair_second_new: float32 [2, 768, 2], P(None, ('wide', 'narrow'))
- input_new: float32 [768, 2304], P(('wide', 'narrow'))
- input_first_new: float32 [768, 2304], P(('wide', 'narrow'))
- input_second_new: float32 [768, 2304], P(('wide', 'narrow'))
- output_new: float32 [768, 768], P(('wide', 'narrow'))
- output_first_new: float32 [768, 768], P(('wide', 'narrow'))
- output_second_new: float32 [768, 768], P(('wide', 'narrow'))
- dense_new: float32 [2, 768, 768], P(None, ('wide', 'narrow'))
- dense_first_new: float32 [2, 768, 768], P(None, ('wide', 'narrow'))
- dense_second_new: float32 [2, 768, 768], P(None, ('wide', 'narrow'))
- feed_new: float32 [2, 768, 3072], P(None, ('wide', 'narrow'))
- feed_first_new: float32 [2, 768, 3072], P(None, ('wide', 'narrow'))
- feed_second_new: float32 [2, 768, 3072], P(None, ('wide', 'narrow'))
- vector_new: float32 [44416], P(('wide', 'narrow'))
- vector_first_new: float32 [44416], P(('wide', 'narrow'))
- vector_second_new: float32 [44416], P(('wide', 'narrow'))
Inputs may be any that keep to these rules, and one draw needn't show every extreme that they name: `seq_lengths`: in each micro-batch one sequence, drawn from the seed, has length 384.
All inputs are finite; a program needn't handle non-finite values.
Results may differ from a plain program's by a relative error of at most 0.007.
The roundings to bfloat16 on the way count: a program that leaves them out, or rounds other values in their place, can miss the bound.
Values may be sent and summed in bfloat16 or wider, within the bound.
No kernel may reach another device: no remote copies, remote signals or barrier semaphores. Data moves between devices by JAX's collectives and lax.ppermute only.
A program may use at most 960 MiB of HBM per device.

v0:
```python
from functools import partial

import jax
import jax.numpy as jnp
from jax import lax
from jax.sharding import PartitionSpec as P

D = 768
HEAD = 64
FF = 3072
STEP_COUNT = 10


NORM_EPS = 1e-12
CLIP_NORM = 0.02
BETA_ONE = 0.9
BETA_TWO = 0.999
ADAM_EPS = 1e-08
DECAY_RATE = 0.01
LEARN_RATE = 0.1
MASKED_FILL = -1000000000.0


def product(left, right):
    return jnp.dot(left, right, preferred_element_type=jnp.float32)


def product_right(left, right):
    return lax.dot_general(
        left, right, (((1,), (1,)), ((), ())), preferred_element_type=jnp.float32
    )


def product_left(left, right):
    return lax.dot_general(
        left, right, (((0,), (0,)), ((), ())), preferred_element_type=jnp.float32
    )


def norm_forward(values, gain, shift):
    average = jnp.mean(values, axis=-1, keepdims=True)
    centered = values - average
    spread = jnp.mean(centered * centered, axis=-1, keepdims=True)
    inverse = lax.rsqrt(spread + NORM_EPS)
    normal = centered * inverse
    return (normal * gain + shift, (normal, inverse))


def norm_backward(grad, saved, gain):
    normal, inverse = saved
    scaled = grad * gain
    inner = (
        scaled
        - jnp.mean(scaled, axis=-1, keepdims=True)
        - normal * jnp.mean(scaled * normal, axis=-1, keepdims=True)
    )
    return (inner * inverse, jnp.sum(grad * normal, axis=0), jnp.sum(grad, axis=0))


def gelu_exact(values):
    return jax.nn.gelu(values, approximate=False)


def gelu_back(values, grad):
    return jax.vjp(gelu_exact, values)[1](grad)[0]


def split_vectors(vectors):
    extents = [D] * 11 + [FF] + [D] * 3
    pieces = []
    start = 0
    for extent in extents:
        pieces.append(vectors[start : start + extent])
        start += extent
    pieces.append(vectors[start:])
    return pieces


def to_heads(values):
    return jnp.moveaxis(values.reshape(values.shape[0], -1, 2, HEAD), 1, 0)


def from_heads(values):
    moved = jnp.moveaxis(values, 0, 1)
    return moved.reshape(moved.shape[0], -1)


def attend_forward(alive, scale, group):
    queries, keys, values = group
    raw = jnp.einsum("qhd,khd->hqk", queries, keys, preferred_element_type=jnp.float32) * scale
    scores = jnp.where(alive, raw, MASKED_FILL)
    top = jnp.max(scores, axis=-1, keepdims=True)
    expo = jnp.exp(scores - top)
    total = jnp.sum(expo, axis=-1, keepdims=True)
    attention = (expo / total).astype(jnp.bfloat16)
    context = jnp.einsum("hqk,khd->qhd", attention, values, preferred_element_type=jnp.float32)
    return (context, (top + jnp.log(total))[..., 0])


def attend_backward(alive, scale, group):
    queries, keys, values, grad_context, log_total = group
    raw = jnp.einsum("qhd,khd->hqk", queries, keys, preferred_element_type=jnp.float32) * scale
    scores = jnp.where(alive, raw, MASKED_FILL)
    attention = jnp.exp(scores - log_total[..., None])
    grad_attention = jnp.einsum(
        "qhd,khd->hqk", grad_context, values, preferred_element_type=jnp.float32
    )
    grad_scores = attention * (
        grad_attention - jnp.sum(grad_attention * attention, axis=-1, keepdims=True)
    )
    grad_raw = grad_scores.astype(jnp.bfloat16) * scale
    grad_queries = jnp.einsum("hqk,khd->qhd", grad_raw, keys, preferred_element_type=jnp.float32)
    grad_keys = jnp.einsum("hqk,qhd->khd", grad_raw, queries, preferred_element_type=jnp.float32)
    grad_values = jnp.einsum(
        "hqk,qhd->khd",
        attention.astype(jnp.bfloat16),
        grad_context,
        preferred_element_type=jnp.float32,
    )
    return (grad_queries, grad_keys, grad_values)


def train_sequence(weights, token_row, length, slots, labels, pair_label, inv_count, inv_seqs):
    table, position, pair_cols, input_proj, output_proj, dense_pair, feed_pair, vectors = weights
    parts = split_vectors(vectors.astype(jnp.float32))
    width = input_proj.shape[0]
    tokens = token_row.shape[0]
    places = jnp.arange(tokens, dtype=jnp.int32)
    second = places >= length // 2
    type_cols = pair_cols[0].astype(jnp.float32)
    embedded = (
        table[token_row].astype(jnp.float32)
        + position.astype(jnp.float32)
        + jnp.where(second[:, None], type_cols[:, 1], type_cols[:, 0])
    )
    normed, saved_zero = norm_forward(embedded, parts[0], parts[1])
    normed_low = normed.astype(jnp.bfloat16)
    bias_mixed = jnp.concatenate([parts[8], jnp.zeros((width,), jnp.float32), parts[9]])
    mixed = (product(normed_low, input_proj) + bias_mixed).astype(jnp.bfloat16)
    queries = to_heads(mixed[:, :width])
    keys = to_heads(mixed[:, width : 2 * width])
    values = to_heads(mixed[:, 2 * width :])
    alive = places[None, None, :] < length
    scale = HEAD ** (-0.5)
    contexts, log_totals = lax.map(partial(attend_forward, alive, scale), (queries, keys, values))
    context_low = from_heads(contexts).astype(jnp.bfloat16)
    branch = product(context_low, output_proj) + parts[10]
    hidden_one, saved_one = norm_forward(normed + branch, parts[2], parts[3])
    one_low = hidden_one.astype(jnp.bfloat16)
    inner = product(one_low, feed_pair[0]) + parts[11]
    active_low = gelu_exact(inner).astype(jnp.bfloat16)
    outer = product_right(active_low, feed_pair[1]) + parts[12]
    hidden_two, saved_two = norm_forward(hidden_one + outer, parts[4], parts[5])
    picked_low = hidden_two[slots].astype(jnp.bfloat16)
    transform = product(picked_low, dense_pair[0]) + parts[13]
    head_out, saved_head = norm_forward(gelu_exact(transform), parts[6], parts[7])
    head_low = head_out.astype(jnp.bfloat16)
    logits = product_right(head_low, table) + parts[15]
    top = jnp.max(logits, axis=-1, keepdims=True)
    log_total = top + jnp.log(jnp.sum(jnp.exp(logits - top), axis=-1, keepdims=True))
    vocab_hit = jnp.arange(logits.shape[1], dtype=jnp.int32)[None, :] == labels[:, None]
    target = jnp.sum(jnp.where(vocab_hit, logits, 0.0), axis=-1)
    counted = (slots < length).astype(jnp.float32)
    masked_sum = jnp.sum(counted * (log_total[:, 0] - target))
    first_low = hidden_two[0:1].astype(jnp.bfloat16)
    pooled = jnp.tanh(product(first_low, dense_pair[1]) + parts[14])
    pooled_low = pooled.astype(jnp.bfloat16)
    pair_logits = product(pooled_low, pair_cols[1])
    pair_top = jnp.max(pair_logits, axis=-1, keepdims=True)
    pair_total = pair_top + jnp.log(
        jnp.sum(jnp.exp(pair_logits - pair_top), axis=-1, keepdims=True)
    )
    pair_hit = jnp.arange(2, dtype=jnp.int32)[None, :] == pair_label
    pair_loss = pair_total[0, 0] - jnp.sum(jnp.where(pair_hit, pair_logits, 0.0))
    grad_logits = (
        (jnp.exp(logits - log_total) - vocab_hit.astype(jnp.float32))
        * (counted * inv_count)[:, None]
    ).astype(jnp.bfloat16)
    grad_table = product_left(grad_logits, head_low)
    grad_vocab_bias = jnp.sum(grad_logits.astype(jnp.float32), axis=0)
    grad_head, grad_head_gain, grad_head_shift = norm_backward(
        product(grad_logits, table), saved_head, parts[6]
    )
    grad_transform = gelu_back(transform, grad_head).astype(jnp.bfloat16)
    grad_dense_zero = product_left(picked_low, grad_transform)
    grad_transform_bias = jnp.sum(grad_transform.astype(jnp.float32), axis=0)
    grad_two = (
        jnp.zeros(hidden_two.shape, jnp.float32)
        .at[slots]
        .add(product_right(grad_transform, dense_pair[0]))
    )
    grad_pair_logits = (
        (jnp.exp(pair_logits - pair_total) - pair_hit.astype(jnp.float32)) * inv_seqs
    ).astype(jnp.bfloat16)
    grad_classifier = product_left(pooled_low, grad_pair_logits)
    grad_pooled = product_right(grad_pair_logits, pair_cols[1])
    grad_pool_pre = (grad_pooled * (1.0 - pooled * pooled)).astype(jnp.bfloat16)
    grad_pooler = product_left(first_low, grad_pool_pre)
    grad_pool_bias = jnp.sum(grad_pool_pre.astype(jnp.float32), axis=0)
    grad_two = grad_two.at[0].add(product_right(grad_pool_pre, dense_pair[1])[0])
    grad_sum_two, grad_feed_gain, grad_feed_shift = norm_backward(grad_two, saved_two, parts[4])
    grad_outer = grad_sum_two.astype(jnp.bfloat16)
    grad_feed_out = product_left(grad_outer, active_low)
    grad_outer_bias = jnp.sum(grad_outer.astype(jnp.float32), axis=0)
    grad_inner = gelu_back(inner, product(grad_outer, feed_pair[1])).astype(jnp.bfloat16)
    grad_feed_in = product_left(one_low, grad_inner)
    grad_inner_bias = jnp.sum(grad_inner.astype(jnp.float32), axis=0)
    grad_one = grad_sum_two + product_right(grad_inner, feed_pair[0])
    grad_sum_one, grad_attend_gain, grad_attend_shift = norm_backward(grad_one, saved_one, parts[2])
    grad_branch = grad_sum_one.astype(jnp.bfloat16)
    grad_output = product_left(context_low, grad_branch)
    grad_branch_bias = jnp.sum(grad_branch.astype(jnp.float32), axis=0)
    grad_context = to_heads(product_right(grad_branch, output_proj).astype(jnp.bfloat16))
    grad_queries, grad_keys, grad_values = lax.map(
        partial(attend_backward, alive, scale), (queries, keys, values, grad_context, log_totals)
    )
    grad_mixed = jnp.concatenate(
        [from_heads(grad_queries), from_heads(grad_keys), from_heads(grad_values)], axis=1
    ).astype(jnp.bfloat16)
    grad_input = product_left(normed_low, grad_mixed)
    grad_mixed_bias = jnp.sum(grad_mixed.astype(jnp.float32), axis=0)
    grad_normed = grad_sum_one + product_right(grad_mixed, input_proj)
    grad_embedded, grad_embed_gain, grad_embed_shift = norm_backward(
        grad_normed, saved_zero, parts[0]
    )
    grad_table = grad_table.at[token_row].add(grad_embedded)
    grad_type = jnp.stack(
        [
            jnp.sum(jnp.where(second[:, None], 0.0, grad_embedded), axis=0),
            jnp.sum(jnp.where(second[:, None], grad_embedded, 0.0), axis=0),
        ],
        axis=1,
    )
    grad_vectors = jnp.concatenate(
        [
            grad_embed_gain,
            grad_embed_shift,
            grad_attend_gain,
            grad_attend_shift,
            grad_feed_gain,
            grad_feed_shift,
            grad_head_gain,
            grad_head_shift,
            grad_mixed_bias[:width],
            grad_mixed_bias[2 * width :],
            grad_branch_bias,
            grad_inner_bias,
            grad_outer_bias,
            grad_transform_bias,
            grad_pool_bias,
            grad_vocab_bias,
        ]
    )
    grads = (
        grad_table,
        grad_embedded,
        jnp.stack([grad_type, grad_classifier]),
        grad_input,
        grad_output,
        jnp.stack([grad_dense_zero, grad_pooler]),
        jnp.stack([grad_feed_in, grad_feed_out]),
        grad_vectors,
    )
    return (grads, masked_sum, pair_loss)


def shards(
    token_ids,
    seq_lengths,
    mlm_slots,
    mlm_labels,
    nsp_labels,
    table_master,
    table_first,
    table_second,
    position_master,
    position_first,
    position_second,
    pair_master,
    pair_first,
    pair_second,
    input_master,
    input_first,
    input_second,
    output_master,
    output_first,
    output_second,
    dense_master,
    dense_first,
    dense_second,
    feed_master,
    feed_first,
    feed_second,
    vector_master,
    vector_first,
    vector_second,
):
    masters = (
        table_master,
        position_master,
        pair_master,
        input_master,
        output_master,
        dense_master,
        feed_master,
        vector_master,
    )
    firsts = (
        table_first,
        position_first,
        pair_first,
        input_first,
        output_first,
        dense_first,
        feed_first,
        vector_first,
    )
    seconds = (
        table_second,
        position_second,
        pair_second,
        input_second,
        output_second,
        dense_second,
        feed_second,
        vector_second,
    )
    micro = token_ids.shape[0]
    counted = (mlm_slots < seq_lengths[:, :, None]).astype(jnp.float32)
    local_count = jnp.sum(counted).reshape(1).astype(jnp.bfloat16)
    gathered = (
        lax.all_gather(table_master.astype(jnp.bfloat16), ("wide", "narrow"), axis=0, tiled=True),
        lax.all_gather(
            position_master.astype(jnp.bfloat16), ("wide", "narrow"), axis=1, tiled=True
        ),
        lax.all_gather(pair_master.astype(jnp.bfloat16), ("wide", "narrow"), axis=1, tiled=True),
        lax.all_gather(input_master.astype(jnp.bfloat16), ("wide", "narrow"), axis=0, tiled=True),
        lax.all_gather(output_master.astype(jnp.bfloat16), ("wide", "narrow"), axis=0, tiled=True),
        lax.all_gather(dense_master.astype(jnp.bfloat16), ("wide", "narrow"), axis=1, tiled=True),
        lax.all_gather(feed_master.astype(jnp.bfloat16), ("wide", "narrow"), axis=1, tiled=True),
        lax.all_gather(vector_master.astype(jnp.bfloat16), ("wide", "narrow"), axis=0, tiled=True),
        lax.all_gather(local_count, ("wide", "narrow"), axis=0, tiled=True),
    )
    weights = gathered[:8]
    masked_count = jnp.sum(gathered[8].astype(jnp.float32))
    inv_count = 1.0 / masked_count
    inv_seqs = 1.0 / (micro * lax.axis_size(("wide", "narrow")) * token_ids.shape[1])
    summed = None
    masked_local = jnp.zeros((), jnp.float32)
    pair_local = jnp.zeros((), jnp.float32)
    for index in range(micro):
        grads, masked_sum, pair_loss = train_sequence(
            weights,
            token_ids[index, 0],
            seq_lengths[index, 0],
            mlm_slots[index, 0],
            mlm_labels[index, 0],
            nsp_labels[index, 0],
            inv_count,
            inv_seqs,
        )
        grads = (
            lax.psum_scatter(grads[0], ("wide", "narrow"), scatter_dimension=0, tiled=True),
            lax.psum_scatter(grads[1], ("wide", "narrow"), scatter_dimension=1, tiled=True),
            lax.psum_scatter(grads[2], ("wide", "narrow"), scatter_dimension=1, tiled=True),
            lax.psum_scatter(grads[3], ("wide", "narrow"), scatter_dimension=0, tiled=True),
            lax.psum_scatter(grads[4], ("wide", "narrow"), scatter_dimension=0, tiled=True),
            lax.psum_scatter(grads[5], ("wide", "narrow"), scatter_dimension=1, tiled=True),
            lax.psum_scatter(grads[6], ("wide", "narrow"), scatter_dimension=1, tiled=True),
            lax.psum_scatter(grads[7], ("wide", "narrow"), scatter_dimension=0, tiled=True),
        )
        summed = (
            grads
            if summed is None
            else tuple((older + newer for older, newer in zip(summed, grads)))
        )
        masked_local = masked_local + masked_sum
        pair_local = pair_local + pair_loss
    squares = sum((jnp.sum(item * item) for item in summed))
    masked_total, pair_total = lax.psum((masked_local, pair_local), ("wide", "narrow"))
    norm_square = lax.psum(squares, ("wide", "narrow"))
    norm = jnp.sqrt(norm_square)
    factor = CLIP_NORM / (norm + 1e-06)
    correct_one = 1.0 - BETA_ONE**STEP_COUNT
    correct_two = 1.0 - BETA_TWO**STEP_COUNT
    updated = []
    for number in range(8):
        grad = summed[number] * factor
        moment_one = BETA_ONE * firsts[number] + (1.0 - BETA_ONE) * grad
        moment_two = BETA_TWO * seconds[number] + (1.0 - BETA_TWO) * grad * grad
        direction = moment_one / correct_one / (jnp.sqrt(moment_two / correct_two) + ADAM_EPS)
        decay = DECAY_RATE if number < 7 else 0.0
        updated.extend(
            [
                masters[number] - LEARN_RATE * (direction + decay * masters[number]),
                moment_one,
                moment_two,
            ]
        )
    masked_sums = jnp.stack([masked_total, masked_count])
    return (masked_sums, pair_total, norm) + tuple(updated)


def solution(mesh):
    placed = (
        P(None, ("wide", "narrow"), None),
        P(None, ("wide", "narrow")),
        P(None, ("wide", "narrow"), None),
        P(None, ("wide", "narrow"), None),
        P(None, ("wide", "narrow")),
        P(("wide", "narrow"), None),
        P(("wide", "narrow"), None),
        P(("wide", "narrow"), None),
        P(None, ("wide", "narrow")),
        P(None, ("wide", "narrow")),
        P(None, ("wide", "narrow")),
        P(None, ("wide", "narrow"), None),
        P(None, ("wide", "narrow"), None),
        P(None, ("wide", "narrow"), None),
        P(("wide", "narrow"), None),
        P(("wide", "narrow"), None),
        P(("wide", "narrow"), None),
        P(("wide", "narrow"), None),
        P(("wide", "narrow"), None),
        P(("wide", "narrow"), None),
        P(None, ("wide", "narrow"), None),
        P(None, ("wide", "narrow"), None),
        P(None, ("wide", "narrow"), None),
        P(None, ("wide", "narrow"), None),
        P(None, ("wide", "narrow"), None),
        P(None, ("wide", "narrow"), None),
        P(("wide", "narrow")),
        P(("wide", "narrow")),
        P(("wide", "narrow")),
    )
    return jax.shard_map(
        shards,
        mesh=mesh,
        in_specs=placed,
        out_specs=(
            P(),
            P(),
            P(),
            P(("wide", "narrow"), None),
            P(("wide", "narrow"), None),
            P(("wide", "narrow"), None),
            P(None, ("wide", "narrow")),
            P(None, ("wide", "narrow")),
            P(None, ("wide", "narrow")),
            P(None, ("wide", "narrow"), None),
            P(None, ("wide", "narrow"), None),
            P(None, ("wide", "narrow"), None),
            P(("wide", "narrow"), None),
            P(("wide", "narrow"), None),
            P(("wide", "narrow"), None),
            P(("wide", "narrow"), None),
            P(("wide", "narrow"), None),
            P(("wide", "narrow"), None),
            P(None, ("wide", "narrow"), None),
            P(None, ("wide", "narrow"), None),
            P(None, ("wide", "narrow"), None),
            P(None, ("wide", "narrow"), None),
            P(None, ("wide", "narrow"), None),
            P(None, ("wide", "narrow"), None),
            P(("wide", "narrow")),
            P(("wide", "narrow")),
            P(("wide", "narrow")),
        ),
        check_vma=False,
    )
```

profile of v0, /device:TPU:0, one launch (start us, length us, event | category | flops | bytes accessed | tf_op | source)
XLA Modules:
  0.0 3658.9 jit_solution(1118060951177087716)
XLA Ops:
  23.5 42.0 %all-reduce.1 = bf16[32]{0:T(256)(128)(2,1)S(1)} all-reduce(bf16[32]{0:T(256)(128)(2,1)S(1)} %dynamic-update-slice.7), channel_id=1, replica_groups=mesh['wide'=8,'narrow'=4] {'wide','narrow'}, use_global_device_ids=true, to_apply=%add.1 | all-reduce | flops 32 | bytes 128
  68.0 69.5 %all_gather.29 = bf16[2,768,2]{2,0,1:T(2,128)(2,1)S(1)} all-gather(bf16[2,24,2]{2,0,1:T(2,128)(2,1)S(1)} %copy.164), channel_id=1, replica_groups=mesh['wide'=8,'narrow'=4] {'wide','narrow'}, dimensions={1}, use_global_device_ids=true | all-gather | bytes 6336 | tf_op jit(solution)/shard_map/all_gather | solution.py:336
  138.7 74.9 %all_gather.28 = bf16[384,768]{0,1:T(8,128)(2,1)S(1)} all-gather(bf16[384,24]{0,1:T(8,128)(2,1)S(1)} %convert_element_type.251), channel_id=1, replica_groups=mesh['wide'=8,'narrow'=4] {'wide','narrow'}, dimensions={1}, use_global_device_ids=true | all-gather | bytes 608256 | tf_op jit(solution)/shard_map/all_gather | solution.py:333
  219.1 189.5 %all-gather.15.cloned.1.call-done = bf16[32,956,768]{2,1,0:T(8,128)(2,1)} async-done(((bf16[1,956,768]{2,1,0:T(8,128)(2,1)}), bf16[32,956,768]{2,1,0:T(8,128)(2,1)}) %all-gather.15.cloned.1.call-update) | async-done | bytes 46989328 | tf_op jit(solution)/shard_map/all_gather | solution.py:332
  408.6 37.1 %reshape.762 = bf16[30592,768]{1,0:T(8,128)(2,1)} reshape(bf16[32,956,768]{2,1,0:T(8,128)(2,1)} %all-gather.15.cloned.1.call-done) | data formatting | bytes 93978624
  445.6 8.6 gather_fusion.2
  454.3 8.2 gather_fusion
  464.1 6.2 all-gather.7.cloned.1.call-done
  470.3 3.8 fusion.133
  480.2 24.9 while.58
  505.1 21.3 all-gather.9.cloned.1.call-done
  536.7 21.0 while.59
  560.5 50.7 %all-gather.11.cloned.1.call-done = bf16[2,768,3072]{2,1,0:T(8,128)(2,1)} async-done(((bf16[2,24,3072]{2,1,0:T(8,128)(2,1)}), bf16[2,768,3072]{2,1,0:T(8,128)(2,1)}) %all-gather.11.cloned.1.call-update) | async-done | bytes 9437200 | tf_op jit(solution)/shard_map/all_gather | solution.py:340
  611.2 15.3 multiply_convert_fusion.2
  631.7 14.2 multiply_convert_fusion.3
  650.4 20.3 all-gather.13.cloned.1.call-done
  693.1 27.2 fusion.271
  720.3 27.0 fusion.270
  747.3 4.8 select_reduce_fusion.1
  759.2 20.9 multiply_reduce_fusion.30
  781.2 5.9 convert_reduce_fusion.1
  787.0 20.3 convert_reduce_fusion.10
  832.1 4.0 convert_reduce_fusion.6
  836.1 8.9 convert_reduce_fusion.2
  849.0 6.2 convert_reduce_fusion.3
  855.3 4.2 convert_reduce_fusion.7
  874.2 89.5 %while.60 = (s32[]{:T(128)}, bf16[6,384,2,64]{1,3,2,0:T(8,128)(2,1)}, bf16[6,384,2,64]{1,3,2,0:T(8,128)(2,1)}, bf16[6,384,2,64]{1,3,2,0:T(8,128)(2,1)}, bf16[6,3...) while((s32[]{:T(128)}, ...), condition=%wide.region_51.52_spmd.clone, body=%wide.region_49.51_spmd.clone.sunk | while | flops 194644608 | bytes 18987928 | solution.py:214
  882.2 3.5 fusion.373
  897.0 3.5 fusion.373
  911.9 3.5 fusion.373
  915.4 3.5 fusion.372
  926.8 3.5 fusion.373
  930.3 3.5 fusion.372
  941.7 3.5 fusion.373
  956.6 3.5 fusion.373
  960.1 3.4 fusion.372
  966.4 89.6 %while.61 = (s32[]{:T(128)}, bf16[6,384,2,64]{1,3,2,0:T(8,128)(2,1)}, bf16[6,384,2,64]{1,3,2,0:T(8,128)(2,1)}, bf16[6,384,2,64]{1,3,2,0:T(8,128)(2,1)}, bf16[6,3...) while((s32[]{:T(128)}, ...), condition=%wide.region_65.66_spmd.clone, body=%wide.region_63.65_spmd.clone.sunk | while | flops 194644608 | bytes 18987928 | solution.py:214
  974.4 3.5 fusion.388
  977.9 3.5 fusion.387
  989.3 3.5 fusion.388
  992.8 3.4 fusion.387
  1004.3 3.5 fusion.388
  1019.2 3.5 fusion.388
  1022.7 3.5 fusion.387
  1034.1 3.5 fusion.388
  1037.7 3.5 fusion.387
  1049.1 3.5 fusion.388
  1059.9 3.8 convolution_add_fusion.10
  1064.1 5.1 multiply_reduce_fusion.8
  1093.9 4.4 fusion.180
  1098.4 5.4 convolution_add_fusion.2
  1104.5 33.6 fusion.228
  1138.1 51.7 %scatter_fusion = f32[30592,768]{1,0:T(8,128)} fusion(f32[30592,768]{1,0:T(8,128)} %fusion.228, s32[384]{0:T(512)S(1)} %copy-done.131, f32[384,768]{1,0:T(8,128)} %copy-done.25), kind=kCustom, calls=%fused_computation.5 | custom fusion | flops 294912 | bytes 3540480 | tf_op jit(solution)/shard_map/scatter-add | solution.py:226
  1189.8 33.6 fusion.229
  1223.4 51.8 %scatter_fusion.1 = f32[30592,768]{1,0:T(8,128)} fusion(f32[30592,768]{1,0:T(8,128)} %fusion.229, s32[384]{0:T(512)S(1)} %copy-done.129, f32[384,768]{1,0:T(8,128)} %copy-done.24), kind=kCustom, calls=%fused_computation.7 | custom fusion | flops 294912 | bytes 3540480 | tf_op jit(solution)/shard_map/scatter-add | solution.py:226
  1275.2 4.5 convolution_bitcast_fusion.10
  1285.4 5.4 convolution_bitcast_fusion.9
  1290.8 11.2 maximum_add_fusion
  1302.0 92.2 %add.716 = f32[30592,768]{1,0:T(8,128)} add(f32[30592,768]{1,0:T(8,128)} %scatter_fusion, f32[30592,768]{1,0:T(8,128)} %scatter_fusion.1) | non-fusion elementwise | flops 23494656 | bytes 281935872 | tf_op jit(solution)/shard_map/add | solution.py:375
  1394.3 2118.2 %fusion.8 = f32[960,768]{1,0:T(8,128)S(1)} fusion(f32[30592,768]{1,0:T(8,128)} %add.716), kind=kCustom, calls=%all-reduce-scatter | all-reduce-scatter fusion | flops 23592960 | bytes 96927744
  3517.4 47.5 %all-reduce.4 = f32[2,768,2]{1,2,0:T(2,128)S(1)} all-reduce(f32[2,768,2]{1,2,0:T(2,128)S(1)} %maximum_add_fusion.2), channel_id=12, replica_groups=mesh['wide'=8,'narrow'=4] {'wide','narrow'}, use_global_device_ids=true, to_apply=%region_76.77.clone | all-reduce | flops 3072 | bytes 24576
  3565.6 8.5 concatenate.27
  3592.2 42.6 %all-reduce.7 = (f32[1]{0:T(128)}, f32[]{:T(128)}, f32[]{:T(128)}) all-reduce(f32[1]{0:T(128)} %bitcast.33, f32[]{:T(128)S(6)} %add.653, f32[]{:T(128)S(6)} %add.674), channel_id=1, replica_groups=mesh['wide'=8,'narrow'=4] {'wide','narrow'}, use_global_device_ids=true, to_apply=%region_32.33 | all-reduce | flops 3 | bytes 24 | tf_op jit(solution)/shard_map/psum | solution.py:380
  3639.5 6.7 multiply_subtract_fusion
  (805 shorter events, 338.8 us)
Async XLA Ops:
  7.2 207.4 %all-reduce.12.cloned.1.call-start = ((), (), s32[]{:S(2)}) async-start(), calls=%async_computation.12 | async-start | bytes 180224
  8.9 399.6 %all-gather.15.cloned.1.call-start = ((), (), s32[]{:S(2)}) async-start(), calls=%async_computation.13 | async-start | bytes 48660480 | tf_op jit(solution)/shard_map/all_gather | solution.py:332
  12.1 53.9 %copy-start.180 = (f32[2,24,2]{1,2,0:T(2,128)S(1)}, f32[2,24,2]{1,2,0:T(2,128)}, u32[]{:S(2)}) copy-start(f32[2,24,2]{1,2,0:T(2,128)} %param.52) | copy-start | bytes 1156
  12.1 53.9 %copy-start.195 = (s32[2,1,56]{2,1,0:T(1,128)S(1)}, s32[2,1,56]{2,1,0:T(1,128)}, u32[]{:S(2)}) copy-start(s32[2,1,56]{2,1,0:T(1,128)} %param.44) | copy-start | bytes 1348
  12.2 54.4 %copy-start.190 = (s32[2,1]{0,1:T(1,128)S(1)}, s32[2,1]{0,1:T(1,128)}, u32[]{:S(2)}) copy-start(s32[2,1]{0,1:T(1,128)} %param.45) | copy-start | bytes 28
  12.2 55.6 %copy-start.187 = (s32[2,1,384]{2,1,0:T(1,128)S(1)}, s32[2,1,384]{2,1,0:T(1,128)}, u32[]{:S(2)}) copy-start(s32[2,1,384]{2,1,0:T(1,128)} %param.41) | copy-start | bytes 9220
  12.2 55.8 %copy-start.98 = (f32[384,24]{0,1:T(8,128)S(1)}, f32[384,24]{0,1:T(8,128)}, u32[]{:S(2)}) copy-start(f32[384,24]{0,1:T(8,128)} %param.49) | copy-start | bytes 110596
  12.2 458.1 %all-gather.7.cloned.1.call-start = ((), (), s32[]{:S(2)}) async-start(), calls=%async_computation.4 | async-start | bytes 3649536 | tf_op jit(solution)/shard_map/all_gather | solution.py:337
  13.7 512.8 %all-gather.9.cloned.1.call-start = ((), (), s32[]{:S(2)}) async-start(), calls=%async_computation.5 | async-start | bytes 1216512 | tf_op jit(solution)/shard_map/all_gather | solution.py:338
  14.4 596.8 %all-gather.11.cloned.1.call-start = ((), (), s32[]{:S(2)}) async-start(), calls=%async_computation.6 | async-start | bytes 9732096 | tf_op jit(solution)/shard_map/all_gather | solution.py:340
  15.2 655.5 %all-gather.13.cloned.1.call-start = ((), (), s32[]{:S(2)}) async-start(), calls=%async_computation.7 | async-start | bytes 2433024 | tf_op jit(solution)/shard_map/all_gather | solution.py:339
  15.9 3559.6 %all-reduce.14.cloned.1.call-start = ((), (), s32[]{:S(2)}) async-start(), calls=%async_computation.14 | async-start | bytes 2719744
  22.0 46.0 %copy-start.191 = (s32[56]{0:T(128)}, s32[56]{0:T(128)S(1)}, u32[]{:S(2)}) copy-start(s32[56]{0:T(128)S(1)} %get-tuple-element.680) | copy-start | bytes 676
  22.0 116.3 %copy-start.192 = (s32[56]{0:T(128)}, s32[56]{0:T(128)S(1)}, u32[]{:S(2)}) copy-start(s32[56]{0:T(128)S(1)} %get-tuple-element.681) | copy-start | bytes 676
  67.8 146.7 %copy-start.128 = (s32[384]{0:T(512)}, s32[384]{0:T(512)S(1)}, u32[]{:S(2)}) copy-start(s32[384]{0:T(512)S(1)} %get-tuple-element.483) | copy-start | bytes 4612
  67.8 146.7 %copy-start.130 = (s32[384]{0:T(512)}, s32[384]{0:T(512)S(1)}, u32[]{:S(2)}) copy-start(s32[384]{0:T(512)S(1)} %get-tuple-element.484) | copy-start | bytes 4612
  138.7 419.0 %copy-start.88 = (f32[768]{0:T(1024)}, f32[768]{0:T(1024)S(1)}, u32[]{:S(2)}) copy-start(f32[768]{0:T(1024)S(1)} %get-tuple-element.473) | copy-start | bytes 9220
  138.7 419.0 %copy-start.90 = (f32[768]{0:T(1024)}, f32[768]{0:T(1024)S(1)}, u32[]{:S(2)}) copy-start(f32[768]{0:T(1024)S(1)} %get-tuple-element.474) | copy-start | bytes 9220
  213.9 343.9 %copy-start.13 = (bf16[384,768]{1,0:T(8,128)(2,1)}, bf16[384,768]{1,0:T(8,128)(2,1)S(1)}, u32[]{:S(2)}) copy-start(bf16[384,768]{1,0:T(8,128)(2,1)S(1)} %copy.163) | copy-start | bytes 1769476
  214.5 312.0 %copy-start.172 = (pred[384]{0:T(512)(128)(4,1)}, pred[384]{0:T(512)(128)(4,1)S(1)}, u32[]{:S(2)}) copy-start(pred[384]{0:T(512)(128)(4,1)S(1)} %get-tuple-element.718) | copy-start | bytes 1156
  214.5 343.3 %copy-start.132 = (pred[384]{0:T(512)(128)(4,1)}, pred[384]{0:T(512)(128)(4,1)S(1)}, u32[]{:S(2)}) copy-start(pred[384]{0:T(512)(128)(4,1)S(1)} %get-tuple-element.717) | copy-start | bytes 1156
  216.0 341.8 %copy-start.100 = (f32[768]{0:T(1024)}, f32[768]{0:T(1024)S(1)}, u32[]{:S(2)}) copy-start(f32[768]{0:T(1024)S(1)} %get-tuple-element.657) | copy-start | bytes 9220
  216.0 341.8 %copy-start.103 = (f32[768]{0:T(1024)}, f32[768]{0:T(1024)S(1)}, u32[]{:S(2)}) copy-start(f32[768]{0:T(1024)S(1)} %get-tuple-element.658) | copy-start | bytes 9220
  216.0 430.0 %copy-start.71 = (f32[768]{0:T(1024)}, f32[768]{0:T(1024)S(1)}, u32[]{:S(2)}) copy-start(f32[768]{0:T(1024)S(1)} %get-tuple-element.655) | copy-start | bytes 9220
  454.3 103.5 %copy-start.10 = (bf16[384,768]{1,0:T(8,128)(2,1)}, bf16[384,768]{1,0:T(8,128)(2,1)S(1)}, u32[]{:S(2)}) copy-start(bf16[384,768]{1,0:T(8,128)(2,1)S(1)} %gather_fusion.2) | copy-start | bytes 1769476
  462.5 64.0 %copy-start.26 = (bf16[384,768]{1,0:T(8,128)(2,1)}, bf16[384,768]{1,0:T(8,128)(2,1)S(1)}, u32[]{:S(2)}) copy-start(bf16[384,768]{1,0:T(8,128)(2,1)S(1)} %gather_fusion) | copy-start | bytes 1769476
  463.2 94.6 %copy-start.109 = (f32[384]{0:T(512)}, f32[384]{0:T(512)S(1)}, u32[]{:S(2)}) copy-start(f32[384]{0:T(512)S(1)} %broadcast_multiply_fusion.14) | copy-start | bytes 4612
  463.2 63.2 %copy-start.121 = (f32[384]{0:T(512)}, f32[384]{0:T(512)S(1)}, u32[]{:S(2)}) copy-start(f32[384]{0:T(512)S(1)} %broadcast_multiply_fusion.17) | copy-start | bytes 4612
  464.1 93.7 %copy-start.118 = (f32[384]{0:T(512)}, f32[384]{0:T(512)S(1)}, u32[]{:S(2)}) copy-start(f32[384]{0:T(512)S(1)} %add_rsqrt_fusion.2) | copy-start | bytes 4612
  464.1 62.4 %copy-start.175 = (f32[384]{0:T(512)}, f32[384]{0:T(512)S(1)}, u32[]{:S(2)}) copy-start(f32[384]{0:T(512)S(1)} %add_rsqrt_fusion.5) | copy-start | bytes 4612
  560.2 66.3 %copy-start.41 = (f32[384,768]{1,0:T(8,128)}, f32[384,768]{1,0:T(8,128)S(1)}, u32[]{:S(2)}) copy-start(f32[384,768]{1,0:T(8,128)S(1)} %get-tuple-element.692) | copy-start | bytes 3538948
  560.5 66.0 %copy-start.115 = (f32[384]{0:T(512)}, f32[384]{0:T(512)S(1)}, u32[]{:S(2)}) copy-start(f32[384]{0:T(512)S(1)} %add_rsqrt_fusion.1) | copy-start | bytes 4612
  649.7 30.7 copy-start.48
  650.4 39.4 %copy-start.81 = (bf16[56,768]{1,0:T(8,128)(2,1)}, bf16[56,768]{1,0:T(8,128)(2,1)S(1)}, u32[]{:S(2)}) copy-start(bf16[56,768]{1,0:T(8,128)(2,1)S(1)} %gather_fusion.3) | copy-start | bytes 258052
  691.1 29.1 copy-start.46
  691.2 68.0 %copy-start.159 = (f32[56]{0:T(128)}, f32[56]{0:T(128)S(1)}, u32[]{:S(2)}) copy-start(f32[56]{0:T(128)S(1)} %broadcast_multiply_fusion.22) | copy-start | bytes 676
  691.4 67.8 %copy-start.182 = (f32[56]{0:T(128)}, f32[56]{0:T(128)S(1)}, u32[]{:S(2)}) copy-start(f32[56]{0:T(128)S(1)} %add_rsqrt_fusion.6) | copy-start | bytes 676
  692.8 27.4 copy-start.47
  1078.8 2503.6 %reduce-scatter.11.cloned.1.call-start = ((), (), s32[]{:S(2)}) async-start(), calls=%async_computation.9 | async-start | bytes 2433024 | tf_op jit(solution)/shard_map/reduce_scatter | solution.py:367
  1083.5 2500.4 %reduce-scatter.13.cloned.1.call-start = ((), (), s32[]{:S(2)}) async-start(), calls=%async_computation.10 | async-start | bytes 4866048 | tf_op jit(solution)/shard_map/reduce_scatter | solution.py:368
  1090.9 2494.6 %reduce-scatter.9.cloned.1.call-start = ((), (), s32[]{:S(2)}) async-start(), calls=%async_computation.8 | async-start | bytes 7299072 | tf_op jit(solution)/shard_map/reduce_scatter | solution.py:366
  1103.8 34.2 copy-start.131
  1103.8 2485.2 %reduce-scatter.15.cloned.1.call-start = ((), (), s32[]{:S(2)}) async-start(), calls=%async_computation.11 | async-start | bytes 19464192 | tf_op jit(solution)/shard_map/reduce_scatter | solution.py:369
  1138.0 51.7 %copy-start.2 = (bf16[56,30592]{1,0:T(8,128)(2,1)S(1)}, bf16[56,30592]{1,0:T(8,128)(2,1)}, u32[]{:S(2)}) copy-start(bf16[56,30592]{1,0:T(8,128)(2,1)} %copy-done.1) | copy-start | bytes 10278916
  1138.1 51.7 %copy-start.160 = (f32[56]{0:T(128)S(1)}, f32[56]{0:T(128)}, u32[]{:S(2)}) copy-start(f32[56]{0:T(128)} %copy-done.159) | copy-start | bytes 676
  1138.1 51.7 %copy-start.183 = (f32[56]{0:T(128)S(1)}, f32[56]{0:T(128)}, u32[]{:S(2)}) copy-start(f32[56]{0:T(128)} %copy-done.182) | copy-start | bytes 676
  1189.8 33.6 copy-start.129
  1223.4 51.8 %copy-start.35 = (f32[384,768]{1,0:T(8,128)S(1)}, f32[384,768]{1,0:T(8,128)}, u32[]{:S(2)}) copy-start(f32[384,768]{1,0:T(8,128)} %copy-done.34) | copy-start | bytes 3538948
  1394.2 2120.4 %copy-start.165 = (f32[768,1]{0,1:T(1,128)S(1)}, f32[768,1]{0,1:T(1,128)}, u32[]{:S(2)}) copy-start(f32[768,1]{0,1:T(1,128)} %stack.90) | copy-start | bytes 9220
  1394.2 2120.4 %copy-start.166 = (f32[768,1]{0,1:T(1,128)S(1)}, f32[768,1]{0,1:T(1,128)}, u32[]{:S(2)}) copy-start(f32[768,1]{0,1:T(1,128)} %stack.91) | copy-start | bytes 9220
  1394.2 2120.4 %copy-start.151 = (f32[768]{0:T(1024)S(1)}, f32[768]{0:T(1024)}, u32[]{:S(2)}) copy-start(f32[768]{0:T(1024)} %get-tuple-element.595) | copy-start | bytes 9220
  1394.2 2120.4 %copy-start.193 = (f32[2]{0:T(128)S(1)}, f32[2]{0:T(128)}, u32[]{:S(2)}) copy-start(f32[2]{0:T(128)} %get-tuple-element.593) | copy-start | bytes 28
  1394.2 2120.5 %copy-start.163 = (f32[768,1]{0,1:T(1,128)S(1)}, f32[768,1]{0,1:T(1,128)}, u32[]{:S(2)}) copy-start(f32[768,1]{0,1:T(1,128)} %stack.85) | copy-start | bytes 9220
  1394.2 2120.5 %copy-start.164 = (f32[768,1]{0,1:T(1,128)S(1)}, f32[768,1]{0,1:T(1,128)}, u32[]{:S(2)}) copy-start(f32[768,1]{0,1:T(1,128)} %stack.84) | copy-start | bytes 9220
  1394.3 2123.1 %copy-start.152 = (f32[768]{0:T(1024)S(1)}, f32[768]{0:T(1024)}, u32[]{:S(2)}) copy-start(f32[768]{0:T(1024)} %get-tuple-element.647) | copy-start | bytes 9220
  1394.3 2123.1 %copy-start.194 = (f32[2]{0:T(128)S(1)}, f32[2]{0:T(128)}, u32[]{:S(2)}) copy-start(f32[2]{0:T(128)} %get-tuple-element.598) | copy-start | bytes 28
  3512.5 53.1 %copy-start.16 = (f32[960,768]{1,0:T(8,128)}, f32[960,768]{1,0:T(8,128)S(1)}, u32[]{:S(2)}) copy-start(f32[960,768]{1,0:T(8,128)S(1)} %fusion.8) | copy-start | bytes 8847364
  3512.6 53.1 %collective-permute-start = (f32[124,768]{1,0:T(8,128)S(1)}, f32[124,768]{1,0:T(8,128)}, u32[]{:S(2)}, u32[]{:S(2)}) collective-permute-start(f32[124,768]{1,0:T(8,128)S(1)} %slice.302), channel_id=1, source_target_pairs={{0,1},{1,2},{2,3},{3,4},{4,5},{5,6},{6,7},{7,8},{8,9},{9,10},{10,1... | collective-permute-start | bytes 1142792
  3575.5 59.9 %copy-start.114 = (f32[1388]{0:T(1024)S(1)}, f32[1388]{0:T(1024)}, u32[]{:S(2)}) copy-start(f32[1388]{0:T(1024)} %param.67) | copy-start | bytes 16660
  3575.5 59.9 %copy-start.178 = (f32[1388]{0:T(1024)S(1)}, f32[1388]{0:T(1024)}, u32[]{:S(2)}) copy-start(f32[1388]{0:T(1024)} %param.68) | copy-start | bytes 16660
  3575.5 59.9 %copy-start.179 = (f32[1388]{0:T(1024)S(1)}, f32[1388]{0:T(1024)}, u32[]{:S(2)}) copy-start(f32[1388]{0:T(1024)} %param.69) | copy-start | bytes 16660
  3575.5 61.4 %copy-start.181 = (f32[2,24,2]{1,2,0:T(2,128)S(1)}, f32[2,24,2]{1,2,0:T(2,128)}, u32[]{:S(2)}) copy-start(f32[2,24,2]{1,2,0:T(2,128)} %param.52) | copy-start | bytes 1156
  3575.5 61.4 %copy-start.188 = (f32[2,24,2]{1,2,0:T(2,128)S(1)}, f32[2,24,2]{1,2,0:T(2,128)}, u32[]{:S(2)}) copy-start(f32[2,24,2]{1,2,0:T(2,128)} %param.53) | copy-start | bytes 1156
  3575.6 61.4 %copy-start.189 = (f32[2,24,2]{1,2,0:T(2,128)S(1)}, f32[2,24,2]{1,2,0:T(2,128)}, u32[]{:S(2)}) copy-start(f32[2,24,2]{1,2,0:T(2,128)} %param.54) | copy-start | bytes 1156
  (163 other events, 850.0 us)
Sparse Core Ops, SparseCore 0:
  14.2 122.7 all-reduce.11
  140.4 268.1 all-gather.14
  412.0 58.2 all-gather.6
  473.5 52.8 all-gather.8
  529.9 81.1 all-gather.10
  614.7 56.0 all-gather.12
  1079.0 130.0 all-reduce.13
  1214.9 98.8 reduce-scatter.10
  1320.3 109.3 reduce-scatter.12
  1435.1 140.9 reduce-scatter.8
  1583.7 298.2 reduce-scatter.14
where the time goes:
time: 3670 us; the launch traced here: 3660 us
  blocking collectives  2390 us (65%)
  matrix products  474 us (13%)
  other arithmetic  326 us (9%)
  waiting for transfers between devices  288 us (8%)
  local copies, waits for them, and re-layouts  137 us (4%)
    unnamed x3, blocking collectives  2210 us
    all_gather x1, waiting for transfers between devices, shards(): lax.all_gather(table_master.astype(jnp.bfloat16), ('wide', 'narrow'), axi...  189 us
    add x6, other arithmetic, shards(): older + newer  108 us
    dot_general x16, matrix products, product(): return jnp.dot(left, right, preferred_element_type=jnp.float32)  104 us
    scatter-add x2, other arithmetic, train_sequence(): grad_table = grad_table.at[token_row].add(grad_embedded)  103 us
    dot_general x12, matrix products, product_left(): lax.dot_general(left, right, (((0,), (0,)), ((), ())), preferred_element_...  98.9 us
    dot_general x16, matrix products, product_right(): lax.dot_general(left, right, (((1,), (1,)), ((), ())), preferred_element_...  85.9 us
    all_gather x1, blocking collectives, shards(): lax.all_gather(position_master.astype(jnp.bfloat16), ('wide', 'narrow'),...  74.9 us
  transfers between devices with their start and end apart: 12, of which 5 were waited for; matrix products, arithmetic and copies ran while one was open for 72% of the time, Pallas kernels for 0%

commit v1 on v0

v1 whole, which is shorter than its diff:
```python
from functools import partial

import jax
import jax.numpy as jnp
from jax import lax
from jax.experimental import pallas as pl
from jax.experimental.pallas import tpu as pltpu
from jax.sharding import PartitionSpec as P

D = 768
HEAD = 64
FF = 3072
STEP_COUNT = 10


NORM_EPS = 1e-12
CLIP_NORM = 0.02
BETA_ONE = 0.9
BETA_TWO = 0.999
ADAM_EPS = 1e-08
DECAY_RATE = 0.01
LEARN_RATE = 0.1
MASKED_FILL = -1000000000.0
AXES = ("wide", "narrow")
ROWS_AHEAD = 96
LANES = 128


def product(left, right):
    return jnp.dot(left, right, preferred_element_type=jnp.float32)


def product_right(left, right):
    return lax.dot_general(
        left, right, (((1,), (1,)), ((), ())), preferred_element_type=jnp.float32
    )


def product_left(left, right):
    return lax.dot_general(
        left, right, (((0,), (0,)), ((), ())), preferred_element_type=jnp.float32
    )


def norm_forward(values, gain, shift):
    average = jnp.mean(values, axis=-1, keepdims=True)
    centered = values - average
    spread = jnp.mean(centered * centered, axis=-1, keepdims=True)
    inverse = lax.rsqrt(spread + NORM_EPS)
    normal = centered * inverse
    return (normal * gain + shift, (normal, inverse))


def norm_backward(grad, saved, gain):
    normal, inverse = saved
    scaled = grad * gain
    inner = (
        scaled
        - jnp.mean(scaled, axis=-1, keepdims=True)
        - normal * jnp.mean(scaled * normal, axis=-1, keepdims=True)
    )
    return (inner * inverse, jnp.sum(grad * normal, axis=0), jnp.sum(grad, axis=0))


def gelu_exact(values):
    return jax.nn.gelu(values, approximate=False)


def gelu_back(values, grad):
    return jax.vjp(gelu_exact, values)[1](grad)[0]


def split_vectors(vectors):
    extents = [D] * 11 + [FF] + [D] * 3
    pieces = []
    start = 0
    for extent in extents:
        pieces.append(vectors[start : start + extent])
        start += extent
    pieces.append(vectors[start:])
    return pieces


def bits_of(size):
    return size.bit_length() - 1


def orders():
    far = [("wide", bit) for bit in range(1, bits_of(lax.axis_size("wide")))]
    return far, far[::-1]


CORE = ("wide", 0)


def my_bit(dim):
    return (lax.axis_index(dim[0]) >> dim[1]) & 1


def swap(values, dim):
    size = lax.axis_size(dim[0])
    return lax.ppermute(values, dim[0], [(i, i ^ (1 << dim[1])) for i in range(size)])


def pin(values, *others):
    return lax.optimization_barrier((values, others))[0]


def place_blocks(spreads, starts, middle, me_ref, *refs):
    count = len(spreads[0])
    outs = refs[8 : 8 + len(starts) - 1]
    held = refs[8 + len(outs) : 10 + len(outs)]
    arrive, leave = refs[10 + len(outs) :]
    me = me_ref[0]
    inward, outward = [], []
    for side in range(2):
        pieces = refs[4 * side : 4 * side + 4]
        each = pieces[0].shape[0]
        left = 0 if side == 0 else middle
        right = middle if side == 0 else starts[-1]
        for code, offset in enumerate(spreads[side]):
            number = side * count + code
            inward.append(
                pltpu.make_async_copy(
                    pieces[code // each].at[code % each], held[side].at[code], arrive.at[number]
                )
            )
            group = []
            for out_ref, start, stop in zip(outs, starts, starts[1:]):
                low, high = max(start, left), min(stop, right)
                if low < high:
                    group.append(
                        pltpu.make_async_copy(
                            held[side].at[code, :, :, low - left : high - left],
                            out_ref.at[me ^ offset, :, :, low - start : high - start],
                            leave.at[number, len(group)],
                        )
                    )
            outward.append(group)
    for copy in inward:
        copy.start()
    for first, group in zip(inward, outward):
        first.wait()
        for copy in group:
            copy.start()
    for group in outward:
        for copy in group:
            copy.wait()


def along_line(block):
    size = lax.axis_size("narrow")
    me = lax.axis_index("narrow")
    rights, lefts = [], []
    right = left = block
    for step in range(1, size):
        right = lax.ppermute(right, "narrow", [(z, z + 1) for z in range(step - 1, size - 1)])
        left = lax.ppermute(left, "narrow", [(z, z - 1) for z in range(1, size - step + 1)])
        rights.append(right)
        lefts.append(left)
    blocks = []
    for spot in range(size):
        chosen = block
        for other in range(size):
            if other > spot:
                chosen = jnp.where(me == other, rights[other - spot - 1], chosen)
            if other < spot:
                chosen = jnp.where(me == other, lefts[spot - other - 1], chosen)
        blocks.append(chosen)
    return blocks


class Gather:
    def __init__(self, arrays):
        self.columns = [array.shape[1] for array in arrays]
        self.rows = arrays[0].shape[0]
        total = sum(self.columns)
        self.middle = total // 2 // LANES * LANES
        self.packed = jnp.concatenate(arrays, axis=1) if len(arrays) > 1 else arrays[0]

    def line(self):
        blocks = along_line(self.packed)
        self.halves = [
            jnp.stack([block[:, : self.middle] for block in blocks])[None],
            jnp.stack([block[:, self.middle :] for block in blocks])[None],
        ]
        return self.halves

    def plane(self):
        self.pieces = []
        for held, order in zip(self.halves, orders()):
            for dim in order[:-1]:
                held = jnp.concatenate([held, swap(held, dim)], axis=0)
            self.pieces.append([held, swap(held, order[-1])])
        return self.pieces

    def finish(self):
        pieces = [half + [swap(piece, CORE) for piece in half] for half in self.pieces]
        count = lax.axis_size("wide")
        spreads = [
            [
                sum(((code >> k) & 1) << dim[1] for k, dim in enumerate(order + [CORE]))
                for code in range(count)
            ]
            for order in orders()
        ]
        starts = [sum(self.columns[:k]) for k in range(len(self.columns) + 1)]
        line = lax.axis_size("narrow")
        dtype = self.packed.dtype
        me = lax.axis_index("wide").astype(jnp.int32).reshape(1)
        moved = 2 * count * line * self.rows * starts[-1] * dtype.itemsize
        outs = pl.pallas_call(
            partial(place_blocks, spreads, starts, self.middle),
            out_shape=tuple(
                jax.ShapeDtypeStruct((count, line, self.rows, columns), dtype)
                for columns in self.columns
            ),
            in_specs=[pl.BlockSpec(memory_space=pltpu.SMEM)]
            + [pl.BlockSpec(memory_space=pl.ANY)] * 8,
            out_specs=(pl.BlockSpec(memory_space=pl.ANY),) * len(self.columns),
            scratch_shapes=[
                pltpu.VMEM((count, line, self.rows, self.middle), dtype),
                pltpu.VMEM((count, line, self.rows, starts[-1] - self.middle), dtype),
                pltpu.SemaphoreType.DMA((2 * count,)),
                pltpu.SemaphoreType.DMA((2 * count, len(self.columns))),
            ],
            compiler_params=pltpu.CompilerParams(vmem_limit_bytes=40 << 20),
            cost_estimate=pl.CostEstimate(flops=0, bytes_accessed=moved, transcendentals=0),
        )(me, *pieces[0], *pieces[1])
        return [out.reshape(count * line * self.rows, -1) for out in outs]


class Scatter:
    def __init__(self, items):
        wide, line = lax.axis_size("wide"), lax.axis_size("narrow")
        self.labels, self.terms, self.dims = [], [], []
        for blocks, which in items:
            self.labels.append([("wide", bit) for bit in range(bits_of(wide))][::-1])
            self.terms.append(
                [blocks.reshape((2,) * bits_of(wide) + (line,) + blocks.shape[1:])]
            )
            self.dims.append([CORE] + orders()[which][::-1])

    def send(self):
        self.away = []
        for labels, terms, dims in zip(self.labels, self.terms, self.dims):
            axis, bit = labels.index(dims[0]), my_bit(dims[0])
            self.away.append(
                sum(
                    lax.dynamic_index_in_dim(term, 1 - bit, axis, keepdims=False).astype(
                        jnp.float32
                    )
                    for term in terms
                ).astype(jnp.bfloat16)
            )
        return self.away

    def receive(self):
        arrived = []
        for number, away in enumerate(self.away):
            dim = self.dims[number].pop(0)
            axis, bit = self.labels[number].index(dim), my_bit(dim)
            arrived.append(swap(away, dim))
            self.terms[number] = [
                lax.dynamic_index_in_dim(term, bit, axis, keepdims=False)
                for term in self.terms[number]
            ] + [arrived[-1]]
            self.labels[number].remove(dim)
        return arrived

    def step(self):
        self.send()
        return self.receive()

    def line(self):
        sums = [sum(term.astype(jnp.float32) for term in terms) for terms in self.terms]
        size = lax.axis_size("narrow")
        me = lax.axis_index("narrow")
        depth = min(item.shape[1] for item in sums)
        flat, cuts = [], []
        for item in sums:
            parts = [item[:, k : k + depth] for k in range(0, item.shape[1], depth)]
            flat.extend(parts)
            cuts.append((len(parts), item.shape[2]))
        whole = jnp.concatenate(flat, axis=2) if len(flat) > 1 else flat[0]
        right = left = None
        for step in range(1, size):
            spot = jnp.clip(me + size - step, 0, size - 1)
            goes = lax.dynamic_index_in_dim(whole, spot, 0, keepdims=False)
            if right is not None:
                goes = goes + right.astype(jnp.float32)
            right = lax.ppermute(
                goes.astype(jnp.bfloat16), "narrow", [(z, z + 1) for z in range(step)]
            )
            spot = jnp.clip(me - size + step, 0, size - 1)
            goes = lax.dynamic_index_in_dim(whole, spot, 0, keepdims=False)
            if left is not None:
                goes = goes + left.astype(jnp.float32)
            left = lax.ppermute(
                goes.astype(jnp.bfloat16),
                "narrow",
                [(z, z - 1) for z in range(size - step, size)],
            )
        total = (
            lax.dynamic_index_in_dim(whole, me, 0, keepdims=False)
            + right.astype(jnp.float32)
            + left.astype(jnp.float32)
        )
        results, start = [], 0
        for parts, columns in cuts:
            pieces = [
                total[:, start + k * columns : start + (k + 1) * columns] for k in range(parts)
            ]
            start += parts * columns
            results.append(jnp.concatenate(pieces, axis=0) if parts > 1 else pieces[0])
        return results


def share_small(values):
    count = lax.axis_size(AXES)
    spread = jnp.broadcast_to(values[None], (count,) + values.shape)
    return lax.all_to_all(spread, AXES, 0, 0)


def pack_kernel(length_ref, ids_ref, slot_ref, label_ref, out_ref):
    out_ref[...] = jnp.zeros_like(out_ref)
    micro, local, tokens = ids_ref.shape
    slots = slot_ref.shape[2]
    row = 0
    for index in range(micro * local):
        for start in range(0, tokens, LANES):
            out_ref[row : row + 1, :] = ids_ref[
                index // local, index % local : index % local + 1, start : start + LANES
            ]
            row += 1
    for ref in (slot_ref, label_ref):
        for index in range(micro * local):
            out_ref[row : row + 1, :slots] = ref[
                index // local, index % local : index % local + 1, :
            ]
            row += 1
    for index in range(micro * local):
        out_ref[row : row + 1, :] = jnp.full(
            (1, LANES), length_ref[index // local, index % local], jnp.int32
        )
        row += 1


def stack_kernel(*refs):
    sources, out_ref, rows_ref = refs[:-2], refs[-2], refs[-1]
    rows_ref[...] = jnp.zeros_like(rows_ref)
    row = 0
    for ref in sources:
        rows_ref[row : row + ref.shape[0], :] = ref[...]
        row += ref.shape[0]
    out_ref[...] = rows_ref[...].T


def stack_columns(rows):
    width = rows[0].shape[1]
    return pl.pallas_call(
        stack_kernel,
        out_shape=jax.ShapeDtypeStruct((width, LANES), jnp.float32),
        scratch_shapes=[pltpu.VMEM((LANES, width), jnp.float32)],
    )(*rows)


def gelu_parts(values):
    below = 0.5 + 0.5 * lax.erf(values * (0.5**0.5))
    density = jnp.exp(-0.5 * values * values) * ((0.5 / jnp.pi) ** 0.5)
    return values * below, below + values * density


def softmax_head(queries, keys, alive):
    raw = lax.dot_general(
        queries, keys, (((1,), (1,)), ((), ())), preferred_element_type=jnp.float32
    ) * HEAD ** (-0.5)
    scores = jnp.where(alive, raw, MASKED_FILL)
    expo = jnp.exp(scores - jnp.max(scores, axis=-1, keepdims=True))
    return expo / jnp.sum(expo, axis=-1, keepdims=True)


def attend_kernel(length_ref, query_ref, key_ref, value_ref, context_ref):
    tokens = query_ref.shape[0]
    alive = lax.broadcasted_iota(jnp.int32, (tokens, tokens), 1) < length_ref[pl.program_id(0)]
    contexts = []
    for start in (0, HEAD):
        part = slice(start, start + HEAD)
        attention = softmax_head(query_ref[:, part], key_ref[:, part], alive)
        contexts.append(product(attention.astype(jnp.bfloat16), value_ref[:, part]))
    context_ref[...] = jnp.concatenate(contexts, axis=1).astype(jnp.bfloat16)


def attend_back_kernel(length_ref, query_ref, key_ref, value_ref, grad_ref, query_out, key_out, value_out):
    tokens = query_ref.shape[0]
    alive = lax.broadcasted_iota(jnp.int32, (tokens, tokens), 1) < length_ref[pl.program_id(0)]
    outs = ([], [], [])
    for start in (0, HEAD):
        part = slice(start, start + HEAD)
        queries, keys, values = query_ref[:, part], key_ref[:, part], value_ref[:, part]
        grad = grad_ref[:, part]
        attention = softmax_head(queries, keys, alive)
        grad_attention = product_right(grad, values)
        grad_scores = attention * (
            grad_attention - jnp.sum(grad_attention * attention, axis=-1, keepdims=True)
        )
        grad_raw = (grad_scores.astype(jnp.bfloat16).astype(jnp.float32) * HEAD ** (-0.5)).astype(
            jnp.bfloat16
        )
        outs[0].append(product(grad_raw, keys))
        outs[1].append(product_left(grad_raw, queries))
        outs[2].append(product_left(attention.astype(jnp.bfloat16), grad))
    for out_ref, pair in zip((query_out, key_out, value_out), outs):
        out_ref[...] = jnp.concatenate(pair, axis=1).astype(jnp.bfloat16)


def head_specs(tokens, pairs, count):
    return [
        pl.BlockSpec((tokens, LANES), lambda s, h, lengths, k=k: (s, k * pairs + h))
        for k in range(count)
    ]


def attend(lengths, mixed, tokens):
    width = mixed.shape[1] // 3
    pairs = width // LANES
    rows = mixed.shape[0]
    return pl.pallas_call(
        attend_kernel,
        grid_spec=pltpu.PrefetchScalarGridSpec(
            num_scalar_prefetch=1,
            grid=(rows // tokens, pairs),
            in_specs=head_specs(tokens, pairs, 3),
            out_specs=head_specs(tokens, pairs, 1)[0],
        ),
        out_shape=jax.ShapeDtypeStruct((rows, width), jnp.bfloat16),
        compiler_params=pltpu.CompilerParams(vmem_limit_bytes=32 << 20),
        cost_estimate=pl.CostEstimate(
            flops=8 * rows * tokens * width,
            bytes_accessed=8 * rows * width,
            transcendentals=rows * tokens * width // HEAD,
        ),
    )(lengths, mixed, mixed, mixed)


def attend_back(lengths, mixed, grad_context, tokens):
    width = mixed.shape[1] // 3
    pairs = width // LANES
    rows = mixed.shape[0]
    out = jax.ShapeDtypeStruct((rows, width), jnp.bfloat16)
    return pl.pallas_call(
        attend_back_kernel,
        grid_spec=pltpu.PrefetchScalarGridSpec(
            num_scalar_prefetch=1,
            grid=(rows // tokens, pairs),
            in_specs=head_specs(tokens, pairs, 3) + head_specs(tokens, pairs, 1),
            out_specs=head_specs(tokens, pairs, 1) * 3,
        ),
        out_shape=(out, out, out),
        compiler_params=pltpu.CompilerParams(vmem_limit_bytes=32 << 20),
        cost_estimate=pl.CostEstimate(
            flops=20 * rows * tokens * width,
            bytes_accessed=14 * rows * width,
            transcendentals=rows * tokens * width // HEAD,
        ),
    )(lengths, mixed, mixed, mixed, grad_context)


def one_hot(count, index):
    return (
        lax.broadcasted_iota(jnp.int32, (count, index.shape[0]), 0) == index[None, :]
    ).astype(jnp.bfloat16)


def exact(left, right):
    return jnp.dot(left, right, precision=lax.Precision.HIGHEST, preferred_element_type=jnp.float32)


def shards(
    token_ids,
    seq_lengths,
    mlm_slots,
    mlm_labels,
    nsp_labels,
    *weights,
):
    masters, firsts, seconds = weights[0::3], weights[1::3], weights[2::3]
    (
        table_master,
        position_master,
        pair_master,
        input_master,
        output_master,
        dense_master,
        feed_master,
        vector_master,
    ) = masters
    micro, local, tokens = token_ids.shape
    slots_each = mlm_slots.shape[2]
    devices = lax.axis_size(AXES)
    me = lax.axis_index(AXES)
    seqs = micro * local
    total = seqs * tokens
    picked = seqs * slots_each
    depth, width = input_master.shape[0], output_master.shape[1]
    inner_width = feed_master.shape[2]
    vocab_rows = table_master.shape[0]
    low = jnp.bfloat16
    places = jnp.arange(tokens, dtype=jnp.int32)

    id_rows = total // LANES
    pack_rows = -(-(id_rows + 3 * seqs) // 8) * 8
    packed = pl.pallas_call(
        pack_kernel,
        out_shape=jax.ShapeDtypeStruct((pack_rows, LANES), jnp.int32),
        in_specs=[pl.BlockSpec(memory_space=pltpu.SMEM)]
        + [pl.BlockSpec(memory_space=pltpu.VMEM)] * 3,
    )(seq_lengths, token_ids, mlm_slots, mlm_labels)
    shared = share_small(packed)
    all_ids = shared[:, :id_rows].reshape(devices * seqs, tokens)
    all_slots, all_labels = (
        shared[:, id_rows + k * seqs : id_rows + (k + 1) * seqs, :slots_each] for k in (0, 1)
    )
    all_lengths = shared[:, id_rows + 2 * seqs : id_rows + 3 * seqs, :1]
    all_counted = (all_slots < all_lengths).astype(jnp.float32).reshape(-1)
    all_labels = all_labels.reshape(-1)
    masked_count = jnp.sum(all_counted)
    inv_count = 1.0 / masked_count
    inv_seqs = 1.0 / (devices * seqs)

    table_low = table_master.astype(low)
    vector_each = vector_master.shape[0]
    vector_columns = -(-vector_each // depth)
    small_used = tokens + 4 + vector_columns
    small_columns = -(-small_used // LANES) * LANES
    small_low = jnp.concatenate(
        [
            position_master.T,
            jnp.moveaxis(pair_master, 0, 1).reshape(depth, 4),
            jnp.pad(vector_master, (0, depth * vector_columns - vector_each)).reshape(
                depth, vector_columns
            ),
            jnp.zeros((depth, small_columns - small_used), jnp.float32),
        ],
        axis=1,
    ).astype(low)
    first_group = Gather([input_master.astype(low), small_low, output_master.astype(low)])
    first_group.line()

    lane_rows = -(-vocab_rows // LANES)

    def split_ids(ids, alive):
        owner = ids // vocab_rows
        within = ids - owner * vocab_rows
        high = owner * lane_rows + within // LANES
        return owner, jnp.where(alive, high, -1), within % LANES

    _, all_high, all_low = split_ids(
        all_ids, places[None, :] < all_lengths.reshape(devices * seqs, 1)
    )
    hits = product_right(
        one_hot(devices * lane_rows, all_high.reshape(-1)), one_hot(LANES, all_low.reshape(-1))
    )
    used = (hits > 0).astype(jnp.float32)
    lane = jnp.arange(LANES)
    before = exact(used, (lane[:, None] < lane[None, :]).astype(jnp.float32))
    row_totals = jnp.sum(used, axis=1).reshape(devices, lane_rows)
    row_index = jnp.arange(lane_rows)
    earlier = jnp.sum(
        jnp.where(row_index[None, :, None] < row_index[None, None, :], row_totals[:, :, None], 0.0),
        axis=1,
    )
    rank = before + earlier.reshape(-1, 1)
    most = jnp.max(jnp.sum(row_totals, axis=1)).astype(jnp.int32)
    ahead = ROWS_AHEAD
    rounds = -(-most // ahead)

    lengths = seq_lengths.reshape(-1)
    my_alive = (places[None, :] < lengths[:, None]).reshape(-1)
    my_owner, my_high, my_low = split_ids(token_ids.reshape(-1), my_alive)
    looked = exact(rank.T, one_hot(devices * lane_rows, my_high).astype(jnp.float32))
    my_rank = jnp.sum(looked * one_hot(LANES, my_low).astype(jnp.float32), axis=0).astype(jnp.int32)

    own_rank = lax.dynamic_slice_in_dim(rank, me * lane_rows, lane_rows, 0).reshape(-1)[:vocab_rows]
    own_used = lax.dynamic_slice_in_dim(used, me * lane_rows, lane_rows, 0).reshape(-1)[:vocab_rows]
    own_slot = jnp.where(own_used > 0, own_rank.astype(jnp.int32), -1)

    def picks(start):
        own = one_hot(ahead, jnp.where(own_slot >= start, own_slot - start, -1))
        inside = my_alive & (my_rank >= start) & (my_rank < start + ahead)
        mine = one_hot(devices * ahead, jnp.where(inside, my_owner * ahead + my_rank - start, -1))
        return own, mine

    own_first, mine_first = picks(0)
    word_group = Gather([product(own_first, table_low).astype(low)])
    word_line = word_group.line()
    first_group.plane()
    late = pin(
        [
            feed_master[0].astype(low),
            feed_master[1].astype(low),
            dense_master[0].astype(low),
            dense_master[1].astype(low),
        ],
        word_line,
    )
    second_group = Gather(late)
    second_group.line()
    word_group.plane()
    input_all, small_all, output_all = first_group.finish()
    (word_rows,) = word_group.finish()
    words = product_left(mine_first, word_rows)

    def fetch_more(state):
        turn, words = state
        own, mine = picks(turn * ahead)
        rows = lax.all_gather(product(own, table_low).astype(low), AXES, axis=0, tiled=True)
        return turn + 1, words + product_left(mine, rows)

    _, words = lax.while_loop(lambda state: state[0] < rounds, fetch_more, (jnp.int32(1), words))

    position = small_all[:, :tokens].T.astype(jnp.float32)
    pair_cols = jnp.moveaxis(small_all[:, tokens : tokens + 4].reshape(width, 2, 2), 1, 0)
    vectors = small_all[:, tokens + 4 : small_used].reshape(devices, depth * vector_columns)
    parts = split_vectors(vectors[:, :vector_each].reshape(-1).astype(jnp.float32))

    second = (places[None, :] >= lengths[:, None] // 2).reshape(-1)
    type_cols = pair_cols[0].astype(jnp.float32)
    embedded = (
        words
        + jnp.tile(position, (seqs, 1))
        + jnp.where(second[:, None], type_cols[:, 1], type_cols[:, 0])
    )
    normed, saved_zero = norm_forward(embedded, parts[0], parts[1])
    normed_low = normed.astype(low)
    bias_mixed = jnp.concatenate([parts[8], jnp.zeros((width,), jnp.float32), parts[9]])
    mixed = (product(normed_low, input_all) + bias_mixed).astype(low)
    second_group.pieces = pin(second_group.plane(), mixed)
    context_low = attend(lengths, mixed, tokens)
    feed_in, feed_out, dense_one, dense_two = second_group.finish()
    branch = product(context_low, output_all) + parts[10]
    hidden_one, saved_one = norm_forward(normed + branch, parts[2], parts[3])
    one_low = hidden_one.astype(low)
    active, slope = gelu_parts(product(one_low, feed_in) + parts[11])
    active_low, slope = lax.optimization_barrier((active.astype(low), slope))
    outer = product_right(active_low, feed_out) + parts[12]
    hidden_two, saved_two = norm_forward(hidden_one + outer, parts[4], parts[5])
    two_low = hidden_two.astype(low)

    my_slots = mlm_slots.reshape(seqs, slots_each) + tokens * jnp.arange(seqs, dtype=jnp.int32)[:, None]
    slot_hot = one_hot(total, my_slots.reshape(-1))
    picked_low = product_left(slot_hot, two_low).astype(low)
    lifted, head_slope = gelu_parts(product(picked_low, dense_one) + parts[13])
    head_out, saved_head = norm_forward(lifted, parts[6], parts[7])
    head_group = Gather([head_out.astype(low)])
    head_group.line()
    head_group.plane()

    first_hot = one_hot(total, tokens * jnp.arange(seqs, dtype=jnp.int32))
    first_low = product_left(first_hot, two_low).astype(low)
    pooled = jnp.tanh(product(first_low, dense_two) + parts[14])
    pooled_low = pooled.astype(low)
    pair_logits = product(pooled_low, pair_cols[1])
    pair_top = jnp.max(pair_logits, axis=-1, keepdims=True)
    pair_total = pair_top + jnp.log(
        jnp.sum(jnp.exp(pair_logits - pair_top), axis=-1, keepdims=True)
    )
    pair_hit = jnp.arange(2, dtype=jnp.int32)[None, :] == nsp_labels.reshape(-1, 1)
    pair_local = jnp.sum(pair_total[:, 0] - jnp.sum(jnp.where(pair_hit, pair_logits, 0.0), axis=1))

    vocab_bias = lax.dynamic_slice_in_dim(parts[15], me * vocab_rows, vocab_rows, 0)
    (heads,) = head_group.finish()
    logits = product_right(heads, table_low) + vocab_bias
    top = jnp.max(logits, axis=-1)
    local_totals = top + jnp.log(jnp.sum(jnp.exp(logits - top[:, None]), axis=-1))
    all_totals = share_small(local_totals.reshape(-1, LANES))
    highest = jnp.max(all_totals, axis=0)
    log_totals = (highest + jnp.log(jnp.sum(jnp.exp(all_totals - highest), axis=0))).reshape(-1)
    vocab_index = me * vocab_rows + jnp.arange(vocab_rows, dtype=jnp.int32)
    masked_shared = jnp.sum(all_counted * log_totals)
    hit = vocab_index[None, :] == all_labels[:, None]
    target_local = jnp.sum(all_counted[:, None] * jnp.where(hit, logits, 0.0))
    grad_logits = (
        (jnp.exp(logits - log_totals[:, None]) - hit.astype(jnp.float32))
        * (all_counted * inv_count)[:, None]
    ).astype(low)
    grad_heads = product(grad_logits, table_low).reshape(devices, picked, width)
    middle = width // 2
    head_sum = Scatter([(grad_heads[:, :, :middle], 0), (grad_heads[:, :, middle:], 1)])
    sent = head_sum.send()
    grad_table = product_left(pin(grad_logits, sent), heads)
    head_sum.receive()
    for _ in range(1, bits_of(lax.axis_size("wide"))):
        head_sum.step()
    grad_vocab = jnp.sum(grad_logits.astype(jnp.float32), axis=0)
    vocab_pad = -(-vocab_rows // (8 * LANES)) * 8 * LANES
    all_vocab = share_small(jnp.pad(grad_vocab, (0, vocab_pad - vocab_rows)).reshape(-1, LANES))
    grad_head = jnp.concatenate(head_sum.line(), axis=1)

    def owners(values):
        return values.reshape(devices, -1, values.shape[1])

    def column_sum(values):
        return jnp.sum(values.astype(jnp.float32), axis=0, keepdims=True)

    grad_gelu, grad_head_gain, grad_head_shift = norm_backward(grad_head, saved_head, parts[6])
    grad_transform = (grad_gelu * head_slope).astype(low)
    grad_dense_zero = product_left(picked_low, grad_transform)
    grad_pair_logits = (
        (jnp.exp(pair_logits - pair_total) - pair_hit.astype(jnp.float32)) * inv_seqs
    ).astype(low)
    grad_classifier = product_left(pooled_low, grad_pair_logits)
    grad_pooled = product_right(grad_pair_logits, pair_cols[1])
    grad_pool_pre = (grad_pooled * (1.0 - pooled * pooled)).astype(low)
    grad_pooler = product_left(first_low, grad_pool_pre)
    grad_two = exact(
        slot_hot.astype(jnp.float32), product_right(grad_transform, dense_one)
    ) + exact(first_hot.astype(jnp.float32), product_right(grad_pool_pre, dense_two))
    grad_sum_two, grad_feed_gain, grad_feed_shift = norm_backward(grad_two, saved_two, parts[4])
    grad_outer = grad_sum_two.astype(low)
    grad_feed_out = product_left(grad_outer, active_low)
    grad_inner = (product(grad_outer, feed_out) * slope).astype(low)
    grad_feed_in = product_left(one_low, grad_inner)
    feed_sum = Scatter(
        [
            (owners(grad_feed_in), 0),
            (owners(grad_dense_zero), 0),
            (owners(grad_feed_out), 1),
            (owners(grad_pooler), 1),
        ]
    )
    sent = feed_sum.send()
    grad_one = grad_sum_two + product_right(pin(grad_inner, sent), feed_in)
    grad_sum_one, grad_attend_gain, grad_attend_shift = norm_backward(grad_one, saved_one, parts[2])
    grad_branch = grad_sum_one.astype(low)
    grad_context = product_right(grad_branch, output_all).astype(low)
    came = feed_sum.receive()
    sent = feed_sum.send()
    grad_context = pin(grad_context, came, sent)
    grad_q, grad_k, grad_v = attend_back(lengths, mixed, grad_context, tokens)
    grad_mixed = jnp.concatenate([grad_q, grad_k, grad_v], axis=1)
    came = feed_sum.receive()
    sent = feed_sum.send()
    grad_mixed = pin(grad_mixed, came, sent)
    grad_normed = grad_sum_one + product_right(grad_mixed, input_all)
    grad_embedded, grad_embed_gain, grad_embed_shift = norm_backward(
        grad_normed, saved_zero, parts[0]
    )
    embedded_low = grad_embedded.astype(low)
    grad_words = product(mine_first, embedded_low).reshape(devices, ahead, width)
    grad_input = product_left(normed_low, grad_mixed)
    grad_output = product_left(context_low, grad_branch)
    while feed_sum.dims[0]:
        feed_sum.receive()
        if feed_sum.dims[0]:
            feed_sum.send()
    in_second = second[:, None]
    rows = [
        jnp.sum(jnp.where(in_second, 0.0, grad_embedded), axis=0, keepdims=True),
        jnp.sum(jnp.where(in_second, grad_embedded, 0.0), axis=0, keepdims=True),
        grad_classifier.T,
    ]
    vector_rows = [
        grad_embed_gain[None],
        grad_embed_shift[None],
        grad_attend_gain[None],
        grad_attend_shift[None],
        grad_feed_gain[None],
        grad_feed_shift[None],
        grad_head_gain[None],
        grad_head_shift[None],
        column_sum(grad_q),
        column_sum(grad_v),
        column_sum(grad_branch),
        column_sum(grad_inner).reshape(-1, width),
        column_sum(grad_outer),
        column_sum(grad_transform),
        column_sum(grad_pool_pre),
    ]
    vector_count = sum(item.shape[0] for item in vector_rows)
    grad_position = jnp.sum(grad_embedded.reshape(seqs, tokens, width), axis=0).T
    grad_small = jnp.concatenate([grad_position, stack_columns(rows + vector_rows)], axis=1)
    last_sum = Scatter(
        [
            (owners(grad_input), 0),
            (owners(grad_output), 1),
            (owners(grad_small), 1),
            (grad_words[:, :, :middle], 0),
            (grad_words[:, :, middle:], 1),
        ]
    )
    for _ in range(bits_of(lax.axis_size("wide"))):
        last_sum.step()
    sum_feed_in, sum_dense, sum_feed_out, sum_pooler = feed_sum.line()
    sum_input, sum_output, sum_small, words_left, words_right = last_sum.line()
    grad_table = grad_table + exact(
        own_first.T.astype(jnp.float32), jnp.concatenate([words_left, words_right], axis=1)
    )

    def return_more(state):
        turn, grad_table = state
        own, mine = picks(turn * ahead)
        back = lax.psum_scatter(
            product(mine, embedded_low), AXES, scatter_dimension=0, tiled=True
        )
        return turn + 1, grad_table + exact(own.T.astype(jnp.float32), back)

    _, grad_table = lax.while_loop(
        lambda state: state[0] < rounds, return_more, (jnp.int32(1), grad_table)
    )

    sum_vector = sum_small[:, tokens + 4 : tokens + 4 + vector_count]
    pieces = [
        grad_table,
        sum_small[:, :tokens],
        jnp.moveaxis(sum_small[:, tokens : tokens + 4].reshape(depth, 2, 2), 1, 0),
        sum_input,
        sum_output,
        jnp.stack([sum_dense, sum_pooler]),
        jnp.stack([sum_feed_in, sum_feed_out]),
    ]
    squares = sum((jnp.sum(item * item) for item in pieces + [sum_vector, grad_vocab]))
    payload = jnp.concatenate(
        [
            jnp.stack([squares, target_local, pair_local]),
            jnp.zeros((LANES - 3,), jnp.float32),
            sum_vector.reshape(-1),
        ]
    )
    payload_pad = -(-payload.shape[0] // LANES) * LANES
    answers = share_small(
        jnp.pad(payload, (0, payload_pad - payload.shape[0])).reshape(-1, LANES)
    )
    totals = jnp.sum(answers[:, 0, :3], axis=0)
    grad_vector = jnp.concatenate(
        [
            answers.reshape(devices, -1)[:, LANES : LANES + depth * vector_count]
            .reshape(devices * depth, vector_count)
            .T.reshape(-1),
            all_vocab.reshape(devices, -1)[:, :vocab_rows].reshape(-1),
        ]
    )
    pieces.append(lax.dynamic_slice_in_dim(grad_vector, me * vector_each, vector_each, 0))
    norm = jnp.sqrt(totals[0])
    masked_total = masked_shared - totals[1]
    pair_total_sum = totals[2]
    factor = CLIP_NORM / (norm + 1e-06)
    correct_one = 1.0 - BETA_ONE**STEP_COUNT
    correct_two = 1.0 - BETA_TWO**STEP_COUNT
    updated = []
    for number in range(8):
        turned = (lambda item: item.T) if number == 1 else (lambda item: item)
        master = turned(masters[number])
        grad = pieces[number] * factor
        moment_one = BETA_ONE * turned(firsts[number]) + (1.0 - BETA_ONE) * grad
        moment_two = BETA_TWO * turned(seconds[number]) + (1.0 - BETA_TWO) * grad * grad
        direction = moment_one / correct_one / (jnp.sqrt(moment_two / correct_two) + ADAM_EPS)
        decay = DECAY_RATE if number < 7 else 0.0
        updated.extend(
            [
                turned(master - LEARN_RATE * (direction + decay * master)),
                turned(moment_one),
                turned(moment_two),
            ]
        )
    masked_sums = jnp.stack([masked_total, masked_count])
    return (masked_sums, pair_total_sum, norm) + tuple(updated)


def solution(mesh):
    placed = (
        P(None, ("wide", "narrow"), None),
        P(None, ("wide", "narrow")),
        P(None, ("wide", "narrow"), None),
        P(None, ("wide", "narrow"), None),
        P(None, ("wide", "narrow")),
        P(("wide", "narrow"), None),
        P(("wide", "narrow"), None),
        P(("wide", "narrow"), None),
        P(None, ("wide", "narrow")),
        P(None, ("wide", "narrow")),
        P(None, ("wide", "narrow")),
        P(None, ("wide", "narrow"), None),
        P(None, ("wide", "narrow"), None),
        P(None, ("wide", "narrow"), None),
        P(("wide", "narrow"), None),
        P(("wide", "narrow"), None),
        P(("wide", "narrow"), None),
        P(("wide", "narrow"), None),
        P(("wide", "narrow"), None),
        P(("wide", "narrow"), None),
        P(None, ("wide", "narrow"), None),
        P(None, ("wide", "narrow"), None),
        P(None, ("wide", "narrow"), None),
        P(None, ("wide", "narrow"), None),
        P(None, ("wide", "narrow"), None),
        P(None, ("wide", "narrow"), None),
        P(("wide", "narrow")),
        P(("wide", "narrow")),
        P(("wide", "narrow")),
    )
    return jax.shard_map(
        shards,
        mesh=mesh,
        in_specs=placed,
        out_specs=(
            P(),
            P(),
            P(),
            P(("wide", "narrow"), None),
            P(("wide", "narrow"), None),
            P(("wide", "narrow"), None),
            P(None, ("wide", "narrow")),
            P(None, ("wide", "narrow")),
            P(None, ("wide", "narrow")),
            P(None, ("wide", "narrow"), None),
            P(None, ("wide", "narrow"), None),
            P(None, ("wide", "narrow"), None),
            P(("wide", "narrow"), None),
            P(("wide", "narrow"), None),
            P(("wide", "narrow"), None),
            P(("wide", "narrow"), None),
            P(("wide", "narrow"), None),
            P(("wide", "narrow"), None),
            P(None, ("wide", "narrow"), None),
            P(None, ("wide", "narrow"), None),
            P(None, ("wide", "narrow"), None),
            P(None, ("wide", "narrow"), None),
            P(None, ("wide", "narrow"), None),
            P(None, ("wide", "narrow"), None),
            P(("wide", "narrow")),
            P(("wide", "narrow")),
            P(("wide", "narrow")),
        ),
        check_vma=False,
    )
```

time: 3670 us -> 838 us (0.23)
  blocking collectives: 2390 us -> 0 us
  matrix products: 474 us -> 120 us
  other arithmetic: 326 us -> 144 us
  starting transfers between devices: 2.9 us -> 145 us
  waiting for transfers between devices: 288 us -> 227 us
  Pallas kernels: 0 us -> 58.7 us
    unnamed x3 -> x0, blocking collectives: 2210 us -> none
    all_gather x5 -> x0, waiting for transfers between devices: 288 us -> none  [the longest x1 189 us: shards(): lax.all_gather(table_master.astype(jnp.bfloat16), ('wide', 'narrow'), axi...]
    ppermute x0 -> x107, waiting for transfers between devices: none -> 208 us  [the longest x65 133 us: swap(): lax.ppermute(values, dim[0], [(i, i ^ 1 << dim[1]) for i in range(size)])]
    dot_general x84 -> x5, matrix products: 185 us -> 5.66 us  [exact(): jnp.dot(left, right, precision=lax.Precision.HIGHEST, preferred_element_t...]
    all_gather x2 -> x0, blocking collectives: 144 us -> none  [the longest x1 74.9 us: shards(): lax.all_gather(position_master.astype(jnp.bfloat16), ('wide', 'narrow'),...]
    ppermute x0 -> x107, starting transfers between devices: none -> 127 us  [the longest x65 48.1 us: swap(): lax.ppermute(values, dim[0], [(i, i ^ 1 << dim[1]) for i in range(size)])]
    scatter-add x4 -> x0, other arithmetic: 108 us -> none  [the longest x2 103 us: train_sequence(): grad_table = grad_table.at[token_row].add(grad_embedded)]
    add x7 -> x14, other arithmetic: 109 us -> 14.6 us  [the longest x8 11.8 us: line(): sum((term.astype(jnp.float32) for term in terms))]
  transfers between devices with their start and end apart: 12 -> 111, of which waited for: 5 -> 40; matrix products, arithmetic and copies ran while one was open for 72% -> 31% of each run, Pallas kernels for 0% -> 6%
where the time goes in v1:
time: 838 us; the launch traced here: 825 us
  waiting for transfers between devices  227 us (27%)
  starting transfers between devices  145 us (17%)
  other arithmetic  144 us (17%)
  matrix products  120 us (14%)
  local copies, waits for them, and re-layouts  103 us (12%)
  Pallas kernels  58.7 us (7%)
  between operations  28.1 us (3%)
    ppermute x65, waiting for transfers between devices, swap(): lax.ppermute(values, dim[0], [(i, i ^ 1 << dim[1]) for i in range(size)])  133 us
    ppermute x65, starting transfers between devices, swap(): lax.ppermute(values, dim[0], [(i, i ^ 1 << dim[1]) for i in range(size)])  48.1 us
    dot_general x10, matrix products, product(): return jnp.dot(left, right, preferred_element_type=jnp.float32)  46.3 us
    ppermute x12, waiting for transfers between devices, along_line(): lax.ppermute(left, 'narrow', [(z, z - 1) for z in range(1, size - step +...  44.4 us
    dot_general x9, matrix products, product_right(): lax.dot_general(left, right, (((1,), (1,)), ((), ())), preferred_element_...  33.9 us
    dot_general x11, matrix products, product_left(): lax.dot_general(left, right, (((0,), (0,)), ((), ())), preferred_element_...  33.8 us
    ppermute x9, starting transfers between devices, line(): lax.ppermute(goes.astype(jnp.bfloat16), 'narrow', [(z, z + 1) for z in ra...  31.7 us
    convert_element_type x22, other arithmetic, send(): self.away.append(sum((lax.dynamic_index_in_dim(term, 1 - bit, axis, keepd...  30.4 us
  transfers between devices with their start and end apart: 111, of which 40 were waited for; matrix products, arithmetic and copies ran while one was open for 31% of the time, Pallas kernels for 6%

profile of v1, /device:TPU:0, one launch (start us, length us, event | category | flops | bytes accessed | tf_op | source)
XLA Modules:
  0.0 825.2 jit_solution(10803727426631073468)
XLA Ops:
  11.5 4.9 collective-permute-start.14
  21.9 6.9 all-to-all-start
  36.7 8.8 %collective-permute-done.18 = bf16[24,3584]{1,0:T(8,128)(2,1)S(1)} collective-permute-done((bf16[24,3584]{1,0:T(8,128)(2,1)S(1)}, bf16[24,3584]{1,0:T(8,128)(2,1)S(1)}, u32[]{:S(2)}, u32[]{:S(2)}) %collective-permute-start.18) | collective-permute-done | bytes 172064 | tf_op jit(solution)/shard_map/ppermute | solution.py:158
  49.9 4.9 convert_reduce_fusion.7
  55.9 5.2 collective-permute-start
  64.6 3.6 collective-permute-done.3
  70.2 5.0 collective-permute-done.4
  76.5 5.7 collective-permute-done.5
  89.8 5.0 collective-permute-done.31
  108.8 9.3 %collective-permute-done.6 = bf16[1,4,96,384]{3,2,1,0:T(8,128)(2,1)S(1)} collective-permute-done((bf16[1,4,96,384]{3,2,1,0:T(8,128)(2,1)S(1)}, bf16[1,4,96,384]{3,2,1,0:T(8,128)(2,1)S(1)}, u32[]{:S(2)}, u32[]{:S(2)}) %collective-permute-start.6) | collective-permute-done | bytes 294944 | tf_op jit(solution)/shard_map/ppermute | solution.py:102
  123.2 10.3 %collective-permute-done.21.refs_1_ = bf16[2,4,24,1792]{3,2,1,0:T(8,128)(2,1)S(1)} collective-permute-done((bf16[2,4,24,1792]{3,2,1,0:T(8,128)(2,1)S(1)}, bf16[2,4,24,1792]{3,2,1,0:T(8,128)(2,1)S(1)}, u32[]{:S(2)}, u32[]{:S(2)}) %collective-permute-start.21) | collective-permute-done | bytes 688160 | tf_op jit(solution)/shard_map/ppermute | solution.py:102
  136.0 5.6 collective-permute-done.7.refs_1_
  142.7 3.3 shard_map.486
  169.3 5.6 fusion.23
  178.2 7.0 collective-permute-done.34
  195.2 3.3 add_convert_fusion.query_ref.key_ref.value_ref
  198.6 17.2 %collective-permute-done.37.refs_5_ = bf16[2,4,24,3840]{3,2,1,0:T(8,128)(2,1)} collective-permute-done((bf16[2,4,24,3840]{3,2,1,0:T(8,128)(2,1)}, bf16[2,4,24,3840]{3,2,1,0:T(8,128)(2,1)}, u32[]{:S(2)}, u32[]{:S(2)}) %collective-permute-start.37) | collective-permute-done | bytes 1474592 | tf_op jit(solution)/shard_map/ppermute | solution.py:102
  226.1 15.0 %shard_map.487 = bf16[768,768]{1,0:T(8,128)(2,1)S(1)} custom-call(s32[2]{0:T(128)S(1)} %bitcast.738, bf16[768,2304]{1,0:T(8,128)(2,1)S(1)} %add_convert_fusion.query_ref.key_ref.value_ref, bf16[768,2304]{1,0:T(8,128)(2,1)S(1)} %add_convert_fusion.query_ref.key_ref.value_ref, bf16[768,2304]{1,0:T(8,128)(2,1)S(1)} %add_convert_fusion.query_ref.key_ref.value_ref), custom_call_target="tpu_custom_call" | custom-call | flops 1811939328 | bytes 4718592 | tf_op jit(solution)/shard_map/pallas_call | solution.py:428
  242.9 8.8 %shard_map.488 = (bf16[8,4,24,3072]{3,2,1,0:T(8,128)(2,1)}, bf16[8,4,24,3072]{3,2,1,0:T(8,128)(2,1)}, bf16[8,4,24,768]{3,2,1,0:T(8,128)(2,1)S(1)}, bf16[8,4,24,768]{3,2,1,0:T(8,128)(2,1)S(1)}) custom-call(s32[1]{0:T(128)} %bitcast.1.me_ref, bf16[2,4,24,3840]{3,2,1,0:T(8,128)(2,1)} %pad_maximum_fusion.3.refs_0_, ...), custom_call_target="tpu_custom_call" | custom-call | bytes 23592960 | tf_op jit(solution)/shard_map/pallas_call | solution.py:212
  251.8 12.1 %fusion.21 = (f32[768,3072]{1,0:T(8,128)}, bf16[768,3072]{1,0:T(8,128)(2,1)S(1)}) fusion(f32[3072]{0:T(1024)S(1)} %slice.461, bf16[768,3072]{1,0:T(8,128)(2,1)} %bitcast.748, f32[768,768]{1,0:T(8,128)S(1)} %get-tuple-element.419, f32[768]{0:T(1024)S(1)} %copy-done.83, f32[768]{0:T(1024)S(1)} %copy-done.78, f32[768]{0:T(1024)S(1)} %add_rsqrt_fusion.1, ...), kind=kOutput, calls=%fused_computation.39 | convolution fusion | flops 3652780032 | bytes 21258240 | tf_op jit(solution)/shard_map/dot_general | solution.py:30
  264.0 4.2 fusion.219
  271.6 4.3 collective-permute-start.42
  280.4 3.5 collective-permute-done.45
  285.8 5.3 collective-permute-done.46
  292.6 5.8 collective-permute-done.47
  302.0 4.2 collective-permute-done.52
  311.6 11.0 %collective-permute-done.53.refs_5_ = bf16[2,4,112,384]{3,2,1,0:T(8,128)(2,1)} collective-permute-done((bf16[2,4,112,384]{3,2,1,0:T(8,128)(2,1)}, bf16[2,4,112,384]{3,2,1,0:T(8,128)(2,1)}, u32[]{:S(2)}, u32[]{:S(2)}) %collective-permute-start.53) | collective-permute-done | bytes 688160 | tf_op jit(solution)/shard_map/ppermute | solution.py:102
  336.6 5.5 add_reduce_fusion
  342.3 5.5 fusion.16
  348.6 3.7 all-to-all-start.1
  352.4 14.3 %all-to-all-done.1 = f32[32,28,128]{2,1,0:T(8,128)} async-done(((f32[32,28,128]{2,1,0:T(8,128)}), f32[32,28,128]{2,1,0:T(8,128)}, u32[]{:S(2)}, u32[]{:S(2)}) %all-to-all-start.1) | async-done | bytes 458784 | tf_op jit(solution)/shard_map/all_to_all | solution.py:322
  375.1 9.1 %convert_reduce_fusion = (f32[956]{0:T(1024)}, bf16[3584,956]{0,1:T(8,128)(2,1)S(1)}) fusion(f32[3584]{0:T(1024)S(1)} %broadcast_multiply_fusion, s32[3584]{0:T(1024)} %eq.107, s32[956]{0:T(1024)} %iota_add_fusion, f32[3584]{0:T(1024)} %bitcast.734, f32[3584,956]{0,1:T(8,128)} %copy-done.17, f32[956]{0:T(1024)} %copy-done.111), kind=kLoop, calls=%fused_computation.31 | loop fusion | flops 30835780 | bytes 20612304 | tf_op jit(solution)/shard_map/reduce_sum | solution.py:695
  384.2 8.8 %fusion.221 = f32[3584,768]{1,0:T(8,128)} fusion(bf16[3584,956]{0,1:T(8,128)(2,1)S(1)} %get-tuple-element.153, bf16[956,768]{1,0:T(8,128)(2,1)S(1)} %copy-done.16), kind=kOutput, calls=%fused_computation.596 | convolution fusion | flops 5262802944 | bytes 19331072 | tf_op jit(solution)/shard_map/dot_general | solution.py:30
  393.0 7.3 fusion.213
  400.3 5.0 fusion.39
  418.1 12.5 %collective-permute-done.60 = bf16[2,4,112,384]{3,2,1,0:T(8,128)(2,1)S(1)} collective-permute-done((bf16[2,4,112,384]{3,2,1,0:T(8,128)(2,1)S(1)}, bf16[2,4,112,384]{3,2,1,0:T(8,128)(2,1)S(1)}, u32[]{:S(2)}, u32[]{:S(2)}) %collective-permute-start.60) | collective-permute-done | bytes 688160 | tf_op jit(solution)/shard_map/ppermute | solution.py:102
  437.7 4.0 collective-permute-done.61
  455.2 5.0 collective-permute-start.63
  465.5 7.2 collective-permute-start.64
  489.5 3.9 fusion.190
  493.4 13.2 %convert_reduce_fusion.1 = (f32[3072]{0:T(1024)}, bf16[768,3072]{1,0:T(8,128)(2,1)}) fusion(f32[768,3072]{1,0:T(8,128)} %get-tuple-element.155, bf16[768,3072]{1,0:T(8,128)(2,1)} %bitcast.750, f32[768,768]{1,0:T(8,128)S(1)} %get-tuple-element.291), kind=kOutput, calls=%fused_computation.40 | convolution fusion | flops 3633902592 | bytes 21245952 | tf_op jit(solution)/shard_map/dot_general | solution.py:30
  506.7 7.3 fusion.195
  520.9 9.5 %multiply_reduce_fusion.2 = (f32[768]{0:T(1024)}, f32[768]{0:T(1024)S(1)}, f32[768]{0:T(1024)S(1)}, f32[768]{0:T(1024)}, f32[768,768]{1,0:T(8,128)S(1)}) fusion(f32[768,768]{1,0:T(8,128)S(1)} %copy-done.27, f32[768]{0:T(1024)S(1)} %add_rsqrt_fusion.1, f32[768]{0:T(1024)S(1)} %broadcast_multiply_fusion.8, f32[768]{0:T(1024)S(1)} %copy-done.78, ...), kind=kOutput, calls=%fused_computation.92 | convolution fusion | flops 3629773824 | bytes 16536576 | tf_op jit(solution)/shard_map/dot_general | solution.py:34
  544.1 3.7 all-to-all-start.3
  554.2 4.1 convolution_convert_fusion.1.grad_ref
  579.1 23.2 %shard_map.490 = (bf16[768,768]{1,0:T(8,128)(2,1)S(1)}, bf16[768,768]{1,0:T(8,128)(2,1)S(1)}, bf16[768,768]{1,0:T(8,128)(2,1)S(1)}) custom-call(s32[2]{0:T(128)S(1)} %bitcast.739, bf16[768,2304]{1,0:T(8,128)(2,1)S(1)} %add_convert_fusion.query_ref.key_ref.value_ref, bf16[768,2304]{1,0:T(8,128)(2,1)S(1)} %add_convert_fusion.query_ref.key_ref.value_ref, ...), custom_call_target="tpu_custom_call" | custom-call | flops 4529848320 | bytes 8257536 | tf_op jit(solution)/shard_map/pallas_call | solution.py:451
  612.2 4.0 multiply_reduce_fusion.3
  616.2 5.2 fusion.122
  622.1 4.4 fusion.22
  649.2 3.4 collective-permute-done.83
  652.6 3.4 collective-permute-start.101
  664.4 8.5 %collective-permute-done.89 = bf16[2,4,96,384]{3,2,1,0:T(8,128)(2,1)S(1)} collective-permute-done((bf16[2,4,96,384]{3,2,1,0:T(8,128)(2,1)S(1)}, bf16[2,4,96,384]{3,2,1,0:T(8,128)(2,1)S(1)}, u32[]{:S(2)}, u32[]{:S(2)}) %collective-permute-start.89) | collective-permute-done | bytes 589856 | tf_op jit(solution)/shard_map/ppermute | solution.py:102
  676.8 18.3 %collective-permute-done.77 = bf16[2,4,24,2304]{3,2,1,0:T(8,128)(2,1)S(1)} collective-permute-done((bf16[2,4,24,2304]{3,2,1,0:T(8,128)(2,1)S(1)}, bf16[2,4,24,2304]{3,2,1,0:T(8,128)(2,1)S(1)}, u32[]{:S(2)}, u32[]{:S(2)}) %collective-permute-start.77) | collective-permute-done | bytes 884768 | tf_op jit(solution)/shard_map/ppermute | solution.py:102
  695.8 5.8 collective-permute-done.90
  705.0 6.9 collective-permute-done.78
  719.5 4.0 collective-permute-done.91
  723.5 4.4 collective-permute-start.92
  729.3 5.4 collective-permute-done.92
  737.5 3.5 collective-permute-start.93
  745.6 8.0 collective-permute-done.96
  757.8 5.5 convolution_add_fusion.2
  775.5 3.5 all-to-all-start.2
  782.3 5.1 all-to-all-done.2
  807.3 5.7 multiply_subtract_fusion
  (837 shorter events, 353.1 us)
Async XLA Ops:
  11.5 22.5 %collective-permute-start.14 = (bf16[24,3584]{1,0:T(8,128)(2,1)S(1)}, bf16[24,3584]{1,0:T(8,128)(2,1)S(1)}, u32[]{:S(2)}, u32[]{:S(2)}) collective-permute-start(bf16[24,3584]{1,0:T(8,128)(2,1)S(1)} %concatenate.69), channel_id=1, source_target_pairs={{0,1},{1,2},{2,3},{4,5},{5,6},{6,7},{8,9},{9,10},{10,11},{12,13},{... | collective-permute-start | bytes 516104 | tf_op jit(solution)/shard_map/ppermute | solution.py:157
  16.5 18.2 %collective-permute-start.17 = (bf16[24,3584]{1,0:T(8,128)(2,1)S(1)}, bf16[24,3584]{1,0:T(8,128)(2,1)S(1)}, u32[]{:S(2)}, u32[]{:S(2)}) collective-permute-start(bf16[24,3584]{1,0:T(8,128)(2,1)S(1)} %concatenate.69), channel_id=1, source_target_pairs={{1,0},{2,1},{3,2},{5,4},{6,5},{7,6},{9,8},{10,9},{11,10},{13,12},{... | collective-permute-start | bytes 516104 | tf_op jit(solution)/shard_map/ppermute | solution.py:158
  21.9 24.9 %all-to-all-start = ((s32[32,16,128]{2,1,0:T(8,128)}), s32[32,16,128]{2,1,0:T(8,128)S(1)}, u32[]{:S(2)}, u32[]{:S(2)}) async-start(s32[32,16,128]{2,1,0:T(8,128)} %broadcast_in_dim.253), calls=%async_computation.1 | async-start | bytes 524288 | tf_op jit(solution)/shard_map/all_to_all | solution.py:322
  36.1 26.8 %collective-permute-start.16 = (bf16[24,3584]{1,0:T(8,128)(2,1)S(1)}, bf16[24,3584]{1,0:T(8,128)(2,1)S(1)}, u32[]{:S(2)}, u32[]{:S(2)}) collective-permute-start(bf16[24,3584]{1,0:T(8,128)(2,1)S(1)} %collective-permute-done.15), channel_id=1, source_target_pairs={{2,3},{6,7},{10,11},{14,15},{18,19},{22,23},{26,27},{30,31}} | collective-permute-start | bytes 516104 | tf_op jit(solution)/shard_map/ppermute | solution.py:157
  45.5 17.4 %collective-permute-start.19 = (bf16[24,3584]{1,0:T(8,128)(2,1)S(1)}, bf16[24,3584]{1,0:T(8,128)(2,1)}, u32[]{:S(2)}, u32[]{:S(2)}) collective-permute-start(bf16[24,3584]{1,0:T(8,128)(2,1)S(1)} %collective-permute-done.18), channel_id=1, source_target_pairs={{1,0},{5,4},{9,8},{13,12},{17,16},{21,20},{25,24},{29,28}} | collective-permute-start | bytes 516104 | tf_op jit(solution)/shard_map/ppermute | solution.py:158
  85.4 15.3 %collective-permute-start.24 = (bf16[1,4,24,1792]{3,2,1,0:T(8,128)(2,1)S(1)}, bf16[1,4,24,1792]{3,2,1,0:T(8,128)(2,1)}, u32[]{:S(2)}, u32[]{:S(2)}) collective-permute-start(bf16[1,4,24,1792]{3,2,1,0:T(8,128)(2,1)S(1)} %maximum_bitcast_fusion.3), channel_id=1, source_target_pairs={{0,16},{4,20},{8,24},{12,28},{16,0},{20,4},{24,8},{28,12},{1,17},{... | collective-permute-start | bytes 1032200 | tf_op jit(solution)/shard_map/ppermute | solution.py:102
  87.0 16.3 %collective-permute-start.20 = (bf16[1,4,24,1792]{3,2,1,0:T(8,128)(2,1)S(1)}, bf16[1,4,24,1792]{3,2,1,0:T(8,128)(2,1)}, u32[]{:S(2)}, u32[]{:S(2)}) collective-permute-start(bf16[1,4,24,1792]{3,2,1,0:T(8,128)(2,1)S(1)} %maximum_bitcast_fusion.2), channel_id=1, source_target_pairs={{0,8},{4,12},{8,0},{12,4},{16,24},{20,28},{24,16},{28,20},{1,9},{5... | collective-permute-start | bytes 1032200 | tf_op jit(solution)/shard_map/ppermute | solution.py:102
  89.1 14.8 %collective-permute-start.29 = (bf16[24,7680]{1,0:T(8,128)(2,1)S(1)}, bf16[24,7680]{1,0:T(8,128)(2,1)S(1)}, u32[]{:S(2)}, u32[]{:S(2)}) collective-permute-start(bf16[24,7680]{1,0:T(8,128)(2,1)S(1)} %collective-permute-done.28), channel_id=1, source_target_pairs={{1,2},{2,3},{5,6},{6,7},{9,10},{10,11},{13,14},{14,15},{17,18},{18... | collective-permute-start | bytes 1105928 | tf_op jit(solution)/shard_map/ppermute | solution.py:157
  101.7 19.9 %collective-permute-start.25 = (bf16[2,4,24,1792]{3,2,1,0:T(8,128)(2,1)S(1)}, bf16[2,4,24,1792]{3,2,1,0:T(8,128)(2,1)S(1)}, u32[]{:S(2)}, u32[]{:S(2)}) collective-permute-start(bf16[2,4,24,1792]{3,2,1,0:T(8,128)(2,1)S(1)} %pad_maximum_fusion.6.refs_4_), channel_id=1, source_target_pairs={{0,8},{4,12},{8,0},{12,4},{16,24},{20,28},{24,16},{28,20},{1,9},{5... | collective-permute-start | bytes 2064392 | tf_op jit(solution)/shard_map/ppermute | solution.py:102
  103.3 14.8 %collective-permute-start.6 = (bf16[1,4,96,384]{3,2,1,0:T(8,128)(2,1)S(1)}, bf16[1,4,96,384]{3,2,1,0:T(8,128)(2,1)S(1)}, u32[]{:S(2)}, u32[]{:S(2)}) collective-permute-start(bf16[1,4,96,384]{3,2,1,0:T(8,128)(2,1)S(1)} %maximum_bitcast_fusion.6), channel_id=1, source_target_pairs={{0,8},{4,12},{8,0},{12,4},{16,24},{20,28},{24,16},{28,20},{1,9},{5... | collective-permute-start | bytes 884744 | tf_op jit(solution)/shard_map/ppermute | solution.py:102
  103.8 14.9 %collective-permute-start.30 = (bf16[24,7680]{1,0:T(8,128)(2,1)S(1)}, bf16[24,7680]{1,0:T(8,128)(2,1)S(1)}, u32[]{:S(2)}, u32[]{:S(2)}) collective-permute-start(bf16[24,7680]{1,0:T(8,128)(2,1)S(1)} %collective-permute-done.29), channel_id=1, source_target_pairs={{2,3},{6,7},{10,11},{14,15},{18,19},{22,23},{26,27},{30,31}} | collective-permute-start | bytes 1105928 | tf_op jit(solution)/shard_map/ppermute | solution.py:157
  106.3 12.5 %collective-permute-start.33 = (bf16[24,7680]{1,0:T(8,128)(2,1)}, bf16[24,7680]{1,0:T(8,128)(2,1)S(1)}, u32[]{:S(2)}, u32[]{:S(2)}) collective-permute-start(bf16[24,7680]{1,0:T(8,128)(2,1)} %collective-permute-done.32), channel_id=1, source_target_pairs={{1,0},{5,4},{9,8},{13,12},{17,16},{21,20},{25,24},{29,28}} | collective-permute-start | bytes 1105928 | tf_op jit(solution)/shard_map/ppermute | solution.py:158
  108.7 14.6 %collective-permute-start.26 = (bf16[2,4,24,1792]{3,2,1,0:T(8,128)(2,1)S(1)}, bf16[2,4,24,1792]{3,2,1,0:T(8,128)(2,1)S(1)}, u32[]{:S(2)}, u32[]{:S(2)}) collective-permute-start(bf16[2,4,24,1792]{3,2,1,0:T(8,128)(2,1)S(1)} %pad_maximum_fusion.6.refs_4_), channel_id=1, source_target_pairs={{0,4},{4,0},{8,12},{12,8},{16,20},{20,16},{24,28},{28,24},{1,5},{5... | collective-permute-start | bytes 2064392 | tf_op jit(solution)/shard_map/ppermute | solution.py:102
  118.1 15.4 %collective-permute-start.21 = (bf16[2,4,24,1792]{3,2,1,0:T(8,128)(2,1)S(1)}, bf16[2,4,24,1792]{3,2,1,0:T(8,128)(2,1)S(1)}, u32[]{:S(2)}, u32[]{:S(2)}) collective-permute-start(bf16[2,4,24,1792]{3,2,1,0:T(8,128)(2,1)S(1)} %pad_maximum_fusion.5.refs_0_), channel_id=1, source_target_pairs={{0,16},{4,20},{8,24},{12,28},{16,0},{20,4},{24,8},{28,12},{1,17},{... | collective-permute-start | bytes 2064392 | tf_op jit(solution)/shard_map/ppermute | solution.py:102
  118.7 16.7 %collective-permute-start.22 = (bf16[2,4,24,1792]{3,2,1,0:T(8,128)(2,1)S(1)}, bf16[2,4,24,1792]{3,2,1,0:T(8,128)(2,1)S(1)}, u32[]{:S(2)}, u32[]{:S(2)}) collective-permute-start(bf16[2,4,24,1792]{3,2,1,0:T(8,128)(2,1)S(1)} %pad_maximum_fusion.5.refs_0_), channel_id=1, source_target_pairs={{0,4},{4,0},{8,12},{12,8},{16,20},{20,16},{24,28},{28,24},{1,5},{5... | collective-permute-start | bytes 2064392 | tf_op jit(solution)/shard_map/ppermute | solution.py:102
  118.8 17.2 %collective-permute-start.11 = (bf16[2,4,96,384]{3,2,1,0:T(8,128)(2,1)S(1)}, bf16[2,4,96,384]{3,2,1,0:T(8,128)(2,1)S(1)}, u32[]{:S(2)}, u32[]{:S(2)}) collective-permute-start(bf16[2,4,96,384]{3,2,1,0:T(8,128)(2,1)S(1)} %pad_maximum_fusion.10.refs_4_), channel_id=1, source_target_pairs={{0,8},{4,12},{8,0},{12,4},{16,24},{20,28},{24,16},{28,20},{1,9},{5... | collective-permute-start | bytes 1769480 | tf_op jit(solution)/shard_map/ppermute | solution.py:102
  121.7 20.0 %collective-permute-start.7 = (bf16[2,4,96,384]{3,2,1,0:T(8,128)(2,1)S(1)}, bf16[2,4,96,384]{3,2,1,0:T(8,128)(2,1)S(1)}, u32[]{:S(2)}, u32[]{:S(2)}) collective-permute-start(bf16[2,4,96,384]{3,2,1,0:T(8,128)(2,1)S(1)} %pad_maximum_fusion.9.refs_0_), channel_id=1, source_target_pairs={{0,16},{4,20},{8,24},{12,28},{16,0},{20,4},{24,8},{28,12},{1,17},{... | collective-permute-start | bytes 1769480 | tf_op jit(solution)/shard_map/ppermute | solution.py:102
  123.2 18.5 %collective-permute-start.27 = (bf16[2,4,24,1792]{3,2,1,0:T(8,128)(2,1)S(1)}, bf16[2,4,24,1792]{3,2,1,0:T(8,128)(2,1)S(1)}, u32[]{:S(2)}, u32[]{:S(2)}) collective-permute-start(bf16[2,4,24,1792]{3,2,1,0:T(8,128)(2,1)S(1)} %collective-permute-done.25.refs_5_), channel_id=1, source_target_pairs={{0,4},{4,0},{8,12},{12,8},{16,20},{20,16},{24,28},{28,24},{1,5},{5... | collective-permute-start | bytes 2064392 | tf_op jit(solution)/shard_map/ppermute | solution.py:102
  135.5 30.2 %collective-permute-start.12 = (bf16[2,4,96,384]{3,2,1,0:T(8,128)(2,1)S(1)}, bf16[2,4,96,384]{3,2,1,0:T(8,128)(2,1)S(1)}, u32[]{:S(2)}, u32[]{:S(2)}) collective-permute-start(bf16[2,4,96,384]{3,2,1,0:T(8,128)(2,1)S(1)} %pad_maximum_fusion.10.refs_4_), channel_id=1, source_target_pairs={{0,4},{4,0},{8,12},{12,8},{16,20},{20,16},{24,28},{28,24},{1,5},{5... | collective-permute-start | bytes 1769480 | tf_op jit(solution)/shard_map/ppermute | solution.py:102
  136.0 31.1 %collective-permute-start.8 = (bf16[2,4,96,384]{3,2,1,0:T(8,128)(2,1)S(1)}, bf16[2,4,96,384]{3,2,1,0:T(8,128)(2,1)S(1)}, u32[]{:S(2)}, u32[]{:S(2)}) collective-permute-start(bf16[2,4,96,384]{3,2,1,0:T(8,128)(2,1)S(1)} %pad_maximum_fusion.9.refs_0_), channel_id=1, source_target_pairs={{0,4},{4,0},{8,12},{12,8},{16,20},{20,16},{24,28},{28,24},{1,5},{5... | collective-permute-start | bytes 1769480 | tf_op jit(solution)/shard_map/ppermute | solution.py:102
  141.7 25.4 %collective-permute-start.13 = (bf16[2,4,96,384]{3,2,1,0:T(8,128)(2,1)S(1)}, bf16[2,4,96,384]{3,2,1,0:T(8,128)(2,1)}, u32[]{:S(2)}, u32[]{:S(2)}) collective-permute-start(bf16[2,4,96,384]{3,2,1,0:T(8,128)(2,1)S(1)} %collective-permute-done.11.refs_5_), channel_id=1, source_target_pairs={{0,4},{4,0},{8,12},{12,8},{16,20},{20,16},{24,28},{28,24},{1,5},{5... | collective-permute-start | bytes 1769480 | tf_op jit(solution)/shard_map/ppermute | solution.py:102
  141.7 25.4 %collective-permute-start.9 = (bf16[2,4,96,384]{3,2,1,0:T(8,128)(2,1)S(1)}, bf16[2,4,96,384]{3,2,1,0:T(8,128)(2,1)}, u32[]{:S(2)}, u32[]{:S(2)}) collective-permute-start(bf16[2,4,96,384]{3,2,1,0:T(8,128)(2,1)S(1)} %collective-permute-done.7.refs_1_), channel_id=1, source_target_pairs={{0,4},{4,0},{8,12},{12,8},{16,20},{20,16},{24,28},{28,24},{1,5},{5... | collective-permute-start | bytes 1769480 | tf_op jit(solution)/shard_map/ppermute | solution.py:102
  142.2 32.7 %collective-permute-start.36 = (bf16[1,4,24,3840]{3,2,1,0:T(8,128)(2,1)}, bf16[1,4,24,3840]{3,2,1,0:T(8,128)(2,1)}, u32[]{:S(2)}, u32[]{:S(2)}) collective-permute-start(bf16[1,4,24,3840]{3,2,1,0:T(8,128)(2,1)} %maximum_bitcast_fusion.1), channel_id=1, source_target_pairs={{0,16},{4,20},{8,24},{12,28},{16,0},{20,4},{24,8},{28,12},{1,17},{... | collective-permute-start | bytes 2211848 | tf_op jit(solution)/shard_map/ppermute | solution.py:102
  165.6 19.6 %collective-permute-start.34 = (bf16[1,4,24,3840]{3,2,1,0:T(8,128)(2,1)}, bf16[1,4,24,3840]{3,2,1,0:T(8,128)(2,1)S(1)}, u32[]{:S(2)}, u32[]{:S(2)}) collective-permute-start(bf16[1,4,24,3840]{3,2,1,0:T(8,128)(2,1)} %maximum_bitcast_fusion), channel_id=1, source_target_pairs={{0,8},{4,12},{8,0},{12,4},{16,24},{20,28},{24,16},{28,20},{1,9},{5... | collective-permute-start | bytes 2211848 | tf_op jit(solution)/shard_map/ppermute | solution.py:102
  177.6 38.1 %collective-permute-start.37 = (bf16[2,4,24,3840]{3,2,1,0:T(8,128)(2,1)}, bf16[2,4,24,3840]{3,2,1,0:T(8,128)(2,1)}, u32[]{:S(2)}, u32[]{:S(2)}) collective-permute-start(bf16[2,4,24,3840]{3,2,1,0:T(8,128)(2,1)} %pad_maximum_fusion.4.refs_4_), channel_id=1, source_target_pairs={{0,8},{4,12},{8,0},{12,4},{16,24},{20,28},{24,16},{28,20},{1,9},{5... | collective-permute-start | bytes 4423688 | tf_op jit(solution)/shard_map/ppermute | solution.py:102
  186.4 32.2 %collective-permute-start.35 = (bf16[2,4,24,3840]{3,2,1,0:T(8,128)(2,1)}, bf16[2,4,24,3840]{3,2,1,0:T(8,128)(2,1)}, u32[]{:S(2)}, u32[]{:S(2)}) collective-permute-start(bf16[2,4,24,3840]{3,2,1,0:T(8,128)(2,1)} %pad_maximum_fusion.3.refs_0_), channel_id=1, source_target_pairs={{0,16},{4,20},{8,24},{12,28},{16,0},{20,4},{24,8},{28,12},{1,17},{... | collective-permute-start | bytes 4423688 | tf_op jit(solution)/shard_map/ppermute | solution.py:102
  218.7 24.2 %collective-permute-start.38 = (bf16[2,4,24,3840]{3,2,1,0:T(8,128)(2,1)}, bf16[2,4,24,3840]{3,2,1,0:T(8,128)(2,1)}, u32[]{:S(2)}, u32[]{:S(2)}) collective-permute-start(bf16[2,4,24,3840]{3,2,1,0:T(8,128)(2,1)} %pad_maximum_fusion.3.refs_0_), channel_id=1, source_target_pairs={{0,4},{4,0},{8,12},{12,8},{16,20},{20,16},{24,28},{28,24},{1,5},{5... | collective-permute-start | bytes 4423688 | tf_op jit(solution)/shard_map/ppermute | solution.py:102
  218.7 24.2 %collective-permute-start.39 = (bf16[2,4,24,3840]{3,2,1,0:T(8,128)(2,1)}, bf16[2,4,24,3840]{3,2,1,0:T(8,128)(2,1)}, u32[]{:S(2)}, u32[]{:S(2)}) collective-permute-start(bf16[2,4,24,3840]{3,2,1,0:T(8,128)(2,1)} %collective-permute-done.35.refs_1_), channel_id=1, source_target_pairs={{0,4},{4,0},{8,12},{12,8},{16,20},{20,16},{24,28},{28,24},{1,5},{5... | collective-permute-start | bytes 4423688 | tf_op jit(solution)/shard_map/ppermute | solution.py:102
  219.2 23.7 %collective-permute-start.40 = (bf16[2,4,24,3840]{3,2,1,0:T(8,128)(2,1)}, bf16[2,4,24,3840]{3,2,1,0:T(8,128)(2,1)}, u32[]{:S(2)}, u32[]{:S(2)}) collective-permute-start(bf16[2,4,24,3840]{3,2,1,0:T(8,128)(2,1)} %pad_maximum_fusion.4.refs_4_), channel_id=1, source_target_pairs={{0,4},{4,0},{8,12},{12,8},{16,20},{20,16},{24,28},{28,24},{1,5},{5... | collective-permute-start | bytes 4423688 | tf_op jit(solution)/shard_map/ppermute | solution.py:102
  219.2 23.7 %collective-permute-start.41 = (bf16[2,4,24,3840]{3,2,1,0:T(8,128)(2,1)}, bf16[2,4,24,3840]{3,2,1,0:T(8,128)(2,1)}, u32[]{:S(2)}, u32[]{:S(2)}) collective-permute-start(bf16[2,4,24,3840]{3,2,1,0:T(8,128)(2,1)} %collective-permute-done.37.refs_5_), channel_id=1, source_target_pairs={{0,4},{4,0},{8,12},{12,8},{16,20},{20,16},{24,28},{28,24},{1,5},{5... | collective-permute-start | bytes 4423688 | tf_op jit(solution)/shard_map/ppermute | solution.py:102
  307.1 15.5 %collective-permute-start.53 = (bf16[2,4,112,384]{3,2,1,0:T(8,128)(2,1)}, bf16[2,4,112,384]{3,2,1,0:T(8,128)(2,1)}, u32[]{:S(2)}, u32[]{:S(2)}) collective-permute-start(bf16[2,4,112,384]{3,2,1,0:T(8,128)(2,1)} %pad_maximum_fusion.8.refs_4_), channel_id=1, source_target_pairs={{0,8},{4,12},{8,0},{12,4},{16,24},{20,28},{24,16},{28,20},{1,9},{5... | collective-permute-start | bytes 2064392 | tf_op jit(solution)/shard_map/ppermute | solution.py:102
  311.1 22.5 %collective-permute-start.54 = (bf16[2,4,112,384]{3,2,1,0:T(8,128)(2,1)}, bf16[2,4,112,384]{3,2,1,0:T(8,128)(2,1)}, u32[]{:S(2)}, u32[]{:S(2)}) collective-permute-start(bf16[2,4,112,384]{3,2,1,0:T(8,128)(2,1)} %pad_maximum_fusion.8.refs_4_), channel_id=1, source_target_pairs={{0,4},{4,0},{8,12},{12,8},{16,20},{20,16},{24,28},{28,24},{1,5},{5... | collective-permute-start | bytes 2064392 | tf_op jit(solution)/shard_map/ppermute | solution.py:102
  311.1 22.5 %collective-permute-start.50 = (bf16[2,4,112,384]{3,2,1,0:T(8,128)(2,1)}, bf16[2,4,112,384]{3,2,1,0:T(8,128)(2,1)}, u32[]{:S(2)}, u32[]{:S(2)}) collective-permute-start(bf16[2,4,112,384]{3,2,1,0:T(8,128)(2,1)} %pad_maximum_fusion.7.refs_0_), channel_id=1, source_target_pairs={{0,4},{4,0},{8,12},{12,8},{16,20},{20,16},{24,28},{28,24},{1,5},{5... | collective-permute-start | bytes 2064392 | tf_op jit(solution)/shard_map/ppermute | solution.py:102
  348.6 18.1 %all-to-all-start.1 = ((f32[32,28,128]{2,1,0:T(8,128)}), f32[32,28,128]{2,1,0:T(8,128)}, u32[]{:S(2)}, u32[]{:S(2)}) async-start(f32[32,28,128]{2,1,0:T(8,128)} %broadcast_in_dim.272), calls=%async_computation.2 | async-start | bytes 1048576 | tf_op jit(solution)/shard_map/all_to_all | solution.py:322
  412.8 17.9 %collective-permute-start.60 = (bf16[2,4,112,384]{3,2,1,0:T(8,128)(2,1)S(1)}, bf16[2,4,112,384]{3,2,1,0:T(8,128)(2,1)S(1)}, u32[]{:S(2)}, u32[]{:S(2)}) collective-permute-start(bf16[2,4,112,384]{3,2,1,0:T(8,128)(2,1)S(1)} %fusion.40), channel_id=1, source_target_pairs={{0,8},{4,12},{8,0},{12,4},{16,24},{20,28},{24,16},{28,20},{1,9},{5... | collective-permute-start | bytes 2064392 | tf_op jit(solution)/shard_map/ppermute | solution.py:102
  416.6 17.6 %collective-permute-start.57 = (bf16[2,4,112,384]{3,2,1,0:T(8,128)(2,1)S(1)}, bf16[2,4,112,384]{3,2,1,0:T(8,128)(2,1)S(1)}, u32[]{:S(2)}, u32[]{:S(2)}) collective-permute-start(bf16[2,4,112,384]{3,2,1,0:T(8,128)(2,1)S(1)} %fusion.41), channel_id=1, source_target_pairs={{0,16},{4,20},{8,24},{12,28},{16,0},{20,4},{24,8},{28,12},{1,17},{... | collective-permute-start | bytes 2064392 | tf_op jit(solution)/shard_map/ppermute | solution.py:102
  437.7 23.8 %collective-permute-start.71 = (bf16[2,2,4,24,768]{4,3,2,1,0:T(8,128)(2,1)}, bf16[2,2,4,24,768]{4,3,2,1,0:T(8,128)(2,1)}, u32[]{:S(2)}, u32[]{:S(2)}) collective-permute-start(bf16[2,2,4,24,768]{4,3,2,1,0:T(8,128)(2,1)} %fusion.73), channel_id=1, source_target_pairs={{0,4},{4,0},{8,12},{12,8},{16,20},{20,16},{24,28},{28,24},{1,5},{5... | collective-permute-start | bytes 1769480 | tf_op jit(solution)/shard_map/ppermute | solution.py:102
  465.5 12.5 %collective-permute-start.64 = (bf16[112,768]{1,0:T(8,128)(2,1)S(1)}, bf16[112,768]{1,0:T(8,128)(2,1)S(1)}, u32[]{:S(2)}, u32[]{:S(2)}) collective-permute-start(bf16[112,768]{1,0:T(8,128)(2,1)S(1)} %get-tuple-element.315), channel_id=1, source_target_pairs={{0,1},{1,2},{2,3},{4,5},{5,6},{6,7},{8,9},{9,10},{10,11},{12,13},{... | collective-permute-start | bytes 516104 | tf_op jit(solution)/shard_map/ppermute | solution.py:292
  476.4 60.9 %collective-permute-start.100 = (bf16[4,24,768]{2,1,0:T(8,128)(2,1)}, bf16[4,24,768]{2,1,0:T(8,128)(2,1)}, u32[]{:S(2)}, u32[]{:S(2)}) collective-permute-start(bf16[4,24,768]{2,1,0:T(8,128)(2,1)} %fusion.145), channel_id=1, source_target_pairs={{0,16},{4,20},{8,24},{12,28},{16,0},{20,4},{24,8},{28,12},{1,17},{... | collective-permute-start | bytes 442376 | tf_op jit(solution)/shard_map/ppermute | solution.py:102
  516.0 56.4 %collective-permute-start.68 = (bf16[2,2,4,24,3072]{4,3,2,1,0:T(8,128)(2,1)}, bf16[2,2,4,24,3072]{4,3,2,1,0:T(8,128)(2,1)}, u32[]{:S(2)}, u32[]{:S(2)}) collective-permute-start(bf16[2,2,4,24,3072]{4,3,2,1,0:T(8,128)(2,1)} %fusion.28), channel_id=1, source_target_pairs={{0,4},{4,0},{8,12},{12,8},{16,20},{20,16},{24,28},{28,24},{1,5},{5... | collective-permute-start | bytes 7077896 | tf_op jit(solution)/shard_map/ppermute | solution.py:102
  518.3 21.0 %collective-permute-start.69 = (bf16[2,2,4,24,768]{4,3,2,1,0:T(8,128)(2,1)S(1)}, bf16[2,2,4,24,768]{4,3,2,1,0:T(8,128)(2,1)S(1)}, u32[]{:S(2)}, u32[]{:S(2)}) collective-permute-start(bf16[2,2,4,24,768]{4,3,2,1,0:T(8,128)(2,1)S(1)} %fusion.72), channel_id=1, source_target_pairs={{0,4},{4,0},{8,12},{12,8},{16,20},{20,16},{24,28},{28,24},{1,5},{5... | collective-permute-start | bytes 1769480 | tf_op jit(solution)/shard_map/ppermute | solution.py:102
  520.1 55.0 %collective-permute-start.70 = (bf16[2,2,4,24,3072]{4,3,2,1,0:T(8,128)(2,1)}, bf16[2,2,4,24,3072]{4,3,2,1,0:T(8,128)(2,1)}, u32[]{:S(2)}, u32[]{:S(2)}) collective-permute-start(bf16[2,2,4,24,3072]{4,3,2,1,0:T(8,128)(2,1)} %fusion.29), channel_id=1, source_target_pairs={{0,4},{4,0},{8,12},{12,8},{16,20},{20,16},{24,28},{28,24},{1,5},{5... | collective-permute-start | bytes 7077896 | tf_op jit(solution)/shard_map/ppermute | solution.py:102
  535.6 12.8 %collective-permute-start.79 = (bf16[2,2,4,24,768]{4,3,2,1,0:T(8,128)(2,1)}, bf16[2,2,4,24,768]{4,3,2,1,0:T(8,128)(2,1)}, u32[]{:S(2)}, u32[]{:S(2)}) collective-permute-start(bf16[2,2,4,24,768]{4,3,2,1,0:T(8,128)(2,1)} %fusion.74), channel_id=1, source_target_pairs={{0,4},{4,0},{8,12},{12,8},{16,20},{20,16},{24,28},{28,24},{1,5},{5... | collective-permute-start | bytes 1769480 | tf_op jit(solution)/shard_map/ppermute | solution.py:102
  544.1 230.7 %all-to-all-start.3 = ((f32[32,8,128]{2,1,0:T(8,128)}), f32[32,8,128]{2,1,0:T(8,128)}, u32[]{:S(2)}, u32[]{:S(2)}) async-start(f32[32,8,128]{2,1,0:T(8,128)} %broadcast_in_dim.296), calls=%async_computation.4 | async-start | bytes 262144 | tf_op jit(solution)/shard_map/all_to_all | solution.py:322
  550.3 16.7 %collective-permute-start.80 = (bf16[2,4,24,768]{3,2,1,0:T(8,128)(2,1)}, bf16[2,4,24,768]{3,2,1,0:T(8,128)(2,1)}, u32[]{:S(2)}, u32[]{:S(2)}) collective-permute-start(bf16[2,4,24,768]{3,2,1,0:T(8,128)(2,1)} %fusion.79), channel_id=1, source_target_pairs={{0,8},{4,12},{8,0},{12,4},{16,24},{20,28},{24,16},{28,20},{1,9},{5... | collective-permute-start | bytes 884744 | tf_op jit(solution)/shard_map/ppermute | solution.py:102
  553.8 16.6 %collective-permute-start.98 = (bf16[4,24,768]{2,1,0:T(8,128)(2,1)}, bf16[4,24,768]{2,1,0:T(8,128)(2,1)}, u32[]{:S(2)}, u32[]{:S(2)}) collective-permute-start(bf16[4,24,768]{2,1,0:T(8,128)(2,1)} %fusion.146), channel_id=1, source_target_pairs={{0,8},{4,12},{8,0},{12,4},{16,24},{20,28},{24,16},{28,20},{1,9},{5... | collective-permute-start | bytes 442376 | tf_op jit(solution)/shard_map/ppermute | solution.py:102
  568.7 143.4 %collective-permute-start.81 = (bf16[4,24,768]{2,1,0:T(8,128)(2,1)}, bf16[4,24,768]{2,1,0:T(8,128)(2,1)}, u32[]{:S(2)}, u32[]{:S(2)}) collective-permute-start(bf16[4,24,768]{2,1,0:T(8,128)(2,1)} %fusion.142), channel_id=1, source_target_pairs={{0,16},{4,20},{8,24},{12,28},{16,0},{20,4},{24,8},{28,12},{1,17},{... | collective-permute-start | bytes 442376 | tf_op jit(solution)/shard_map/ppermute | solution.py:102
  574.7 29.5 %collective-permute-start.72 = (bf16[2,4,24,3072]{3,2,1,0:T(8,128)(2,1)S(1)}, bf16[2,4,24,3072]{3,2,1,0:T(8,128)(2,1)S(1)}, u32[]{:S(2)}, u32[]{:S(2)}) collective-permute-start(bf16[2,4,24,3072]{3,2,1,0:T(8,128)(2,1)S(1)} %fusion.31), channel_id=1, source_target_pairs={{0,16},{4,20},{8,24},{12,28},{16,0},{20,4},{24,8},{28,12},{1,17},{... | collective-permute-start | bytes 3538952 | tf_op jit(solution)/shard_map/ppermute | solution.py:102
  577.3 30.2 %collective-permute-start.74 = (bf16[2,4,24,3072]{3,2,1,0:T(8,128)(2,1)S(1)}, bf16[2,4,24,3072]{3,2,1,0:T(8,128)(2,1)S(1)}, u32[]{:S(2)}, u32[]{:S(2)}) collective-permute-start(bf16[2,4,24,3072]{3,2,1,0:T(8,128)(2,1)S(1)} %fusion.30), channel_id=1, source_target_pairs={{0,8},{4,12},{8,0},{12,4},{16,24},{20,28},{24,16},{28,20},{1,9},{5... | collective-permute-start | bytes 3538952 | tf_op jit(solution)/shard_map/ppermute | solution.py:102
  607.3 35.9 %collective-permute-start.97 = (bf16[4,24,3072]{2,1,0:T(8,128)(2,1)}, bf16[4,24,3072]{2,1,0:T(8,128)(2,1)}, u32[]{:S(2)}, u32[]{:S(2)}) collective-permute-start(bf16[4,24,3072]{2,1,0:T(8,128)(2,1)} %fusion.49), channel_id=1, source_target_pairs={{0,8},{4,12},{8,0},{12,4},{16,24},{20,28},{24,16},{28,20},{1,9},{5... | collective-permute-start | bytes 1769480 | tf_op jit(solution)/shard_map/ppermute | solution.py:102
  610.4 34.9 %collective-permute-start.99 = (bf16[4,24,3072]{2,1,0:T(8,128)(2,1)}, bf16[4,24,3072]{2,1,0:T(8,128)(2,1)}, u32[]{:S(2)}, u32[]{:S(2)}) collective-permute-start(bf16[4,24,3072]{2,1,0:T(8,128)(2,1)} %fusion.48), channel_id=1, source_target_pairs={{0,16},{4,20},{8,24},{12,28},{16,0},{20,4},{24,8},{28,12},{1,17},{... | collective-permute-start | bytes 1769480 | tf_op jit(solution)/shard_map/ppermute | solution.py:102
  630.8 25.3 %collective-permute-start.88 = (bf16[2,2,4,96,384]{4,3,2,1,0:T(8,128)(2,1)}, bf16[2,2,4,96,384]{4,3,2,1,0:T(8,128)(2,1)}, u32[]{:S(2)}, u32[]{:S(2)}) collective-permute-start(bf16[2,2,4,96,384]{4,3,2,1,0:T(8,128)(2,1)} %fusion.43), channel_id=1, source_target_pairs={{0,4},{4,0},{8,12},{12,8},{16,20},{20,16},{24,28},{28,24},{1,5},{5... | collective-permute-start | bytes 3538952 | tf_op jit(solution)/shard_map/ppermute | solution.py:102
  642.5 15.6 %collective-permute-start.85 = (bf16[2,2,4,96,384]{4,3,2,1,0:T(8,128)(2,1)S(1)}, bf16[2,2,4,96,384]{4,3,2,1,0:T(8,128)(2,1)S(1)}, u32[]{:S(2)}, u32[]{:S(2)}) collective-permute-start(bf16[2,2,4,96,384]{4,3,2,1,0:T(8,128)(2,1)S(1)} %fusion.42), channel_id=1, source_target_pairs={{0,4},{4,0},{8,12},{12,8},{16,20},{20,16},{24,28},{28,24},{1,5},{5... | collective-permute-start | bytes 3538952 | tf_op jit(solution)/shard_map/ppermute | solution.py:102
  643.1 16.7 %collective-permute-start.76 = (bf16[2,2,4,24,2304]{4,3,2,1,0:T(8,128)(2,1)S(1)}, bf16[2,2,4,24,2304]{4,3,2,1,0:T(8,128)(2,1)S(1)}, u32[]{:S(2)}, u32[]{:S(2)}) collective-permute-start(bf16[2,2,4,24,2304]{4,3,2,1,0:T(8,128)(2,1)S(1)} %fusion.35), channel_id=1, source_target_pairs={{0,4},{4,0},{8,12},{12,8},{16,20},{20,16},{24,28},{28,24},{1,5},{5... | collective-permute-start | bytes 5308424 | tf_op jit(solution)/shard_map/ppermute | solution.py:102
  656.2 59.5 %collective-permute-start.104 = (bf16[24,7680]{1,0:T(8,128)(2,1)S(1)}, bf16[24,7680]{1,0:T(8,128)(2,1)S(1)}, u32[]{:S(2)}, u32[]{:S(2)}) collective-permute-start(bf16[24,7680]{1,0:T(8,128)(2,1)S(1)} %get-tuple-element.310), channel_id=1, source_target_pairs={{3,2},{7,6},{11,10},{15,14},{19,18},{23,22},{27,26},{31,30}} | collective-permute-start | bytes 1105928 | tf_op jit(solution)/shard_map/ppermute | solution.py:299
  658.1 14.7 %collective-permute-start.89 = (bf16[2,4,96,384]{3,2,1,0:T(8,128)(2,1)S(1)}, bf16[2,4,96,384]{3,2,1,0:T(8,128)(2,1)S(1)}, u32[]{:S(2)}, u32[]{:S(2)}) collective-permute-start(bf16[2,4,96,384]{3,2,1,0:T(8,128)(2,1)S(1)} %fusion.46), channel_id=1, source_target_pairs={{0,8},{4,12},{8,0},{12,4},{16,24},{20,28},{24,16},{28,20},{1,9},{5... | collective-permute-start | bytes 1769480 | tf_op jit(solution)/shard_map/ppermute | solution.py:102
  659.8 16.3 %collective-permute-start.86 = (bf16[2,4,96,384]{3,2,1,0:T(8,128)(2,1)S(1)}, bf16[2,4,96,384]{3,2,1,0:T(8,128)(2,1)S(1)}, u32[]{:S(2)}, u32[]{:S(2)}) collective-permute-start(bf16[2,4,96,384]{3,2,1,0:T(8,128)(2,1)S(1)} %fusion.47), channel_id=1, source_target_pairs={{0,16},{4,20},{8,24},{12,28},{16,0},{20,4},{24,8},{28,12},{1,17},{... | collective-permute-start | bytes 1769480 | tf_op jit(solution)/shard_map/ppermute | solution.py:102
  663.8 31.4 %collective-permute-start.77 = (bf16[2,4,24,2304]{3,2,1,0:T(8,128)(2,1)S(1)}, bf16[2,4,24,2304]{3,2,1,0:T(8,128)(2,1)S(1)}, u32[]{:S(2)}, u32[]{:S(2)}) collective-permute-start(bf16[2,4,24,2304]{3,2,1,0:T(8,128)(2,1)S(1)} %fusion.36), channel_id=1, source_target_pairs={{0,16},{4,20},{8,24},{12,28},{16,0},{20,4},{24,8},{28,12},{1,17},{... | collective-permute-start | bytes 2654216 | tf_op jit(solution)/shard_map/ppermute | solution.py:102
  672.8 40.5 %collective-permute-start.84 = (bf16[4,24,512]{2,1,0:T(8,128)(2,1)S(1)}, bf16[4,24,512]{2,1,0:T(8,128)(2,1)S(1)}, u32[]{:S(2)}, u32[]{:S(2)}) collective-permute-start(bf16[4,24,512]{2,1,0:T(8,128)(2,1)S(1)} %fusion.148), channel_id=1, source_target_pairs={{0,16},{4,20},{8,24},{12,28},{16,0},{20,4},{24,8},{28,12},{1,17},{... | collective-permute-start | bytes 294920 | tf_op jit(solution)/shard_map/ppermute | solution.py:102
  676.1 25.5 %collective-permute-start.90 = (bf16[4,96,384]{2,1,0:T(8,128)(2,1)S(1)}, bf16[4,96,384]{2,1,0:T(8,128)(2,1)S(1)}, u32[]{:S(2)}, u32[]{:S(2)}) collective-permute-start(bf16[4,96,384]{2,1,0:T(8,128)(2,1)S(1)} %fusion.75), channel_id=1, source_target_pairs={{0,16},{4,20},{8,24},{12,28},{16,0},{20,4},{24,8},{28,12},{1,17},{... | collective-permute-start | bytes 884744 | tf_op jit(solution)/shard_map/ppermute | solution.py:102
  703.3 12.5 %collective-permute-start.102 = (bf16[24,7680]{1,0:T(8,128)(2,1)S(1)}, bf16[24,7680]{1,0:T(8,128)(2,1)S(1)}, u32[]{:S(2)}, u32[]{:S(2)}) collective-permute-start(bf16[24,7680]{1,0:T(8,128)(2,1)S(1)} %fusion.59), channel_id=1, source_target_pairs={{0,1},{1,2},{4,5},{5,6},{8,9},{9,10},{12,13},{13,14},{16,17},{17,1... | collective-permute-start | bytes 1105928 | tf_op jit(solution)/shard_map/ppermute | solution.py:292
  715.9 12.0 %collective-permute-start.105 = (bf16[24,7680]{1,0:T(8,128)(2,1)S(1)}, bf16[24,7680]{1,0:T(8,128)(2,1)S(1)}, u32[]{:S(2)}, u32[]{:S(2)}) collective-permute-start(bf16[24,7680]{1,0:T(8,128)(2,1)S(1)} %get-tuple-element.308), channel_id=1, source_target_pairs={{2,1},{3,2},{6,5},{7,6},{10,9},{11,10},{14,13},{15,14},{18,17},{19... | collective-permute-start | bytes 1105928 | tf_op jit(solution)/shard_map/ppermute | solution.py:299
  716.7 19.0 %collective-permute-start.103 = (bf16[24,7680]{1,0:T(8,128)(2,1)S(1)}, bf16[24,7680]{1,0:T(8,128)(2,1)S(1)}, u32[]{:S(2)}, u32[]{:S(2)}) collective-permute-start(bf16[24,7680]{1,0:T(8,128)(2,1)S(1)} %get-tuple-element.307), channel_id=1, source_target_pairs={{0,1},{1,2},{2,3},{4,5},{5,6},{6,7},{8,9},{9,10},{10,11},{12,13},{... | collective-permute-start | bytes 1105928 | tf_op jit(solution)/shard_map/ppermute | solution.py:292
  741.2 12.4 %collective-permute-start.96 = (bf16[24,6656]{1,0:T(8,128)(2,1)S(1)}, bf16[24,6656]{1,0:T(8,128)(2,1)S(1)}, u32[]{:S(2)}, u32[]{:S(2)}) collective-permute-start(bf16[24,6656]{1,0:T(8,128)(2,1)S(1)} %fusion.67), channel_id=1, source_target_pairs={{1,0},{2,1},{3,2},{5,4},{6,5},{7,6},{9,8},{10,9},{11,10},{13,12},{... | collective-permute-start | bytes 958472 | tf_op jit(solution)/shard_map/ppermute | solution.py:299
  (217 other events, 1859.4 us)

commit v2 on v1

--- a/solution.py
+++ b/solution.py
@@ -148,26 +148,9 @@
             copy.wait()
 
 
-def along_line(block):
+def reach(values, step):
     size = lax.axis_size("narrow")
-    me = lax.axis_index("narrow")
-    rights, lefts = [], []
-    right = left = block
-    for step in range(1, size):
-        right = lax.ppermute(right, "narrow", [(z, z + 1) for z in range(step - 1, size - 1)])
-        left = lax.ppermute(left, "narrow", [(z, z - 1) for z in range(1, size - step + 1)])
-        rights.append(right)
-        lefts.append(left)
-    blocks = []
-    for spot in range(size):
-        chosen = block
-        for other in range(size):
-            if other > spot:
-                chosen = jnp.where(me == other, rights[other - spot - 1], chosen)
-            if other < spot:
-                chosen = jnp.where(me == other, lefts[spot - other - 1], chosen)
-        blocks.append(chosen)
-    return blocks
+    return lax.ppermute(values, "narrow", [(z, z ^ step) for z in range(size)])
 
 
 class Gather:
@@ -178,8 +161,16 @@
         self.middle = total // 2 // LANES * LANES
         self.packed = jnp.concatenate(arrays, axis=1) if len(arrays) > 1 else arrays[0]
 
-    def line(self):
-        blocks = along_line(self.packed)
+    def line(self, *before):
+        size = lax.axis_size("narrow")
+        me = lax.axis_index("narrow")
+        arrived = pin([reach(self.packed, step) for step in range(1, size)], *before)
+        blocks = []
+        for spot in range(size):
+            chosen = self.packed
+            for step in range(1, size):
+                chosen = jnp.where(me == spot ^ step, arrived[step - 1], chosen)
+            blocks.append(chosen)
         self.halves = [
             jnp.stack([block[:, : self.middle] for block in blocks])[None],
             jnp.stack([block[:, self.middle :] for block in blocks])[None],
@@ -194,8 +185,12 @@
             self.pieces.append([held, swap(held, order[-1])])
         return self.pieces
 
+    def core(self):
+        self.pieces = [half + [swap(piece, CORE) for piece in half] for half in self.pieces]
+        return self.pieces
+
     def finish(self):
-        pieces = [half + [swap(piece, CORE) for piece in half] for half in self.pieces]
+        pieces = self.pieces
         count = lax.axis_size("wide")
         spreads = [
             [
@@ -233,81 +228,83 @@
 class Scatter:
     def __init__(self, items):
         wide, line = lax.axis_size("wide"), lax.axis_size("narrow")
-        self.labels, self.terms, self.dims = [], [], []
+        self.terms, self.dims, self.fixed = [], [], []
         for blocks, which in items:
-            self.labels.append([("wide", bit) for bit in range(bits_of(wide))][::-1])
-            self.terms.append(
-                [blocks.reshape((2,) * bits_of(wide) + (line,) + blocks.shape[1:])]
-            )
+            labels = tuple(("wide", bit) for bit in range(bits_of(wide)))[::-1]
+            shape = (2,) * bits_of(wide) + (line,) + blocks.shape[1:]
+            self.terms.append([(blocks.reshape(shape), labels)])
             self.dims.append([CORE] + orders()[which][::-1])
+            self.fixed.append({})
+
+    def cut(self, number, fixed):
+        total = None
+        for array, labels in self.terms[number]:
+            starts = [fixed.get(label, 0) for label in labels]
+            sizes = [1 if label in fixed else 2 for label in labels]
+            starts += [0, 0, 0]
+            sizes += list(array.shape[-3:])
+            starts = [jnp.asarray(start, jnp.int32) for start in starts]
+            kept = [2 for label in labels if label not in fixed] + sizes[-3:]
+            part = lax.dynamic_slice(array, starts, sizes).reshape(kept).astype(jnp.float32)
+            total = part if total is None else total + part
+        return total
 
     def send(self):
         self.away = []
-        for labels, terms, dims in zip(self.labels, self.terms, self.dims):
-            axis, bit = labels.index(dims[0]), my_bit(dims[0])
-            self.away.append(
-                sum(
-                    lax.dynamic_index_in_dim(term, 1 - bit, axis, keepdims=False).astype(
-                        jnp.float32
-                    )
-                    for term in terms
-                ).astype(jnp.bfloat16)
-            )
+        for number, dims in enumerate(self.dims):
+            fixed = dict(self.fixed[number])
+            fixed[dims[0]] = 1 - my_bit(dims[0])
+            self.away.append(self.cut(number, fixed).astype(jnp.bfloat16))
         return self.away
 
     def receive(self):
         arrived = []
         for number, away in enumerate(self.away):
             dim = self.dims[number].pop(0)
-            axis, bit = self.labels[number].index(dim), my_bit(dim)
+            self.fixed[number][dim] = my_bit(dim)
             arrived.append(swap(away, dim))
-            self.terms[number] = [
-                lax.dynamic_index_in_dim(term, bit, axis, keepdims=False)
-                for term in self.terms[number]
-            ] + [arrived[-1]]
-            self.labels[number].remove(dim)
+            labels = self.terms[number][0][1]
+            left = tuple(label for label in labels if label not in self.fixed[number])
+            self.terms[number].append((arrived[-1], left))
         return arrived
 
     def step(self):
         self.send()
         return self.receive()
 
+    def hold(self, *others):
+        arrays = pin([[term[0] for term in terms] for terms in self.terms], *others)
+        self.terms = [
+            [(array, term[1]) for array, term in zip(held, terms)]
+            for held, terms in zip(arrays, self.terms)
+        ]
+
     def line(self):
-        sums = [sum(term.astype(jnp.float32) for term in terms) for terms in self.terms]
         size = lax.axis_size("narrow")
         me = lax.axis_index("narrow")
-        depth = min(item.shape[1] for item in sums)
-        flat, cuts = [], []
-        for item in sums:
-            parts = [item[:, k : k + depth] for k in range(0, item.shape[1], depth)]
-            flat.extend(parts)
-            cuts.append((len(parts), item.shape[2]))
-        whole = jnp.concatenate(flat, axis=2) if len(flat) > 1 else flat[0]
-        right = left = None
-        for step in range(1, size):
-            spot = jnp.clip(me + size - step, 0, size - 1)
-            goes = lax.dynamic_index_in_dim(whole, spot, 0, keepdims=False)
-            if right is not None:
-                goes = goes + right.astype(jnp.float32)
-            right = lax.ppermute(
-                goes.astype(jnp.bfloat16), "narrow", [(z, z + 1) for z in range(step)]
-            )
-            spot = jnp.clip(me - size + step, 0, size - 1)
-            goes = lax.dynamic_index_in_dim(whole, spot, 0, keepdims=False)
-            if left is not None:
-                goes = goes + left.astype(jnp.float32)
-            left = lax.ppermute(
-                goes.astype(jnp.bfloat16),
-                "narrow",
-                [(z, z - 1) for z in range(size - step, size)],
-            )
-        total = (
-            lax.dynamic_index_in_dim(whole, me, 0, keepdims=False)
-            + right.astype(jnp.float32)
-            + left.astype(jnp.float32)
-        )
+        depth = min(terms[0][0].shape[-2] for terms in self.terms)
+        sums = [self.cut(number, fixed) for number, fixed in enumerate(self.fixed)]
+        sums = lax.optimization_barrier(sums)
+
+        def columns_of(spot):
+            flat = []
+            for item in sums:
+                block = lax.dynamic_index_in_dim(item, spot, 0, keepdims=False)
+                flat.extend(block[k : k + depth] for k in range(0, block.shape[0], depth))
+            return jnp.concatenate(flat, axis=1) if len(flat) > 1 else flat[0]
+
+        self.goes = [columns_of(me ^ step).astype(jnp.bfloat16) for step in range(1, size)]
+        self.own = columns_of(me)
+        return self.goes
+
+    def finish(self, *before):
+        arrived = [reach(item, step + 1) for step, item in enumerate(self.goes)]
+        arrived = pin(arrived, *before)
+        depth = self.own.shape[0]
+        total = self.own + sum(item.astype(jnp.float32) for item in arrived)
         results, start = [], 0
-        for parts, columns in cuts:
+        for terms in self.terms:
+            parts, columns = terms[0][0].shape[-2] // depth, terms[0][0].shape[-1]
             pieces = [
                 total[:, start + k * columns : start + (k + 1) * columns] for k in range(parts)
             ]
@@ -346,23 +343,251 @@
         row += 1
 
 
-def stack_kernel(*refs):
-    sources, out_ref, rows_ref = refs[:-2], refs[-2], refs[-1]
-    rows_ref[...] = jnp.zeros_like(rows_ref)
-    row = 0
-    for ref in sources:
-        rows_ref[row : row + ref.shape[0], :] = ref[...]
-        row += ref.shape[0]
-    out_ref[...] = rows_ref[...].T
-
-
-def stack_columns(rows):
-    width = rows[0].shape[1]
+def norm_back_rows(grad, normal, inverse, gain):
+    scaled = grad * gain
+    inner = (
+        scaled
+        - jnp.mean(scaled, axis=-1, keepdims=True)
+        - normal * jnp.mean(scaled * normal, axis=-1, keepdims=True)
+    )
+    return (
+        inner * inverse,
+        jnp.sum(grad * normal, axis=0, keepdims=True),
+        jnp.sum(grad, axis=0, keepdims=True),
+    )
+
+
+SMALL_ROWS = 32
+VECTOR_AT = 4
+
+
+def feed_back_kernel(
+    grad_ref,
+    normal_two_ref,
+    inverse_two_ref,
+    gain_two_ref,
+    slope_ref,
+    out_proj_ref,
+    in_proj_ref,
+    normal_one_ref,
+    inverse_one_ref,
+    gain_one_ref,
+    attend_proj_ref,
+    outer_ref,
+    inner_ref,
+    sum_ref,
+    branch_ref,
+    context_ref,
+    rows_ref,
+):
+    @pl.when(pl.program_id(0) == 0)
+    def _():
+        rows_ref[...] = jnp.zeros_like(rows_ref)
+
+    def add_row(place, row):
+        at = VECTOR_AT + place
+        rows_ref[at : at + 1, :] = rows_ref[at : at + 1, :] + row
+
+    def column_sum(values):
+        return jnp.sum(values.astype(jnp.float32), axis=0, keepdims=True)
+
+    width = grad_ref.shape[1]
+    grad, gain_sum, shift_sum = norm_back_rows(
+        grad_ref[...], normal_two_ref[...], inverse_two_ref[...], gain_two_ref[...]
+    )
+    add_row(4, gain_sum)
+    add_row(5, shift_sum)
+    outer = grad.astype(jnp.bfloat16)
+    outer_ref[...] = outer
+    add_row(15, column_sum(outer))
+    for number, start in enumerate(range(0, slope_ref.shape[1], width)):
+        part = slice(start, start + width)
+        inner = (product(outer, out_proj_ref[:, part]) * slope_ref[:, part]).astype(jnp.bfloat16)
+        inner_ref[:, part] = inner
+        add_row(11 + number, column_sum(inner))
+        grad = grad + product_right(inner, in_proj_ref[:, part])
+    grad, gain_sum, shift_sum = norm_back_rows(
+        grad, normal_one_ref[...], inverse_one_ref[...], gain_one_ref[...]
+    )
+    add_row(2, gain_sum)
+    add_row(3, shift_sum)
+    sum_ref[...] = grad
+    branch = grad.astype(jnp.bfloat16)
+    branch_ref[...] = branch
+    add_row(10, column_sum(branch))
+    context_ref[...] = product_right(branch, attend_proj_ref[...]).astype(jnp.bfloat16)
+
+
+def feed_back(grad, saved_two, gain_two, slope, feed_out, feed_in, saved_one, gain_one, output_all):
+    rows, width = grad.shape
+    inner = slope.shape[1]
+    tile = 256 if rows % 256 == 0 else rows
+
+    def tiled(columns):
+        return pl.BlockSpec((tile, columns), lambda i: (i, 0))
+
+    def whole(array):
+        return pl.BlockSpec(array.shape, lambda i: (0, 0), pipeline_mode=pl.Buffered(1))
+
+    low = jnp.bfloat16
+    gain_two, gain_one = gain_two[None], gain_one[None]
     return pl.pallas_call(
-        stack_kernel,
-        out_shape=jax.ShapeDtypeStruct((width, LANES), jnp.float32),
-        scratch_shapes=[pltpu.VMEM((LANES, width), jnp.float32)],
-    )(*rows)
+        feed_back_kernel,
+        grid=(rows // tile,),
+        in_specs=[
+            tiled(width),
+            tiled(width),
+            tiled(1),
+            whole(gain_two),
+            tiled(inner),
+            whole(feed_out),
+            whole(feed_in),
+            tiled(width),
+            tiled(1),
+            whole(gain_one),
+            whole(output_all),
+        ],
+        out_specs=(
+            tiled(width),
+            tiled(inner),
+            tiled(width),
+            tiled(width),
+            tiled(width),
+            pl.BlockSpec((SMALL_ROWS, width), lambda i: (0, 0)),
+        ),
+        out_shape=(
+            jax.ShapeDtypeStruct((rows, width), low),
+            jax.ShapeDtypeStruct((rows, inner), low),
+            jax.ShapeDtypeStruct((rows, width), jnp.float32),
+            jax.ShapeDtypeStruct((rows, width), low),
+            jax.ShapeDtypeStruct((rows, width), low),
+            jax.ShapeDtypeStruct((SMALL_ROWS, width), jnp.float32),
+        ),
+        compiler_params=pltpu.CompilerParams(vmem_limit_bytes=56 << 20),
+        cost_estimate=pl.CostEstimate(
+            flops=2 * rows * width * (2 * inner + width),
+            bytes_accessed=rows * (6 * inner + 22 * width) + 2 * width * (2 * inner + width),
+            transcendentals=0,
+        ),
+    )(
+        grad,
+        *saved_two,
+        gain_two,
+        slope,
+        feed_out,
+        feed_in,
+        *saved_one,
+        gain_one,
+        output_all,
+    )
+
+
+def embed_back_kernel(
+    length_ref,
+    mixed_ref,
+    proj_ref,
+    sum_ref,
+    normal_ref,
+    inverse_ref,
+    gain_ref,
+    feed_rows_ref,
+    pair_rows_ref,
+    head_gain_ref,
+    head_shift_ref,
+    transform_ref,
+    pool_ref,
+    low_ref,
+    small_ref,
+    position_ref,
+    rows_ref,
+):
+    step = pl.program_id(0)
+    tokens, width = sum_ref.shape
+
+    @pl.when(step == 0)
+    def _():
+        position_ref[...] = jnp.zeros_like(position_ref)
+        rows_ref[...] = jnp.zeros_like(rows_ref)
+        rows_ref[:SMALL_ROWS, :] = feed_rows_ref[...]
+        rows_ref[2:4, :] = pair_rows_ref[...]
+        for place, ref in ((6, head_gain_ref), (7, head_shift_ref), (16, transform_ref), (17, pool_ref)):
+            rows_ref[VECTOR_AT + place : VECTOR_AT + place + 1, :] = ref[...]
+
+    def add_row(at, row):
+        rows_ref[at : at + 1, :] = rows_ref[at : at + 1, :] + row
+
+    def column_sum(values):
+        return jnp.sum(values.astype(jnp.float32), axis=0, keepdims=True)
+
+    grad = sum_ref[...]
+    for number in range(3):
+        grad = grad + product_right(
+            mixed_ref[:, number * width : (number + 1) * width],
+            proj_ref[:, number * width : (number + 1) * width],
+        )
+    grad, gain_sum, shift_sum = norm_back_rows(
+        grad, normal_ref[...], inverse_ref[...], gain_ref[...]
+    )
+    low_ref[...] = grad.astype(jnp.bfloat16)
+    position_ref[...] = position_ref[...] + grad
+    second = lax.broadcasted_iota(jnp.int32, (tokens, 1), 0) >= length_ref[step] // 2
+    late = jnp.sum(jnp.where(second, grad, 0.0), axis=0, keepdims=True)
+    early = jnp.sum(jnp.where(second, 0.0, grad), axis=0, keepdims=True)
+    add_row(0, early)
+    add_row(1, late)
+    add_row(VECTOR_AT, gain_sum)
+    add_row(VECTOR_AT + 1, shift_sum)
+    add_row(VECTOR_AT + 8, column_sum(mixed_ref[:, :width]))
+    add_row(VECTOR_AT + 9, column_sum(mixed_ref[:, 2 * width :]))
+
+    @pl.when(step == pl.num_programs(0) - 1)
+    def _():
+        small_ref[:, :tokens] = position_ref[...].T
+        small_ref[:, tokens:] = rows_ref[...].T
+
+
+def embed_back(lengths, grad_mixed, input_all, grad_sum, saved, gain, feed_rows, head_rows, tokens):
+    rows, width = grad_sum.shape
+    gain = gain[None]
+
+    def tiled(columns):
+        return pl.BlockSpec((tokens, columns), lambda i, lengths: (i, 0))
+
+    def whole(array):
+        return pl.BlockSpec(
+            array.shape, lambda i, lengths: (0, 0), pipeline_mode=pl.Buffered(1)
+        )
+
+    small = jax.ShapeDtypeStruct((width, tokens + LANES), jnp.float32)
+    return pl.pallas_call(
+        embed_back_kernel,
+        grid_spec=pltpu.PrefetchScalarGridSpec(
+            num_scalar_prefetch=1,
+            grid=(rows // tokens,),
+            in_specs=[
+                tiled(3 * width),
+                whole(input_all),
+                tiled(width),
+                tiled(width),
+                tiled(1),
+                whole(gain),
+                whole(feed_rows),
+            ]
+            + [whole(item) for item in head_rows],
+            out_specs=(tiled(width), whole(small)),
+            scratch_shapes=[
+                pltpu.VMEM((tokens, width), jnp.float32),
+                pltpu.VMEM((LANES, width), jnp.float32),
+            ],
+        ),
+        out_shape=(jax.ShapeDtypeStruct((rows, width), jnp.bfloat16), small),
+        compiler_params=pltpu.CompilerParams(vmem_limit_bytes=48 << 20),
+        cost_estimate=pl.CostEstimate(
+            flops=6 * rows * width * width,
+            bytes_accessed=rows * width * 16 + 6 * width * width,
+            transcendentals=0,
+        ),
+    )(lengths, grad_mixed, input_all, grad_sum, *saved, gain, feed_rows, *head_rows)
 
 
 def gelu_parts(values):
@@ -391,7 +616,7 @@
     context_ref[...] = jnp.concatenate(contexts, axis=1).astype(jnp.bfloat16)
 
 
-def attend_back_kernel(length_ref, query_ref, key_ref, value_ref, grad_ref, query_out, key_out, value_out):
+def attend_back_kernel(length_ref, query_ref, key_ref, value_ref, grad_ref, out_ref):
     tokens = query_ref.shape[0]
     alive = lax.broadcasted_iota(jnp.int32, (tokens, tokens), 1) < length_ref[pl.program_id(0)]
     outs = ([], [], [])
@@ -410,8 +635,11 @@
         outs[0].append(product(grad_raw, keys))
         outs[1].append(product_left(grad_raw, queries))
         outs[2].append(product_left(attention.astype(jnp.bfloat16), grad))
-    for out_ref, pair in zip((query_out, key_out, value_out), outs):
-        out_ref[...] = jnp.concatenate(pair, axis=1).astype(jnp.bfloat16)
+    for number, pair in enumerate(outs):
+        start = number * (out_ref.shape[1] // 3) + pl.program_id(1) * LANES
+        out_ref[:, pl.ds(pl.multiple_of(start, LANES), LANES)] = jnp.concatenate(
+            pair, axis=1
+        ).astype(jnp.bfloat16)
 
 
 def head_specs(tokens, pairs, count):
@@ -447,16 +675,16 @@
     width = mixed.shape[1] // 3
     pairs = width // LANES
     rows = mixed.shape[0]
-    out = jax.ShapeDtypeStruct((rows, width), jnp.bfloat16)
+    out = jax.ShapeDtypeStruct((rows, 3 * width), jnp.bfloat16)
     return pl.pallas_call(
         attend_back_kernel,
         grid_spec=pltpu.PrefetchScalarGridSpec(
             num_scalar_prefetch=1,
             grid=(rows // tokens, pairs),
             in_specs=head_specs(tokens, pairs, 3) + head_specs(tokens, pairs, 1),
-            out_specs=head_specs(tokens, pairs, 1) * 3,
+            out_specs=pl.BlockSpec((tokens, 3 * width), lambda s, h, lengths: (s, 0)),
         ),
-        out_shape=(out, out, out),
+        out_shape=out,
         compiler_params=pltpu.CompilerParams(vmem_limit_bytes=32 << 20),
         cost_estimate=pl.CostEstimate(
             flops=20 * rows * tokens * width,
@@ -516,7 +744,8 @@
         in_specs=[pl.BlockSpec(memory_space=pltpu.SMEM)]
         + [pl.BlockSpec(memory_space=pltpu.VMEM)] * 3,
     )(seq_lengths, token_ids, mlm_slots, mlm_labels)
-    shared = share_small(packed)
+    spread = jnp.broadcast_to(packed[None], (devices,) + packed.shape)
+    shared = lax.all_to_all(spread, AXES, 0, 0)
     all_ids = shared[:, :id_rows].reshape(devices * seqs, tokens)
     all_slots, all_labels = (
         shared[:, id_rows + k * seqs : id_rows + (k + 1) * seqs, :slots_each] for k in (0, 1)
@@ -544,8 +773,7 @@
         ],
         axis=1,
     ).astype(low)
-    first_group = Gather([input_master.astype(low), small_low, output_master.astype(low)])
-    first_group.line()
+    first_group = Gather(pin([input_master.astype(low), small_low], spread))
 
     lane_rows = -(-vocab_rows // LANES)
 
@@ -592,23 +820,38 @@
         return own, mine
 
     own_first, mine_first = picks(0)
-    word_group = Gather([product(own_first, table_low).astype(low)])
-    word_line = word_group.line()
-    first_group.plane()
-    late = pin(
-        [
-            feed_master[0].astype(low),
-            feed_master[1].astype(low),
-            dense_master[0].astype(low),
-            dense_master[1].astype(low),
-        ],
-        word_line,
-    )
-    second_group = Gather(late)
-    second_group.line()
-    word_group.plane()
-    input_all, small_all, output_all = first_group.finish()
+    own_rows = product(own_first, table_low).astype(low)
+    word_group = Gather([own_rows])
+    first_group.line(own_rows)
+    first_plane = first_group.plane()
+    word_group.line()
+    word_plane = word_group.plane()
+    second_group = Gather(
+        pin(
+            [output_master.astype(low), feed_master[0].astype(low)],
+            [half[0] for half in word_plane],
+            first_plane,
+        )
+    )
+    first_core = first_group.core()
+    second_group.line(word_plane, first_core)
+    word_group.pieces = pin(word_plane, first_core, all_counted, all_labels)
+    input_all, small_all = first_group.finish()
+    word_core = word_group.core()
     (word_rows,) = word_group.finish()
+    second_plane = second_group.plane()
+    third_group = Gather(
+        pin(
+            [
+                feed_master[1].astype(low),
+                dense_master[0].astype(low),
+                dense_master[1].astype(low),
+            ],
+            word_plane,
+            first_core,
+        )
+    )
+    third_group.line([half[0] for half in second_plane])
     words = product_left(mine_first, word_rows)
 
     def fetch_more(state):
@@ -635,9 +878,14 @@
     normed_low = normed.astype(low)
     bias_mixed = jnp.concatenate([parts[8], jnp.zeros((width,), jnp.float32), parts[9]])
     mixed = (product(normed_low, input_all) + bias_mixed).astype(low)
-    second_group.pieces = pin(second_group.plane(), mixed)
+    third_group.plane()
     context_low = attend(lengths, mixed, tokens)
-    feed_in, feed_out, dense_one, dense_two = second_group.finish()
+    second_group.pieces = pin(second_group.pieces, mixed)
+    second_group.core()
+    output_all, feed_in = second_group.finish()
+    third_group.pieces = pin(third_group.pieces, context_low)
+    third_group.core()
+    feed_out, dense_one, dense_two = third_group.finish()
     branch = product(context_low, output_all) + parts[10]
     hidden_one, saved_one = norm_forward(normed + branch, parts[2], parts[3])
     one_low = hidden_one.astype(low)
@@ -669,6 +917,7 @@
     pair_local = jnp.sum(pair_total[:, 0] - jnp.sum(jnp.where(pair_hit, pair_logits, 0.0), axis=1))
 
     vocab_bias = lax.dynamic_slice_in_dim(parts[15], me * vocab_rows, vocab_rows, 0)
+    head_group.core()
     (heads,) = head_group.finish()
     logits = product_right(heads, table_low) + vocab_bias
     top = jnp.max(logits, axis=-1)
@@ -677,25 +926,30 @@
     highest = jnp.max(all_totals, axis=0)
     log_totals = (highest + jnp.log(jnp.sum(jnp.exp(all_totals - highest), axis=0))).reshape(-1)
     vocab_index = me * vocab_rows + jnp.arange(vocab_rows, dtype=jnp.int32)
-    masked_shared = jnp.sum(all_counted * log_totals)
     hit = vocab_index[None, :] == all_labels[:, None]
     target_local = jnp.sum(all_counted[:, None] * jnp.where(hit, logits, 0.0))
     grad_logits = (
         (jnp.exp(logits - log_totals[:, None]) - hit.astype(jnp.float32))
         * (all_counted * inv_count)[:, None]
     ).astype(low)
-    grad_heads = product(grad_logits, table_low).reshape(devices, picked, width)
     middle = width // 2
-    head_sum = Scatter([(grad_heads[:, :, :middle], 0), (grad_heads[:, :, middle:], 1)])
+    head_sum = Scatter(
+        [
+            (product(grad_logits, side).reshape(devices, picked, middle), number)
+            for number, side in enumerate((table_low[:, :middle], table_low[:, middle:]))
+        ]
+    )
     sent = head_sum.send()
     grad_table = product_left(pin(grad_logits, sent), heads)
+    masked_shared = jnp.sum(all_counted * pin(log_totals, sent))
     head_sum.receive()
     for _ in range(1, bits_of(lax.axis_size("wide"))):
         head_sum.step()
     grad_vocab = jnp.sum(grad_logits.astype(jnp.float32), axis=0)
     vocab_pad = -(-vocab_rows // (8 * LANES)) * 8 * LANES
     all_vocab = share_small(jnp.pad(grad_vocab, (0, vocab_pad - vocab_rows)).reshape(-1, LANES))
-    grad_head = jnp.concatenate(head_sum.line(), axis=1)
+    head_sum.line()
+    grad_head = jnp.concatenate(head_sum.finish(grad_table, all_vocab), axis=1)
 
     def owners(values):
         return values.reshape(devices, -1, values.shape[1])
@@ -716,10 +970,10 @@
     grad_two = exact(
         slot_hot.astype(jnp.float32), product_right(grad_transform, dense_one)
     ) + exact(first_hot.astype(jnp.float32), product_right(grad_pool_pre, dense_two))
-    grad_sum_two, grad_feed_gain, grad_feed_shift = norm_backward(grad_two, saved_two, parts[4])
-    grad_outer = grad_sum_two.astype(low)
+    grad_outer, grad_inner, grad_sum_one, grad_branch, grad_context, feed_rows = feed_back(
+        grad_two, saved_two, parts[4], slope, feed_out, feed_in, saved_one, parts[2], output_all
+    )
     grad_feed_out = product_left(grad_outer, active_low)
-    grad_inner = (product(grad_outer, feed_out) * slope).astype(low)
     grad_feed_in = product_left(one_low, grad_inner)
     feed_sum = Scatter(
         [
@@ -729,73 +983,74 @@
             (owners(grad_pooler), 1),
         ]
     )
-    sent = feed_sum.send()
-    grad_one = grad_sum_two + product_right(pin(grad_inner, sent), feed_in)
-    grad_sum_one, grad_attend_gain, grad_attend_shift = norm_backward(grad_one, saved_one, parts[2])
-    grad_branch = grad_sum_one.astype(low)
-    grad_context = product_right(grad_branch, output_all).astype(low)
+    feed_sum.send()
     came = feed_sum.receive()
     sent = feed_sum.send()
     grad_context = pin(grad_context, came, sent)
-    grad_q, grad_k, grad_v = attend_back(lengths, mixed, grad_context, tokens)
-    grad_mixed = jnp.concatenate([grad_q, grad_k, grad_v], axis=1)
+    grad_mixed = attend_back(lengths, mixed, grad_context, tokens)
     came = feed_sum.receive()
     sent = feed_sum.send()
     grad_mixed = pin(grad_mixed, came, sent)
-    grad_normed = grad_sum_one + product_right(grad_mixed, input_all)
-    grad_embedded, grad_embed_gain, grad_embed_shift = norm_backward(
-        grad_normed, saved_zero, parts[0]
-    )
-    embedded_low = grad_embedded.astype(low)
-    grad_words = product(mine_first, embedded_low).reshape(devices, ahead, width)
-    grad_input = product_left(normed_low, grad_mixed)
-    grad_output = product_left(context_low, grad_branch)
+    in_sum = Scatter(
+        [
+            (owners(product_left(normed_low, grad_mixed[:, : 2 * width])), 0),
+            (owners(product_left(normed_low, grad_mixed[:, 2 * width :])), 1),
+            (owners(product_left(context_low, pin(grad_branch, grad_mixed))), 1),
+        ]
+    )
+    sent = in_sum.send()
+    feed_came = [feed_sum.receive()]
     while feed_sum.dims[0]:
-        feed_sum.receive()
-        if feed_sum.dims[0]:
-            feed_sum.send()
-    in_second = second[:, None]
-    rows = [
-        jnp.sum(jnp.where(in_second, 0.0, grad_embedded), axis=0, keepdims=True),
-        jnp.sum(jnp.where(in_second, grad_embedded, 0.0), axis=0, keepdims=True),
-        grad_classifier.T,
+        feed_came.append(feed_sum.step())
+    in_came = in_sum.receive()
+    embedded_low, grad_small = embed_back(
+        lengths,
+        pin(grad_mixed, sent),
+        input_all,
+        grad_sum_one,
+        saved_zero,
+        parts[0],
+        feed_rows,
+        (
+            grad_classifier.T,
+            grad_head_gain[None],
+            grad_head_shift[None],
+            column_sum(grad_transform),
+            column_sum(grad_pool_pre),
+        ),
+        tokens,
+    )
+    embedded_low, grad_small = pin((embedded_low, grad_small), feed_came, in_came)
+    in_away = in_sum.send()
+    embedded_low, grad_small = pin((embedded_low, grad_small), in_away)
+    word_sums = [
+        (product(mine_first, side).reshape(devices, ahead, middle), number)
+        for number, side in enumerate((embedded_low[:, :middle], embedded_low[:, middle:]))
     ]
-    vector_rows = [
-        grad_embed_gain[None],
-        grad_embed_shift[None],
-        grad_attend_gain[None],
-        grad_attend_shift[None],
-        grad_feed_gain[None],
-        grad_feed_shift[None],
-        grad_head_gain[None],
-        grad_head_shift[None],
-        column_sum(grad_q),
-        column_sum(grad_v),
-        column_sum(grad_branch),
-        column_sum(grad_inner).reshape(-1, width),
-        column_sum(grad_outer),
-        column_sum(grad_transform),
-        column_sum(grad_pool_pre),
-    ]
-    vector_count = sum(item.shape[0] for item in vector_rows)
-    grad_position = jnp.sum(grad_embedded.reshape(seqs, tokens, width), axis=0).T
-    grad_small = jnp.concatenate([grad_position, stack_columns(rows + vector_rows)], axis=1)
-    last_sum = Scatter(
-        [
-            (owners(grad_input), 0),
-            (owners(grad_output), 1),
-            (owners(grad_small), 1),
-            (grad_words[:, :, :middle], 0),
-            (grad_words[:, :, middle:], 1),
-        ]
-    )
-    for _ in range(bits_of(lax.axis_size("wide"))):
+    vector_count = (vector_each * devices - devices * vocab_rows) // width
+    last_sum = Scatter(word_sums + [(owners(grad_small), 1)])
+    last_away = last_sum.send()
+    in_came = in_sum.receive()
+    feed_sum.hold(last_away)
+    feed_away = feed_sum.line()
+    in_sum.hold(feed_away)
+    in_away = in_sum.send()
+    last_sum.receive()
+    last_sum.hold(in_away)
+    last_away = last_sum.send()
+    in_sum.receive()
+    while in_sum.dims[0]:
+        in_sum.step()
+    in_sum.hold(last_away)
+    in_away = in_sum.line()
+    last_sum.receive()
+    while last_sum.dims[0]:
         last_sum.step()
-    sum_feed_in, sum_dense, sum_feed_out, sum_pooler = feed_sum.line()
-    sum_input, sum_output, sum_small, words_left, words_right = last_sum.line()
-    grad_table = grad_table + exact(
-        own_first.T.astype(jnp.float32), jnp.concatenate([words_left, words_right], axis=1)
-    )
+    sent = last_sum.line()
+    sum_feed_in, sum_dense, sum_feed_out, sum_pooler = feed_sum.finish(sent)
+    sum_mixed, sum_value, sum_output = in_sum.finish(sent)
+    words_left, words_right, sum_small = last_sum.finish()
+    sum_input = jnp.concatenate([sum_mixed, sum_value], axis=1)
 
     def return_more(state):
         turn, grad_table = state
@@ -809,9 +1064,19 @@
         lambda state: state[0] < rounds, return_more, (jnp.int32(1), grad_table)
     )
 
+    def halves(values):
+        high = values.astype(low)
+        return high, (values - high.astype(jnp.float32)).astype(low)
+
+    table_high, table_rest = halves(grad_table)
+    chosen = product(own_first, table_high) + product(own_first, table_rest)
+    table_square = jnp.sum(grad_table * grad_table)
+    present = jnp.sum(own_first.astype(jnp.float32), axis=1, keepdims=True)
+    words_own = jnp.concatenate([words_left, words_right], axis=1)
+    table_square = table_square + jnp.sum(present * words_own * (words_own + 2.0 * chosen))
+
     sum_vector = sum_small[:, tokens + 4 : tokens + 4 + vector_count]
     pieces = [
-        grad_table,
         sum_small[:, :tokens],
         jnp.moveaxis(sum_small[:, tokens : tokens + 4].reshape(depth, 2, 2), 1, 0),
         sum_input,
@@ -819,28 +1084,33 @@
         jnp.stack([sum_dense, sum_pooler]),
         jnp.stack([sum_feed_in, sum_feed_out]),
     ]
-    squares = sum((jnp.sum(item * item) for item in pieces + [sum_vector, grad_vocab]))
-    payload = jnp.concatenate(
-        [
-            jnp.stack([squares, target_local, pair_local]),
-            jnp.zeros((LANES - 3,), jnp.float32),
-            sum_vector.reshape(-1),
-        ]
-    )
-    payload_pad = -(-payload.shape[0] // LANES) * LANES
-    answers = share_small(
-        jnp.pad(payload, (0, payload_pad - payload.shape[0])).reshape(-1, LANES)
-    )
-    totals = jnp.sum(answers[:, 0, :3], axis=0)
+    vector_flat = depth * vector_count
+    vector_pad = -(-vector_flat // LANES) * LANES
+    all_vector = share_small(
+        jnp.pad(sum_vector.reshape(-1), (0, vector_pad - vector_flat)).reshape(-1, LANES)
+    )
+    squares = table_square + sum(
+        (jnp.sum(item * item) for item in pieces + [sum_vector, grad_vocab])
+    )
+    scalars = jnp.stack([squares, target_local, pair_local])
+    totals = jnp.sum(share_small(jnp.pad(scalars, (0, LANES - 3))[None])[:, 0, :3], axis=0)
+    grad_table = grad_table + product_left(
+        jnp.concatenate([own_first, own_first], axis=0),
+        jnp.concatenate(halves(words_own), axis=0),
+    )
     grad_vector = jnp.concatenate(
         [
-            answers.reshape(devices, -1)[:, LANES : LANES + depth * vector_count]
+            all_vector.reshape(devices, -1)[:, :vector_flat]
             .reshape(devices * depth, vector_count)
             .T.reshape(-1),
             all_vocab.reshape(devices, -1)[:, :vocab_rows].reshape(-1),
         ]
     )
-    pieces.append(lax.dynamic_slice_in_dim(grad_vector, me * vector_each, vector_each, 0))
+    pieces = (
+        [grad_table]
+        + pieces
+        + [lax.dynamic_slice_in_dim(grad_vector, me * vector_each, vector_each, 0)]
+    )
     norm = jnp.sqrt(totals[0])
     masked_total = masked_shared - totals[1]
     pair_total_sum = totals[2]

time: 838 us -> 703 us (0.84)
  waiting for transfers between devices: 227 us -> 139 us
  local copies, waits for them, and re-layouts: 103 us -> 66.8 us
  Pallas kernels: 58.7 us -> 82.2 us
  matrix products: 120 us -> 98.4 us
  starting transfers between devices: 145 us -> 133 us
    ppermute x42 -> x27, waiting for transfers between devices: 74.5 us -> 28.8 us  [reach(): return lax.ppermute(values, 'narrow', [(z, z ^ step) for z in range(size)])]
    ppermute x65 -> x76, waiting for transfers between devices: 133 us -> 100 us  [swap(): lax.ppermute(values, dim[0], [(i, i ^ 1 << dim[1]) for i in range(size)])]
    ppermute x42 -> x27, starting transfers between devices: 78.8 us -> 51.4 us  [reach(): return lax.ppermute(values, 'narrow', [(z, z ^ step) for z in range(size)])]
    pallas_call x1 -> x2, Pallas kernels: 1.78 us -> 29.2 us  [the longest x1 19.5 us: feed_back(): pl.pallas_call(feed_back_kernel, grid=(rows // tile,), in_specs=[tiled(wi...]
    dot_general x10 -> x13, matrix products: 46.3 us -> 31.6 us  [product(): return jnp.dot(left, right, preferred_element_type=jnp.float32)]
    dot_general x9 -> x6, matrix products: 33.9 us -> 20.6 us  [product_right(): lax.dot_general(left, right, (((1,), (1,)), ((), ())), preferred_element_...]
    slice x3 -> x0, local copies, waits for them, and re-layouts: 10.8 us -> none  [the longest x1 7.27 us: shards(): grad_heads[:, :, middle:]]
    all_to_all x4, waiting for transfers between devices: 19.4 us -> 9.79 us  [share_small(): return lax.all_to_all(spread, AXES, 0, 0)]
  transfers between devices with their start and end apart: 111 -> 108, of which waited for: 40 -> 29; matrix products, arithmetic and copies ran while one was open for 31% -> 31% of each run, Pallas kernels for 6% -> 8%
where the time goes in v2:
time: 703 us; the launch traced here: 692 us
  other arithmetic  143 us (20%)
  waiting for transfers between devices  139 us (20%)
  starting transfers between devices  133 us (19%)
  matrix products  98.4 us (14%)
  Pallas kernels  82.2 us (12%)
  local copies, waits for them, and re-layouts  66.8 us (10%)
  between operations  28.9 us (4%)
    ppermute x76, waiting for transfers between devices, swap(): lax.ppermute(values, dim[0], [(i, i ^ 1 << dim[1]) for i in range(size)])  100 us
    ppermute x76, starting transfers between devices, swap(): lax.ppermute(values, dim[0], [(i, i ^ 1 << dim[1]) for i in range(size)])  56.9 us
    ppermute x27, starting transfers between devices, reach(): return lax.ppermute(values, 'narrow', [(z, z ^ step) for z in range(size)])  51.4 us
    dot_general x13, matrix products, product_left(): lax.dot_general(left, right, (((0,), (0,)), ((), ())), preferred_element_...  41.3 us
    convert_element_type x24, other arithmetic, send(): self.away.append(self.cut(number, fixed).astype(jnp.bfloat16))  35.3 us
    dot_general x13, matrix products, product(): return jnp.dot(left, right, preferred_element_type=jnp.float32)  31.6 us
    ppermute x27, waiting for transfers between devices, reach(): return lax.ppermute(values, 'narrow', [(z, z ^ step) for z in range(size)])  28.8 us
    pallas_call x1, Pallas kernels, attend_back(): pl.pallas_call(attend_back_kernel, grid_spec=pltpu.PrefetchScalarGridSpec...  22.7 us
  transfers between devices with their start and end apart: 108, of which 29 were waited for; matrix products, arithmetic and copies ran while one was open for 31% of the time, Pallas kernels for 8%

profile of v2, /device:TPU:0, one launch (start us, length us, event | category | flops | bytes accessed | tf_op | source)
XLA Modules:
  0.0 691.8 jit_solution(12976297867409462769)
XLA Ops:
  11.3 7.3 %all-to-all-start = ((s32[32,16,128]{2,1,0:T(8,128)}), s32[32,16,128]{2,1,0:T(8,128)S(1)}, u32[]{:S(2)}, u32[]{:S(2)}) async-start(s32[32,16,128]{2,1,0:T(8,128)} %broadcast_in_dim.126), calls=%async_computation.1 | async-start | bytes 524288 | tf_op jit(solution)/shard_map/all_to_all | solution.py:748
  24.0 2.4 collective-permute-start.8
  35.6 4.9 convert_reduce_fusion.3
  43.1 3.3 collective-permute-start.1
  64.7 12.8 %collective-permute-done.3 = bf16[1,4,96,384]{3,2,1,0:T(8,128)(2,1)S(1)} collective-permute-done((bf16[1,4,96,384]{3,2,1,0:T(8,128)(2,1)S(1)}, bf16[1,4,96,384]{3,2,1,0:T(8,128)(2,1)S(1)}, u32[]{:S(2)}, u32[]{:S(2)}) %collective-permute-start.3) | collective-permute-done | bytes 294944 | tf_op jit(solution)/shard_map/ppermute | solution.py:102
  80.3 5.1 collective-permute-start.22
  85.4 2.4 collective-permute-start.24
  96.8 4.4 collective-permute-start.33
  102.3 2.4 collective-permute-start.35
  130.5 5.6 fusion.24
  136.8 2.3 fusion.39
  142.2 11.9 %collective-permute-done.36 = bf16[1,4,24,2304]{3,2,1,0:T(8,128)(2,1)} collective-permute-done((bf16[1,4,24,2304]{3,2,1,0:T(8,128)(2,1)}, bf16[1,4,24,2304]{3,2,1,0:T(8,128)(2,1)}, u32[]{:S(2)}, u32[]{:S(2)}) %collective-permute-start.36) | collective-permute-done | bytes 442400 | tf_op jit(solution)/shard_map/ppermute | solution.py:102
  159.6 3.1 add_convert_fusion.query_ref.key_ref.value_ref
  163.4 12.5 %collective-permute-done.37.refs_1_ = bf16[2,4,24,2304]{3,2,1,0:T(8,128)(2,1)S(1)} collective-permute-done((bf16[2,4,24,2304]{3,2,1,0:T(8,128)(2,1)S(1)}, bf16[2,4,24,2304]{3,2,1,0:T(8,128)(2,1)S(1)}, u32[]{:S(2)}, u32[]{:S(2)}) %collective-permute-start.37) | collective-permute-done | bytes 884768 | tf_op jit(solution)/shard_map/ppermute | solution.py:102
  180.6 15.1 %shard_map.487 = bf16[768,768]{1,0:T(8,128)(2,1)S(1)} custom-call(s32[2]{0:T(128)S(1)} %bitcast.904, bf16[768,2304]{1,0:T(8,128)(2,1)S(1)} %add_convert_fusion.query_ref.key_ref.value_ref, bf16[768,2304]{1,0:T(8,128)(2,1)S(1)} %add_convert_fusion.query_ref.key_ref.value_ref, bf16[768,2304]{1,0:T(8,128)(2,1)S(1)} %add_convert_fusion.query_ref.key_ref.value_ref), custom_call_target="tpu_custom_call" | custom-call | flops 1811939328 | bytes 4718592 | tf_op jit(solution)/shard_map/pallas_call | solution.py:656
  197.0 3.2 shard_map.488
  202.7 10.0 %fusion.21 = (f32[768,3072]{1,0:T(8,128)}, bf16[768,3072]{1,0:T(8,128)(2,1)}) fusion(f32[3072]{0:T(1024)S(1)} %slice.745, bf16[768,3072]{1,0:T(8,128)(2,1)S(1)} %bitcast.848, f32[768,768]{1,0:T(8,128)S(1)} %subtract_multiply_fusion.1.normal_one_ref, f32[768]{0:T(1024)S(1)} %copy-done.98, f32[768]{0:T(1024)S(1)} %get-tuple-element.593), kind=kOutput, calls=%fused_computation.39 | convolution fusion | flops 3651600384 | bytes 21252096 | tf_op jit(solution)/shard_map/dot_general | solution.py:30
  212.7 4.3 shard_map.489
  217.0 7.9 %fusion.219 = (f32[768]{0:T(1024)S(1)}, f32[768,768]{1,0:T(8,128)S(1)}) fusion(f32[768]{0:T(1024)S(1)} %copy-done.168, bf16[768,3072]{1,0:T(8,128)(2,1)} %get-tuple-element.267, bf16[768,3072]{1,0:T(8,128)(2,1)S(1)} %bitcast.850, f32[768]{0:T(1024)S(1)} %copy-done.98, f32[768,768]{1,0:T(8,128)S(1)} %subtract_multiply_fusion.1.normal_one_ref, ...), kind=kOutput, calls=%fused_computation.687 | convolution fusion | flops 3626827008 | bytes 14168064 | tf_op jit(solution)/shard_map/dot_general | solution.py:34
  230.4 2.3 collective-permute-start.46
  232.7 4.8 collective-permute-done.44
  237.5 6.4 collective-permute-done.45
  246.5 7.0 %collective-permute-done.47 = bf16[1,4,112,384]{3,2,1,0:T(8,128)(2,1)S(1)} collective-permute-done((bf16[1,4,112,384]{3,2,1,0:T(8,128)(2,1)S(1)}, bf16[1,4,112,384]{3,2,1,0:T(8,128)(2,1)S(1)}, u32[]{:S(2)}, u32[]{:S(2)}) %collective-permute-start.47) | collective-permute-done | bytes 344096 | tf_op jit(solution)/shard_map/ppermute | solution.py:102
  257.9 12.4 %collective-permute-done.48.refs_1_ = bf16[2,4,112,384]{3,2,1,0:T(8,128)(2,1)} collective-permute-done((bf16[2,4,112,384]{3,2,1,0:T(8,128)(2,1)}, bf16[2,4,112,384]{3,2,1,0:T(8,128)(2,1)}, u32[]{:S(2)}, u32[]{:S(2)}) %collective-permute-start.48) | collective-permute-done | bytes 688160 | tf_op jit(solution)/shard_map/ppermute | solution.py:102
  276.2 3.0 shard_map.490
  279.2 5.5 add_reduce_fusion
  284.8 5.5 fusion.16
  291.2 7.2 %all-to-all-start.1 = ((f32[32,28,128]{2,1,0:T(8,128)}), f32[32,28,128]{2,1,0:T(8,128)}, u32[]{:S(2)}, u32[]{:S(2)}) async-start(f32[32,28,128]{2,1,0:T(8,128)} %broadcast_in_dim.229), calls=%async_computation.2 | async-start | bytes 1048576 | tf_op jit(solution)/shard_map/all_to_all | solution.py:319
  307.4 5.3 all-to-all-done.1
  316.3 8.7 %convert_reduce_fusion = (f32[956]{0:T(1024)S(1)}, bf16[3584,956]{0,1:T(8,128)(2,1)S(1)}) fusion(f32[3584]{0:T(1024)} %broadcast_multiply_fusion, s32[3584]{0:T(1024)} %eq.107, s32[956]{0:T(1024)} %iota_add_fusion, f32[3584]{0:T(1024)S(1)} %add_bitcast_fusion, f32[3584,956]{0,1:T(8,128)} %copy-done.29, f32[956]{0:T(1024)} %copy-done.135), kind=kLoop, calls=%fused_computation.31 | loop fusion | flops 30835780 | bytes 20612304 | tf_op jit(solution)/shard_map/reduce_sum | solution.py:948
  325.0 4.0 fusion.67
  330.5 4.0 fusion.65
  341.4 12.3 %collective-permute-done.56 = bf16[2,4,112,384]{3,2,1,0:T(8,128)(2,1)S(1)} collective-permute-done((bf16[2,4,112,384]{3,2,1,0:T(8,128)(2,1)S(1)}, bf16[2,4,112,384]{3,2,1,0:T(8,128)(2,1)S(1)}, u32[]{:S(2)}, u32[]{:S(2)}) %collective-permute-start.56) | collective-permute-done | bytes 688160 | tf_op jit(solution)/shard_map/ppermute | solution.py:102
  356.3 7.5 %fusion.221 = f32[956,768]{1,0:T(8,128)} fusion(bf16[3584,956]{0,1:T(8,128)(2,1)S(1)} %get-tuple-element.284, bf16[3584,768]{1,0:T(8,128)(2,1)S(1)} %bitcast.833), kind=kOutput, calls=%fused_computation.689 | convolution fusion | flops 5262802944 | bytes 15294464 | tf_op jit(solution)/shard_map/dot_general | solution.py:40
  366.1 3.5 all-to-all-start.2
  371.2 3.4 collective-permute-done.60
  378.7 2.4 collective-permute-start.62
  385.0 7.7 %collective-permute-done.62 = bf16[112,768]{1,0:T(8,128)(2,1)} collective-permute-done((bf16[112,768]{1,0:T(8,128)(2,1)}, bf16[112,768]{1,0:T(8,128)(2,1)}, u32[]{:S(2)}, u32[]{:S(2)}) %collective-permute-start.62) | collective-permute-done | bytes 172064 | tf_op jit(solution)/shard_map/ppermute | solution.py:153
  399.1 2.5 convolution_add_fusion.1.grad_ref
  401.6 19.5 %shard_map.491 = (bf16[768,768]{1,0:T(8,128)(2,1)}, bf16[768,3072]{1,0:T(8,128)(2,1)}, f32[768,768]{1,0:T(8,128)}, bf16[768,768]{1,0:T(8,128)(2,1)}, bf16[768,768]{1,0:T(8,128)(2,1)}, /*index=5*/f32[32,768]{1,0:T(8,128)}) custom-call(f32[768,768]{1,0:T(8,128)} %convolution_add_fusion.1.grad_ref, f32[768,768]{1,0:T(8,128)} %copy-done.33, ...), custom_call_target="tpu_custom_call" | custom-call | flops 8153726976 | bytes 37748736 | tf_op jit(solution)/shard_map/pallas_call | solution.py:434
  421.1 5.8 fusion.109
  429.1 7.7 %fusion.225 = f32[768,3072]{1,0:T(8,128)S(1)} fusion(bf16[768,768]{1,0:T(8,128)(2,1)S(1)} %copy-done.63, bf16[768,3072]{1,0:T(8,128)(2,1)} %get-tuple-element.267), kind=kOutput, calls=%fused_computation.693 | convolution fusion | flops 3623878656 | bytes 15335424 | tf_op jit(solution)/shard_map/dot_general | solution.py:40
  436.8 3.6 copy-done.31
  453.0 2.2 fusion.33
  456.8 2.3 fusion.32
  465.2 22.7 %shard_map.492.mixed_ref = bf16[768,2304]{1,0:T(8,128)(2,1)S(1)} custom-call(s32[2]{0:T(128)S(1)} %bitcast.905, bf16[768,2304]{1,0:T(8,128)(2,1)S(1)} %add_convert_fusion.query_ref.key_ref.value_ref, bf16[768,2304]{1,0:T(8,128)(2,1)S(1)} %add_convert_fusion.query_ref.key_ref.value_ref, bf16[768,2304]{1,0:T(8,128)(2,1)S(1)} %add_convert_fusion.query_ref.key_ref.value_ref, ...), custom_call_target="tpu_custom_call" | custom-call | flops 4529848320 | bytes 8257536 | tf_op jit(solution)/shard_map/pallas_call | solution.py:679
  487.9 4.0 fusion.54
  491.9 2.8 fusion.53
  512.1 9.6 %shard_map.493 = (bf16[768,768]{1,0:T(8,128)(2,1)S(1)}, f32[768,512]{1,0:T(8,128)S(1)}) custom-call(s32[2]{0:T(128)S(1)} %bitcast.906, bf16[768,2304]{1,0:T(8,128)(2,1)} %copy-done.8, bf16[768,2304]{1,0:T(8,128)(2,1)} %bitcast.839, f32[768,768]{1,0:T(8,128)S(1)} %copy-done.11, f32[768,768]{1,0:T(8,128)} %get-tuple-element.484.normal_ref, ...), custom_call_target="tpu_custom_call" | custom-call | flops 2717908992 | bytes 12976128 | tf_op jit(solution)/shard_map/pallas_call | solution.py:562
  529.5 2.6 fusion.52
  532.1 2.6 fusion.23
  534.7 2.6 fusion.22
  542.5 3.0 fusion.51
  554.8 2.4 collective-permute-start.100
  570.0 2.6 collective-permute-done.96
  578.5 11.5 %collective-permute-done.89 = bf16[2,4,24,512]{3,2,1,0:T(8,128)(2,1)S(1)} collective-permute-done((bf16[2,4,24,512]{3,2,1,0:T(8,128)(2,1)S(1)}, bf16[2,4,24,512]{3,2,1,0:T(8,128)(2,1)S(1)}, u32[]{:S(2)}, u32[]{:S(2)}) %collective-permute-start.89) | collective-permute-done | bytes 196640 | tf_op jit(solution)/shard_map/ppermute | solution.py:102
  598.8 2.3 collective-permute-done.86
  609.3 7.5 %collective-permute-start.92 = (bf16[24,3584]{1,0:T(8,128)(2,1)S(1)}, bf16[24,3584]{1,0:T(8,128)(2,1)S(1)}, u32[]{:S(2)}, u32[]{:S(2)}) collective-permute-start(bf16[24,3584]{1,0:T(8,128)(2,1)S(1)} %get-tuple-element.575), channel_id=1, source_target_pairs={{0,2},{1,3},{2,0},{3,1},{4,6},{5,7},{6,4},{7,5},{8,10},{9,11},{10,... | collective-permute-start | bytes 516104 | tf_op jit(solution)/shard_map/ppermute | solution.py:153
  617.3 3.7 collective-permute-start.93
  623.8 7.5 %collective-permute-done.92 = bf16[24,3584]{1,0:T(8,128)(2,1)S(1)} collective-permute-done((bf16[24,3584]{1,0:T(8,128)(2,1)S(1)}, bf16[24,3584]{1,0:T(8,128)(2,1)S(1)}, u32[]{:S(2)}, u32[]{:S(2)}) %collective-permute-start.92) | collective-permute-done | bytes 172064 | tf_op jit(solution)/shard_map/ppermute | solution.py:153
  644.7 3.7 all-to-all-start.3
  651.1 4.5 all-to-all-done.3
  656.8 3.3 all-to-all-start.4
  671.5 6.9 multiply_subtract_fusion
  (900 shorter events, 279.8 us)
Async XLA Ops:
  11.3 21.6 %all-to-all-start = ((s32[32,16,128]{2,1,0:T(8,128)}), s32[32,16,128]{2,1,0:T(8,128)S(1)}, u32[]{:S(2)}, u32[]{:S(2)}) async-start(s32[32,16,128]{2,1,0:T(8,128)} %broadcast_in_dim.126), calls=%async_computation.1 | async-start | bytes 524288 | tf_op jit(solution)/shard_map/all_to_all | solution.py:748
  22.2 27.2 %collective-permute-start.7 = (bf16[24,2816]{1,0:T(8,128)(2,1)S(1)}, bf16[24,2816]{1,0:T(8,128)(2,1)S(1)}, u32[]{:S(2)}, u32[]{:S(2)}) collective-permute-start(bf16[24,2816]{1,0:T(8,128)(2,1)S(1)} %constant_dynamic-update-slice_fusion), channel_id=1, source_target_pairs={{0,1},{1,0},{2,3},{3,2},{4,5},{5,4},{6,7},{7,6},{8,9},{9,8},{10,11... | collective-permute-start | bytes 405512 | tf_op jit(solution)/shard_map/ppermute | solution.py:153
  24.0 25.6 %collective-permute-start.8 = (bf16[24,2816]{1,0:T(8,128)(2,1)S(1)}, bf16[24,2816]{1,0:T(8,128)(2,1)S(1)}, u32[]{:S(2)}, u32[]{:S(2)}) collective-permute-start(bf16[24,2816]{1,0:T(8,128)(2,1)S(1)} %constant_dynamic-update-slice_fusion), channel_id=1, source_target_pairs={{0,2},{1,3},{2,0},{3,1},{4,6},{5,7},{6,4},{7,5},{8,10},{9,11},{10,... | collective-permute-start | bytes 405512 | tf_op jit(solution)/shard_map/ppermute | solution.py:153
  26.4 23.2 %collective-permute-start.9 = (bf16[24,2816]{1,0:T(8,128)(2,1)S(1)}, bf16[24,2816]{1,0:T(8,128)(2,1)}, u32[]{:S(2)}, u32[]{:S(2)}) collective-permute-start(bf16[24,2816]{1,0:T(8,128)(2,1)S(1)} %constant_dynamic-update-slice_fusion), channel_id=1, source_target_pairs={{0,3},{1,2},{2,1},{3,0},{4,7},{5,6},{6,5},{7,4},{8,11},{9,10},{10,... | collective-permute-start | bytes 405512 | tf_op jit(solution)/shard_map/ppermute | solution.py:153
  57.8 20.9 %collective-permute-start.11 = (bf16[2,4,24,1408]{3,2,1,0:T(8,128)(2,1)S(1)}, bf16[2,4,24,1408]{3,2,1,0:T(8,128)(2,1)S(1)}, u32[]{:S(2)}, u32[]{:S(2)}) collective-permute-start(bf16[2,4,24,1408]{3,2,1,0:T(8,128)(2,1)S(1)} %pad_maximum_fusion.9.refs_0_), channel_id=1, source_target_pairs={{0,16},{4,20},{8,24},{12,28},{16,0},{20,4},{24,8},{28,12},{1,17},{... | collective-permute-start | bytes 1622024 | tf_op jit(solution)/shard_map/ppermute | solution.py:102
  60.4 18.6 %collective-permute-start.15 = (bf16[2,4,24,1408]{3,2,1,0:T(8,128)(2,1)S(1)}, bf16[2,4,24,1408]{3,2,1,0:T(8,128)(2,1)S(1)}, u32[]{:S(2)}, u32[]{:S(2)}) collective-permute-start(bf16[2,4,24,1408]{3,2,1,0:T(8,128)(2,1)S(1)} %pad_maximum_fusion.10.refs_4_), channel_id=1, source_target_pairs={{0,8},{4,12},{8,0},{12,4},{16,24},{20,28},{24,16},{28,20},{1,9},{5... | collective-permute-start | bytes 1622024 | tf_op jit(solution)/shard_map/ppermute | solution.py:102
  61.2 16.3 %collective-permute-start.3 = (bf16[1,4,96,384]{3,2,1,0:T(8,128)(2,1)S(1)}, bf16[1,4,96,384]{3,2,1,0:T(8,128)(2,1)S(1)}, u32[]{:S(2)}, u32[]{:S(2)}) collective-permute-start(bf16[1,4,96,384]{3,2,1,0:T(8,128)(2,1)S(1)} %maximum_bitcast_fusion.6), channel_id=1, source_target_pairs={{0,8},{4,12},{8,0},{12,4},{16,24},{20,28},{24,16},{28,20},{1,9},{5... | collective-permute-start | bytes 884744 | tf_op jit(solution)/shard_map/ppermute | solution.py:102
  62.6 14.9 %collective-permute-start.5 = (bf16[1,4,96,384]{3,2,1,0:T(8,128)(2,1)S(1)}, bf16[1,4,96,384]{3,2,1,0:T(8,128)(2,1)S(1)}, u32[]{:S(2)}, u32[]{:S(2)}) collective-permute-start(bf16[1,4,96,384]{3,2,1,0:T(8,128)(2,1)S(1)} %maximum_bitcast_fusion.7), channel_id=1, source_target_pairs={{0,16},{4,20},{8,24},{12,28},{16,0},{20,4},{24,8},{28,12},{1,17},{... | collective-permute-start | bytes 884744 | tf_op jit(solution)/shard_map/ppermute | solution.py:102
  64.1 15.3 %collective-permute-start.12 = (bf16[2,4,24,1408]{3,2,1,0:T(8,128)(2,1)S(1)}, bf16[2,4,24,1408]{3,2,1,0:T(8,128)(2,1)S(1)}, u32[]{:S(2)}, u32[]{:S(2)}) collective-permute-start(bf16[2,4,24,1408]{3,2,1,0:T(8,128)(2,1)S(1)} %pad_maximum_fusion.9.refs_0_), channel_id=1, source_target_pairs={{0,4},{4,0},{8,12},{12,8},{16,20},{20,16},{24,28},{28,24},{1,5},{5... | collective-permute-start | bytes 1622024 | tf_op jit(solution)/shard_map/ppermute | solution.py:102
  77.5 15.8 %collective-permute-start.4 = (bf16[2,4,96,384]{3,2,1,0:T(8,128)(2,1)S(1)}, bf16[2,4,96,384]{3,2,1,0:T(8,128)(2,1)S(1)}, u32[]{:S(2)}, u32[]{:S(2)}) collective-permute-start(bf16[2,4,96,384]{3,2,1,0:T(8,128)(2,1)S(1)} %pad_maximum_fusion.6.refs_0_), channel_id=1, source_target_pairs={{0,16},{4,20},{8,24},{12,28},{16,0},{20,4},{24,8},{28,12},{1,17},{... | collective-permute-start | bytes 1769480 | tf_op jit(solution)/shard_map/ppermute | solution.py:102
  79.4 15.5 %collective-permute-start.6 = (bf16[2,4,96,384]{3,2,1,0:T(8,128)(2,1)S(1)}, bf16[2,4,96,384]{3,2,1,0:T(8,128)(2,1)S(1)}, u32[]{:S(2)}, u32[]{:S(2)}) collective-permute-start(bf16[2,4,96,384]{3,2,1,0:T(8,128)(2,1)S(1)} %pad_maximum_fusion.7.refs_4_), channel_id=1, source_target_pairs={{0,8},{4,12},{8,0},{12,4},{16,24},{20,28},{24,16},{28,20},{1,9},{5... | collective-permute-start | bytes 1769480 | tf_op jit(solution)/shard_map/ppermute | solution.py:102
  80.3 21.9 %collective-permute-start.22 = (bf16[24,3840]{1,0:T(8,128)(2,1)S(1)}, bf16[24,3840]{1,0:T(8,128)(2,1)S(1)}, u32[]{:S(2)}, u32[]{:S(2)}) collective-permute-start(bf16[24,3840]{1,0:T(8,128)(2,1)S(1)} %constant_dynamic-update-slice_fusion.2), channel_id=1, source_target_pairs={{0,1},{1,0},{2,3},{3,2},{4,5},{5,4},{6,7},{7,6},{8,9},{9,8},{10,11... | collective-permute-start | bytes 552968 | tf_op jit(solution)/shard_map/ppermute | solution.py:153
  85.4 19.3 %collective-permute-start.23 = (bf16[24,3840]{1,0:T(8,128)(2,1)S(1)}, bf16[24,3840]{1,0:T(8,128)(2,1)}, u32[]{:S(2)}, u32[]{:S(2)}) collective-permute-start(bf16[24,3840]{1,0:T(8,128)(2,1)S(1)} %constant_dynamic-update-slice_fusion.2), channel_id=1, source_target_pairs={{0,2},{1,3},{2,0},{3,1},{4,6},{5,7},{6,4},{7,5},{8,10},{9,11},{10,... | collective-permute-start | bytes 552968 | tf_op jit(solution)/shard_map/ppermute | solution.py:153
  85.4 19.3 %collective-permute-start.24 = (bf16[24,3840]{1,0:T(8,128)(2,1)S(1)}, bf16[24,3840]{1,0:T(8,128)(2,1)}, u32[]{:S(2)}, u32[]{:S(2)}) collective-permute-start(bf16[24,3840]{1,0:T(8,128)(2,1)S(1)} %constant_dynamic-update-slice_fusion.2), channel_id=1, source_target_pairs={{0,3},{1,2},{2,1},{3,0},{4,7},{5,6},{6,5},{7,4},{8,11},{9,10},{10,... | collective-permute-start | bytes 552968 | tf_op jit(solution)/shard_map/ppermute | solution.py:153
  96.8 24.2 %collective-permute-start.33 = (bf16[24,4608]{1,0:T(8,128)(2,1)}, bf16[24,4608]{1,0:T(8,128)(2,1)}, u32[]{:S(2)}, u32[]{:S(2)}) collective-permute-start(bf16[24,4608]{1,0:T(8,128)(2,1)} %constant_dynamic-update-slice_fusion.4), channel_id=1, source_target_pairs={{0,1},{1,0},{2,3},{3,2},{4,5},{5,4},{6,7},{7,6},{8,9},{9,8},{10,11... | collective-permute-start | bytes 663560 | tf_op jit(solution)/shard_map/ppermute | solution.py:153
  101.2 19.8 %collective-permute-start.34 = (bf16[24,4608]{1,0:T(8,128)(2,1)}, bf16[24,4608]{1,0:T(8,128)(2,1)}, u32[]{:S(2)}, u32[]{:S(2)}) collective-permute-start(bf16[24,4608]{1,0:T(8,128)(2,1)} %constant_dynamic-update-slice_fusion.4), channel_id=1, source_target_pairs={{0,2},{1,3},{2,0},{3,1},{4,6},{5,7},{6,4},{7,5},{8,10},{9,11},{10,... | collective-permute-start | bytes 663560 | tf_op jit(solution)/shard_map/ppermute | solution.py:153
  102.3 19.2 %collective-permute-start.35 = (bf16[24,4608]{1,0:T(8,128)(2,1)}, bf16[24,4608]{1,0:T(8,128)(2,1)}, u32[]{:S(2)}, u32[]{:S(2)}) collective-permute-start(bf16[24,4608]{1,0:T(8,128)(2,1)} %constant_dynamic-update-slice_fusion.4), channel_id=1, source_target_pairs={{0,3},{1,2},{2,1},{3,0},{4,7},{5,6},{6,5},{7,4},{8,11},{9,10},{10,... | collective-permute-start | bytes 663560 | tf_op jit(solution)/shard_map/ppermute | solution.py:153
  121.5 41.2 %collective-permute-start.26 = (bf16[2,4,24,1920]{3,2,1,0:T(8,128)(2,1)}, bf16[2,4,24,1920]{3,2,1,0:T(8,128)(2,1)}, u32[]{:S(2)}, u32[]{:S(2)}) collective-permute-start(bf16[2,4,24,1920]{3,2,1,0:T(8,128)(2,1)} %pad_maximum_fusion.2.refs_0_), channel_id=1, source_target_pairs={{0,16},{4,20},{8,24},{12,28},{16,0},{20,4},{24,8},{28,12},{1,17},{... | collective-permute-start | bytes 2211848 | tf_op jit(solution)/shard_map/ppermute | solution.py:102
  126.1 36.6 %collective-permute-start.28 = (bf16[2,4,24,1920]{3,2,1,0:T(8,128)(2,1)}, bf16[2,4,24,1920]{3,2,1,0:T(8,128)(2,1)}, u32[]{:S(2)}, u32[]{:S(2)}) collective-permute-start(bf16[2,4,24,1920]{3,2,1,0:T(8,128)(2,1)} %pad_maximum_fusion.3.refs_4_), channel_id=1, source_target_pairs={{0,8},{4,12},{8,0},{12,4},{16,24},{20,28},{24,16},{28,20},{1,9},{5... | collective-permute-start | bytes 2211848 | tf_op jit(solution)/shard_map/ppermute | solution.py:102
  127.6 26.5 %collective-permute-start.36 = (bf16[1,4,24,2304]{3,2,1,0:T(8,128)(2,1)}, bf16[1,4,24,2304]{3,2,1,0:T(8,128)(2,1)}, u32[]{:S(2)}, u32[]{:S(2)}) collective-permute-start(bf16[1,4,24,2304]{3,2,1,0:T(8,128)(2,1)} %maximum_bitcast_fusion), channel_id=1, source_target_pairs={{0,8},{4,12},{8,0},{12,4},{16,24},{20,28},{24,16},{28,20},{1,9},{5... | collective-permute-start | bytes 1327112 | tf_op jit(solution)/shard_map/ppermute | solution.py:102
  128.1 27.8 %collective-permute-start.38 = (bf16[1,4,24,2304]{3,2,1,0:T(8,128)(2,1)}, bf16[1,4,24,2304]{3,2,1,0:T(8,128)(2,1)}, u32[]{:S(2)}, u32[]{:S(2)}) collective-permute-start(bf16[1,4,24,2304]{3,2,1,0:T(8,128)(2,1)} %maximum_bitcast_fusion.1), channel_id=1, source_target_pairs={{0,16},{4,20},{8,24},{12,28},{16,0},{20,4},{24,8},{28,12},{1,17},{... | collective-permute-start | bytes 1327112 | tf_op jit(solution)/shard_map/ppermute | solution.py:102
  155.3 20.5 %collective-permute-start.37 = (bf16[2,4,24,2304]{3,2,1,0:T(8,128)(2,1)S(1)}, bf16[2,4,24,2304]{3,2,1,0:T(8,128)(2,1)S(1)}, u32[]{:S(2)}, u32[]{:S(2)}) collective-permute-start(bf16[2,4,24,2304]{3,2,1,0:T(8,128)(2,1)S(1)} %pad_maximum_fusion.refs_0_), channel_id=1, source_target_pairs={{0,16},{4,20},{8,24},{12,28},{16,0},{20,4},{24,8},{28,12},{1,17},{... | collective-permute-start | bytes 2654216 | tf_op jit(solution)/shard_map/ppermute | solution.py:102
  158.1 37.7 %collective-permute-start.39 = (bf16[2,4,24,2304]{3,2,1,0:T(8,128)(2,1)}, bf16[2,4,24,2304]{3,2,1,0:T(8,128)(2,1)}, u32[]{:S(2)}, u32[]{:S(2)}) collective-permute-start(bf16[2,4,24,2304]{3,2,1,0:T(8,128)(2,1)} %pad_maximum_fusion.1.refs_4_), channel_id=1, source_target_pairs={{0,8},{4,12},{8,0},{12,4},{16,24},{20,28},{24,16},{28,20},{1,9},{5... | collective-permute-start | bytes 2654216 | tf_op jit(solution)/shard_map/ppermute | solution.py:102
  162.7 33.6 %collective-permute-start.29 = (bf16[2,4,24,1920]{3,2,1,0:T(8,128)(2,1)}, bf16[2,4,24,1920]{3,2,1,0:T(8,128)(2,1)}, u32[]{:S(2)}, u32[]{:S(2)}) collective-permute-start(bf16[2,4,24,1920]{3,2,1,0:T(8,128)(2,1)} %pad_maximum_fusion.2.refs_0_), channel_id=1, source_target_pairs={{0,4},{4,0},{8,12},{12,8},{16,20},{20,16},{24,28},{28,24},{1,5},{5... | collective-permute-start | bytes 2211848 | tf_op jit(solution)/shard_map/ppermute | solution.py:102
  162.8 33.6 %collective-permute-start.30 = (bf16[2,4,24,1920]{3,2,1,0:T(8,128)(2,1)}, bf16[2,4,24,1920]{3,2,1,0:T(8,128)(2,1)}, u32[]{:S(2)}, u32[]{:S(2)}) collective-permute-start(bf16[2,4,24,1920]{3,2,1,0:T(8,128)(2,1)} %collective-permute-done.26.refs_1_), channel_id=1, source_target_pairs={{0,4},{4,0},{8,12},{12,8},{16,20},{20,16},{24,28},{28,24},{1,5},{5... | collective-permute-start | bytes 2211848 | tf_op jit(solution)/shard_map/ppermute | solution.py:102
  163.3 33.5 %collective-permute-start.31 = (bf16[2,4,24,1920]{3,2,1,0:T(8,128)(2,1)}, bf16[2,4,24,1920]{3,2,1,0:T(8,128)(2,1)}, u32[]{:S(2)}, u32[]{:S(2)}) collective-permute-start(bf16[2,4,24,1920]{3,2,1,0:T(8,128)(2,1)} %pad_maximum_fusion.3.refs_4_), channel_id=1, source_target_pairs={{0,4},{4,0},{8,12},{12,8},{16,20},{20,16},{24,28},{28,24},{1,5},{5... | collective-permute-start | bytes 2211848 | tf_op jit(solution)/shard_map/ppermute | solution.py:102
  176.8 20.2 %collective-permute-start.32 = (bf16[2,4,24,1920]{3,2,1,0:T(8,128)(2,1)}, bf16[2,4,24,1920]{3,2,1,0:T(8,128)(2,1)}, u32[]{:S(2)}, u32[]{:S(2)}) collective-permute-start(bf16[2,4,24,1920]{3,2,1,0:T(8,128)(2,1)} %collective-permute-done.28.refs_5_), channel_id=1, source_target_pairs={{0,4},{4,0},{8,12},{12,8},{16,20},{20,16},{24,28},{28,24},{1,5},{5... | collective-permute-start | bytes 2211848 | tf_op jit(solution)/shard_map/ppermute | solution.py:102
  195.8 16.9 %collective-permute-start.40 = (bf16[2,4,24,2304]{3,2,1,0:T(8,128)(2,1)S(1)}, bf16[2,4,24,2304]{3,2,1,0:T(8,128)(2,1)S(1)}, u32[]{:S(2)}, u32[]{:S(2)}) collective-permute-start(bf16[2,4,24,2304]{3,2,1,0:T(8,128)(2,1)S(1)} %copy-done.10), channel_id=1, source_target_pairs={{0,4},{4,0},{8,12},{12,8},{16,20},{20,16},{24,28},{28,24},{1,5},{5... | collective-permute-start | bytes 2654216 | tf_op jit(solution)/shard_map/ppermute | solution.py:102
  196.4 16.3 %collective-permute-start.41 = (bf16[2,4,24,2304]{3,2,1,0:T(8,128)(2,1)S(1)}, bf16[2,4,24,2304]{3,2,1,0:T(8,128)(2,1)S(1)}, u32[]{:S(2)}, u32[]{:S(2)}) collective-permute-start(bf16[2,4,24,2304]{3,2,1,0:T(8,128)(2,1)S(1)} %copy-done.16), channel_id=1, source_target_pairs={{0,4},{4,0},{8,12},{12,8},{16,20},{20,16},{24,28},{28,24},{1,5},{5... | collective-permute-start | bytes 2654216 | tf_op jit(solution)/shard_map/ppermute | solution.py:102
  196.5 16.2 %collective-permute-start.42 = (bf16[2,4,24,2304]{3,2,1,0:T(8,128)(2,1)}, bf16[2,4,24,2304]{3,2,1,0:T(8,128)(2,1)S(1)}, u32[]{:S(2)}, u32[]{:S(2)}) collective-permute-start(bf16[2,4,24,2304]{3,2,1,0:T(8,128)(2,1)} %pad_maximum_fusion.1.refs_4_), channel_id=1, source_target_pairs={{0,4},{4,0},{8,12},{12,8},{16,20},{20,16},{24,28},{28,24},{1,5},{5... | collective-permute-start | bytes 2654216 | tf_op jit(solution)/shard_map/ppermute | solution.py:102
  196.9 15.8 %collective-permute-start.43 = (bf16[2,4,24,2304]{3,2,1,0:T(8,128)(2,1)}, bf16[2,4,24,2304]{3,2,1,0:T(8,128)(2,1)S(1)}, u32[]{:S(2)}, u32[]{:S(2)}) collective-permute-start(bf16[2,4,24,2304]{3,2,1,0:T(8,128)(2,1)} %collective-permute-done.39.refs_5_), channel_id=1, source_target_pairs={{0,4},{4,0},{8,12},{12,8},{16,20},{20,16},{24,28},{28,24},{1,5},{5... | collective-permute-start | bytes 2654216 | tf_op jit(solution)/shard_map/ppermute | solution.py:102
  228.3 15.6 %collective-permute-start.45 = (bf16[112,768]{1,0:T(8,128)(2,1)S(1)}, bf16[112,768]{1,0:T(8,128)(2,1)S(1)}, u32[]{:S(2)}, u32[]{:S(2)}) collective-permute-start(bf16[112,768]{1,0:T(8,128)(2,1)S(1)} %add_convert_fusion.2), channel_id=1, source_target_pairs={{0,2},{1,3},{2,0},{3,1},{4,6},{5,7},{6,4},{7,5},{8,10},{9,11},{10,... | collective-permute-start | bytes 516104 | tf_op jit(solution)/shard_map/ppermute | solution.py:153
  254.5 15.9 %collective-permute-start.48 = (bf16[2,4,112,384]{3,2,1,0:T(8,128)(2,1)}, bf16[2,4,112,384]{3,2,1,0:T(8,128)(2,1)}, u32[]{:S(2)}, u32[]{:S(2)}) collective-permute-start(bf16[2,4,112,384]{3,2,1,0:T(8,128)(2,1)} %pad_maximum_fusion.4.refs_0_), channel_id=1, source_target_pairs={{0,16},{4,20},{8,24},{12,28},{16,0},{20,4},{24,8},{28,12},{1,17},{... | collective-permute-start | bytes 2064392 | tf_op jit(solution)/shard_map/ppermute | solution.py:102
  255.9 15.6 %collective-permute-start.52 = (bf16[2,4,112,384]{3,2,1,0:T(8,128)(2,1)}, bf16[2,4,112,384]{3,2,1,0:T(8,128)(2,1)}, u32[]{:S(2)}, u32[]{:S(2)}) collective-permute-start(bf16[2,4,112,384]{3,2,1,0:T(8,128)(2,1)} %pad_maximum_fusion.5.refs_4_), channel_id=1, source_target_pairs={{0,8},{4,12},{8,0},{12,4},{16,24},{20,28},{24,16},{28,20},{1,9},{5... | collective-permute-start | bytes 2064392 | tf_op jit(solution)/shard_map/ppermute | solution.py:102
  257.4 18.7 %collective-permute-start.49 = (bf16[2,4,112,384]{3,2,1,0:T(8,128)(2,1)}, bf16[2,4,112,384]{3,2,1,0:T(8,128)(2,1)}, u32[]{:S(2)}, u32[]{:S(2)}) collective-permute-start(bf16[2,4,112,384]{3,2,1,0:T(8,128)(2,1)} %pad_maximum_fusion.4.refs_0_), channel_id=1, source_target_pairs={{0,4},{4,0},{8,12},{12,8},{16,20},{20,16},{24,28},{28,24},{1,5},{5... | collective-permute-start | bytes 2064392 | tf_op jit(solution)/shard_map/ppermute | solution.py:102
  257.4 18.7 %collective-permute-start.53 = (bf16[2,4,112,384]{3,2,1,0:T(8,128)(2,1)}, bf16[2,4,112,384]{3,2,1,0:T(8,128)(2,1)}, u32[]{:S(2)}, u32[]{:S(2)}) collective-permute-start(bf16[2,4,112,384]{3,2,1,0:T(8,128)(2,1)} %pad_maximum_fusion.5.refs_4_), channel_id=1, source_target_pairs={{0,4},{4,0},{8,12},{12,8},{16,20},{20,16},{24,28},{28,24},{1,5},{5... | collective-permute-start | bytes 2064392 | tf_op jit(solution)/shard_map/ppermute | solution.py:102
  291.2 21.5 %all-to-all-start.1 = ((f32[32,28,128]{2,1,0:T(8,128)}), f32[32,28,128]{2,1,0:T(8,128)}, u32[]{:S(2)}, u32[]{:S(2)}) async-start(f32[32,28,128]{2,1,0:T(8,128)} %broadcast_in_dim.229), calls=%async_computation.2 | async-start | bytes 1048576 | tf_op jit(solution)/shard_map/all_to_all | solution.py:319
  336.3 17.4 %collective-permute-start.56 = (bf16[2,4,112,384]{3,2,1,0:T(8,128)(2,1)S(1)}, bf16[2,4,112,384]{3,2,1,0:T(8,128)(2,1)S(1)}, u32[]{:S(2)}, u32[]{:S(2)}) collective-permute-start(bf16[2,4,112,384]{3,2,1,0:T(8,128)(2,1)S(1)} %fusion.44), channel_id=1, source_target_pairs={{0,16},{4,20},{8,24},{12,28},{16,0},{20,4},{24,8},{28,12},{1,17},{... | collective-permute-start | bytes 2064392 | tf_op jit(solution)/shard_map/ppermute | solution.py:102
  340.8 23.0 %collective-permute-start.59 = (bf16[2,4,112,384]{3,2,1,0:T(8,128)(2,1)S(1)}, bf16[2,4,112,384]{3,2,1,0:T(8,128)(2,1)S(1)}, u32[]{:S(2)}, u32[]{:S(2)}) collective-permute-start(bf16[2,4,112,384]{3,2,1,0:T(8,128)(2,1)S(1)} %fusion.43), channel_id=1, source_target_pairs={{0,8},{4,12},{8,0},{12,4},{16,24},{20,28},{24,16},{28,20},{1,9},{5... | collective-permute-start | bytes 2064392 | tf_op jit(solution)/shard_map/ppermute | solution.py:102
  366.1 17.8 %all-to-all-start.2 = ((f32[32,8,128]{2,1,0:T(8,128)}), f32[32,8,128]{2,1,0:T(8,128)}, u32[]{:S(2)}, u32[]{:S(2)}) async-start(f32[32,8,128]{2,1,0:T(8,128)} %broadcast_in_dim.231), calls=%async_computation.3 | async-start | bytes 262144 | tf_op jit(solution)/shard_map/all_to_all | solution.py:319
  428.7 24.3 %collective-permute-start.64 = (bf16[2,2,4,24,3072]{4,3,2,1,0:T(8,128)(2,1)}, bf16[2,2,4,24,3072]{4,3,2,1,0:T(8,128)(2,1)}, u32[]{:S(2)}, u32[]{:S(2)}) collective-permute-start(bf16[2,2,4,24,3072]{4,3,2,1,0:T(8,128)(2,1)} %fusion.30), channel_id=1, source_target_pairs={{0,4},{4,0},{8,12},{12,8},{16,20},{20,16},{24,28},{28,24},{1,5},{5... | collective-permute-start | bytes 7077896 | tf_op jit(solution)/shard_map/ppermute | solution.py:102
  455.3 32.6 %collective-permute-start.68 = (bf16[2,4,24,3072]{3,2,1,0:T(8,128)(2,1)S(1)}, bf16[2,4,24,3072]{3,2,1,0:T(8,128)(2,1)S(1)}, u32[]{:S(2)}, u32[]{:S(2)}) collective-permute-start(bf16[2,4,24,3072]{3,2,1,0:T(8,128)(2,1)S(1)} %fusion.33), channel_id=1, source_target_pairs={{0,16},{4,20},{8,24},{12,28},{16,0},{20,4},{24,8},{28,12},{1,17},{... | collective-permute-start | bytes 3538952 | tf_op jit(solution)/shard_map/ppermute | solution.py:102
  459.0 32.8 %collective-permute-start.70 = (bf16[2,4,24,3072]{3,2,1,0:T(8,128)(2,1)S(1)}, bf16[2,4,24,3072]{3,2,1,0:T(8,128)(2,1)S(1)}, u32[]{:S(2)}, u32[]{:S(2)}) collective-permute-start(bf16[2,4,24,3072]{3,2,1,0:T(8,128)(2,1)S(1)} %fusion.32), channel_id=1, source_target_pairs={{0,8},{4,12},{8,0},{12,4},{16,24},{20,28},{24,16},{28,20},{1,9},{5... | collective-permute-start | bytes 3538952 | tf_op jit(solution)/shard_map/ppermute | solution.py:102
  502.5 27.0 %collective-permute-start.76 = (bf16[2,2,4,24,1536]{4,3,2,1,0:T(8,128)(2,1)}, bf16[2,2,4,24,1536]{4,3,2,1,0:T(8,128)(2,1)}, u32[]{:S(2)}, u32[]{:S(2)}) collective-permute-start(bf16[2,2,4,24,1536]{4,3,2,1,0:T(8,128)(2,1)} %fusion.45), channel_id=1, source_target_pairs={{0,4},{4,0},{8,12},{12,8},{16,20},{20,16},{24,28},{28,24},{1,5},{5... | collective-permute-start | bytes 3538952 | tf_op jit(solution)/shard_map/ppermute | solution.py:102
  503.5 18.3 %collective-permute-start.77 = (bf16[2,2,4,24,768]{4,3,2,1,0:T(8,128)(2,1)}, bf16[2,2,4,24,768]{4,3,2,1,0:T(8,128)(2,1)}, u32[]{:S(2)}, u32[]{:S(2)}) collective-permute-start(bf16[2,2,4,24,768]{4,3,2,1,0:T(8,128)(2,1)} %fusion.80), channel_id=1, source_target_pairs={{0,4},{4,0},{8,12},{12,8},{16,20},{20,16},{24,28},{28,24},{1,5},{5... | collective-permute-start | bytes 1769480 | tf_op jit(solution)/shard_map/ppermute | solution.py:102
  504.8 18.4 %collective-permute-start.78 = (bf16[2,2,4,24,768]{4,3,2,1,0:T(8,128)(2,1)}, bf16[2,2,4,24,768]{4,3,2,1,0:T(8,128)(2,1)}, u32[]{:S(2)}, u32[]{:S(2)}) collective-permute-start(bf16[2,2,4,24,768]{4,3,2,1,0:T(8,128)(2,1)} %fusion.81), channel_id=1, source_target_pairs={{0,4},{4,0},{8,12},{12,8},{16,20},{20,16},{24,28},{28,24},{1,5},{5... | collective-permute-start | bytes 1769480 | tf_op jit(solution)/shard_map/ppermute | solution.py:102
  505.6 23.9 %collective-permute-start.72 = (bf16[4,24,3072]{2,1,0:T(8,128)(2,1)}, bf16[4,24,3072]{2,1,0:T(8,128)(2,1)}, u32[]{:S(2)}, u32[]{:S(2)}) collective-permute-start(bf16[4,24,3072]{2,1,0:T(8,128)(2,1)} %fusion.54), channel_id=1, source_target_pairs={{0,8},{4,12},{8,0},{12,4},{16,24},{20,28},{24,16},{28,20},{1,9},{5... | collective-permute-start | bytes 1769480 | tf_op jit(solution)/shard_map/ppermute | solution.py:102
  507.5 22.0 %collective-permute-start.74 = (bf16[4,24,3072]{2,1,0:T(8,128)(2,1)}, bf16[4,24,3072]{2,1,0:T(8,128)(2,1)S(1)}, u32[]{:S(2)}, u32[]{:S(2)}) collective-permute-start(bf16[4,24,3072]{2,1,0:T(8,128)(2,1)} %fusion.53), channel_id=1, source_target_pairs={{0,16},{4,20},{8,24},{12,28},{16,0},{20,4},{24,8},{28,12},{1,17},{... | collective-permute-start | bytes 1769480 | tf_op jit(solution)/shard_map/ppermute | solution.py:102
  527.5 27.1 %collective-permute-start.83 = (bf16[2,4,24,768]{3,2,1,0:T(8,128)(2,1)}, bf16[2,4,24,768]{3,2,1,0:T(8,128)(2,1)}, u32[]{:S(2)}, u32[]{:S(2)}) collective-permute-start(bf16[2,4,24,768]{3,2,1,0:T(8,128)(2,1)} %fusion.89), channel_id=1, source_target_pairs={{0,8},{4,12},{8,0},{12,4},{16,24},{20,28},{24,16},{28,20},{1,9},{5... | collective-permute-start | bytes 884744 | tf_op jit(solution)/shard_map/ppermute | solution.py:102
  529.1 25.7 %collective-permute-start.84 = (bf16[2,4,24,768]{3,2,1,0:T(8,128)(2,1)}, bf16[2,4,24,768]{3,2,1,0:T(8,128)(2,1)}, u32[]{:S(2)}, u32[]{:S(2)}) collective-permute-start(bf16[2,4,24,768]{3,2,1,0:T(8,128)(2,1)} %fusion.88), channel_id=1, source_target_pairs={{0,8},{4,12},{8,0},{12,4},{16,24},{20,28},{24,16},{28,20},{1,9},{5... | collective-permute-start | bytes 884744 | tf_op jit(solution)/shard_map/ppermute | solution.py:102
  537.4 19.8 %collective-permute-start.82 = (bf16[2,4,24,1536]{3,2,1,0:T(8,128)(2,1)}, bf16[2,4,24,1536]{3,2,1,0:T(8,128)(2,1)}, u32[]{:S(2)}, u32[]{:S(2)}) collective-permute-start(bf16[2,4,24,1536]{3,2,1,0:T(8,128)(2,1)} %fusion.52), channel_id=1, source_target_pairs={{0,16},{4,20},{8,24},{12,28},{16,0},{20,4},{24,8},{28,12},{1,17},{... | collective-permute-start | bytes 1769480 | tf_op jit(solution)/shard_map/ppermute | solution.py:102
  540.0 22.7 %collective-permute-start.79 = (bf16[2,2,4,96,384]{4,3,2,1,0:T(8,128)(2,1)}, bf16[2,2,4,96,384]{4,3,2,1,0:T(8,128)(2,1)}, u32[]{:S(2)}, u32[]{:S(2)}) collective-permute-start(bf16[2,2,4,96,384]{4,3,2,1,0:T(8,128)(2,1)} %fusion.46), channel_id=1, source_target_pairs={{0,4},{4,0},{8,12},{12,8},{16,20},{20,16},{24,28},{28,24},{1,5},{5... | collective-permute-start | bytes 3538952 | tf_op jit(solution)/shard_map/ppermute | solution.py:102
  541.2 22.0 %collective-permute-start.80 = (bf16[2,2,4,96,384]{4,3,2,1,0:T(8,128)(2,1)}, bf16[2,2,4,96,384]{4,3,2,1,0:T(8,128)(2,1)}, u32[]{:S(2)}, u32[]{:S(2)}) collective-permute-start(bf16[2,2,4,96,384]{4,3,2,1,0:T(8,128)(2,1)} %fusion.47), channel_id=1, source_target_pairs={{0,4},{4,0},{8,12},{12,8},{16,20},{20,16},{24,28},{28,24},{1,5},{5... | collective-permute-start | bytes 3538952 | tf_op jit(solution)/shard_map/ppermute | solution.py:102
  554.8 52.3 %collective-permute-start.100 = (bf16[24,7680]{1,0:T(8,128)(2,1)S(1)}, bf16[24,7680]{1,0:T(8,128)(2,1)S(1)}, u32[]{:S(2)}, u32[]{:S(2)}) collective-permute-start(bf16[24,7680]{1,0:T(8,128)(2,1)S(1)} %pad_maximum_fusion.11), channel_id=1, source_target_pairs={{0,1},{1,0},{2,3},{3,2},{4,5},{5,4},{6,7},{7,6},{8,9},{9,8},{10,11... | collective-permute-start | bytes 1105928 | tf_op jit(solution)/shard_map/ppermute | solution.py:153
  557.2 51.5 %collective-permute-start.101 = (bf16[24,7680]{1,0:T(8,128)(2,1)S(1)}, bf16[24,7680]{1,0:T(8,128)(2,1)S(1)}, u32[]{:S(2)}, u32[]{:S(2)}) collective-permute-start(bf16[24,7680]{1,0:T(8,128)(2,1)S(1)} %pad_maximum_fusion.12), channel_id=1, source_target_pairs={{0,2},{1,3},{2,0},{3,1},{4,6},{5,7},{6,4},{7,5},{8,10},{9,11},{10,... | collective-permute-start | bytes 1105928 | tf_op jit(solution)/shard_map/ppermute | solution.py:153
  569.5 22.1 %collective-permute-start.85 = (bf16[2,4,96,384]{3,2,1,0:T(8,128)(2,1)S(1)}, bf16[2,4,96,384]{3,2,1,0:T(8,128)(2,1)S(1)}, u32[]{:S(2)}, u32[]{:S(2)}) collective-permute-start(bf16[2,4,96,384]{3,2,1,0:T(8,128)(2,1)S(1)} %fusion.49), channel_id=1, source_target_pairs={{0,16},{4,20},{8,24},{12,28},{16,0},{20,4},{24,8},{28,12},{1,17},{... | collective-permute-start | bytes 1769480 | tf_op jit(solution)/shard_map/ppermute | solution.py:102
  572.6 21.7 %collective-permute-start.87 = (bf16[2,4,96,384]{3,2,1,0:T(8,128)(2,1)S(1)}, bf16[2,4,96,384]{3,2,1,0:T(8,128)(2,1)S(1)}, u32[]{:S(2)}, u32[]{:S(2)}) collective-permute-start(bf16[2,4,96,384]{3,2,1,0:T(8,128)(2,1)S(1)} %fusion.48), channel_id=1, source_target_pairs={{0,8},{4,12},{8,0},{12,4},{16,24},{20,28},{24,16},{28,20},{1,9},{5... | collective-permute-start | bytes 1769480 | tf_op jit(solution)/shard_map/ppermute | solution.py:102
  573.2 16.9 %collective-permute-start.89 = (bf16[2,4,24,512]{3,2,1,0:T(8,128)(2,1)S(1)}, bf16[2,4,24,512]{3,2,1,0:T(8,128)(2,1)S(1)}, u32[]{:S(2)}, u32[]{:S(2)}) collective-permute-start(bf16[2,4,24,512]{3,2,1,0:T(8,128)(2,1)S(1)} %fusion.98), channel_id=1, source_target_pairs={{0,8},{4,12},{8,0},{12,4},{16,24},{20,28},{24,16},{28,20},{1,9},{5... | collective-permute-start | bytes 589832 | tf_op jit(solution)/shard_map/ppermute | solution.py:102
  590.1 19.2 %collective-permute-start.102 = (bf16[24,7680]{1,0:T(8,128)(2,1)S(1)}, bf16[24,7680]{1,0:T(8,128)(2,1)S(1)}, u32[]{:S(2)}, u32[]{:S(2)}) collective-permute-start(bf16[24,7680]{1,0:T(8,128)(2,1)S(1)} %pad_maximum_fusion.13), channel_id=1, source_target_pairs={{0,3},{1,2},{2,1},{3,0},{4,7},{5,6},{6,5},{7,4},{8,11},{9,10},{10,... | collective-permute-start | bytes 1105928 | tf_op jit(solution)/shard_map/ppermute | solution.py:153
  601.1 16.2 %collective-permute-start.97 = (bf16[24,3072]{1,0:T(8,128)(2,1)S(1)}, bf16[24,3072]{1,0:T(8,128)(2,1)S(1)}, u32[]{:S(2)}, u32[]{:S(2)}) collective-permute-start(bf16[24,3072]{1,0:T(8,128)(2,1)S(1)} %pad_maximum_fusion.17), channel_id=1, source_target_pairs={{0,1},{1,0},{2,3},{3,2},{4,5},{5,4},{6,7},{7,6},{8,9},{9,8},{10,11... | collective-permute-start | bytes 442376 | tf_op jit(solution)/shard_map/ppermute | solution.py:153
  604.0 17.0 %collective-permute-start.98 = (bf16[24,3072]{1,0:T(8,128)(2,1)S(1)}, bf16[24,3072]{1,0:T(8,128)(2,1)S(1)}, u32[]{:S(2)}, u32[]{:S(2)}) collective-permute-start(bf16[24,3072]{1,0:T(8,128)(2,1)S(1)} %pad_maximum_fusion.18), channel_id=1, source_target_pairs={{0,2},{1,3},{2,0},{3,1},{4,6},{5,7},{6,4},{7,5},{8,10},{9,11},{10,... | collective-permute-start | bytes 442376 | tf_op jit(solution)/shard_map/ppermute | solution.py:153
  608.7 15.1 %collective-permute-start.91 = (bf16[24,3584]{1,0:T(8,128)(2,1)S(1)}, bf16[24,3584]{1,0:T(8,128)(2,1)S(1)}, u32[]{:S(2)}, u32[]{:S(2)}) collective-permute-start(bf16[24,3584]{1,0:T(8,128)(2,1)S(1)} %get-tuple-element.576), channel_id=1, source_target_pairs={{0,1},{1,0},{2,3},{3,2},{4,5},{5,4},{6,7},{7,6},{8,9},{9,8},{10,11... | collective-permute-start | bytes 516104 | tf_op jit(solution)/shard_map/ppermute | solution.py:153
  609.3 21.9 %collective-permute-start.92 = (bf16[24,3584]{1,0:T(8,128)(2,1)S(1)}, bf16[24,3584]{1,0:T(8,128)(2,1)S(1)}, u32[]{:S(2)}, u32[]{:S(2)}) collective-permute-start(bf16[24,3584]{1,0:T(8,128)(2,1)S(1)} %get-tuple-element.575), channel_id=1, source_target_pairs={{0,2},{1,3},{2,0},{3,1},{4,6},{5,7},{6,4},{7,5},{8,10},{9,11},{10,... | collective-permute-start | bytes 516104 | tf_op jit(solution)/shard_map/ppermute | solution.py:153
  656.8 24.6 %all-to-all-start.4 = ((f32[32,4,128]{2,1,0:T(4,128)}), f32[32,4,128]{2,1,0:T(4,128)}, u32[]{:S(2)}, u32[]{:S(2)}) async-start(f32[32,4,128]{2,1,0:T(4,128)} %broadcast_in_dim.243), calls=%async_computation.5 | async-start | bytes 131072 | tf_op jit(solution)/shard_map/all_to_all | solution.py:319
  (230 other events, 1747.9 us)

commit v3 on v2

--- a/solution.py
+++ b/solution.py
@@ -153,6 +153,10 @@
     return lax.ppermute(values, "narrow", [(z, z ^ step) for z in range(size)])
 
 
+def trade(blocks):
+    return lax.all_to_all(blocks, "narrow", 0, 0)
+
+
 class Gather:
     def __init__(self, arrays):
         self.columns = [array.shape[1] for array in arrays]
@@ -177,12 +181,25 @@
         ]
         return self.halves
 
-    def plane(self):
+    def line_whole(self, *before):
+        size = lax.axis_size("narrow")
+        blocks = trade(jnp.broadcast_to(self.packed[None], (size,) + self.packed.shape))
+        blocks = pin(blocks, *before)
+        self.halves = [
+            blocks[None, :, :, : self.middle],
+            blocks[None, :, :, self.middle :],
+        ]
+        return self.halves
+
+    def plane(self, first=(), last=()):
         self.pieces = []
-        for held, order in zip(self.halves, orders()):
+        for held, order in zip(pin(self.halves, first), orders()):
             for dim in order[:-1]:
                 held = jnp.concatenate([held, swap(held, dim)], axis=0)
-            self.pieces.append([held, swap(held, order[-1])])
+            self.pieces.append([held])
+        self.pieces = pin(self.pieces, last)
+        for piece, order in zip(self.pieces, orders()):
+            piece.append(swap(piece[0], order[-1]))
         return self.pieces
 
     def core(self):
@@ -272,6 +289,11 @@
         self.send()
         return self.receive()
 
+    def absorb(self, other):
+        self.terms += other.terms
+        self.fixed += other.fixed
+        self.dims += other.dims
+
     def hold(self, *others):
         arrays = pin([[term[0] for term in terms] for terms in self.terms], *others)
         self.terms = [
@@ -283,25 +305,39 @@
         size = lax.axis_size("narrow")
         me = lax.axis_index("narrow")
         depth = min(terms[0][0].shape[-2] for terms in self.terms)
-        sums = [self.cut(number, fixed) for number, fixed in enumerate(self.fixed)]
-        sums = lax.optimization_barrier(sums)
-
-        def columns_of(spot):
-            flat = []
-            for item in sums:
-                block = lax.dynamic_index_in_dim(item, spot, 0, keepdims=False)
-                flat.extend(block[k : k + depth] for k in range(0, block.shape[0], depth))
-            return jnp.concatenate(flat, axis=1) if len(flat) > 1 else flat[0]
-
-        self.goes = [columns_of(me ^ step).astype(jnp.bfloat16) for step in range(1, size)]
-        self.own = columns_of(me)
+        flat = []
+        for number, fixed in enumerate(self.fixed):
+            block = self.cut(number, fixed)
+            flat.extend(block[:, k : k + depth] for k in range(0, block.shape[1], depth))
+        whole = jnp.concatenate(flat, axis=2) if len(flat) > 1 else flat[0]
+        whole = lax.optimization_barrier(whole)
+        self.goes = [
+            lax.dynamic_index_in_dim(whole, me ^ step, 0, keepdims=False).astype(jnp.bfloat16)
+            for step in range(1, size)
+        ]
+        self.own = lax.dynamic_index_in_dim(whole, me, 0, keepdims=False)
         return self.goes
 
     def finish(self, *before):
         arrived = [reach(item, step + 1) for step, item in enumerate(self.goes)]
         arrived = pin(arrived, *before)
-        depth = self.own.shape[0]
-        total = self.own + sum(item.astype(jnp.float32) for item in arrived)
+        return self.apart(self.own + sum(item.astype(jnp.float32) for item in arrived))
+
+    def line_whole(self, *before):
+        depth = min(terms[0][0].shape[-2] for terms in self.terms)
+        flat = []
+        for number, fixed in enumerate(self.fixed):
+            block = self.cut(number, fixed).astype(jnp.bfloat16)
+            flat.extend(block[:, k : k + depth] for k in range(0, block.shape[1], depth))
+        self.goes = pin(jnp.concatenate(flat, axis=2) if len(flat) > 1 else flat[0], *before)
+        self.arrived = trade(self.goes)
+        return self.arrived
+
+    def finish_whole(self):
+        return self.apart(jnp.sum(self.arrived.astype(jnp.float32), axis=0))
+
+    def apart(self, total):
+        depth = total.shape[0]
         results, start = [], 0
         for terms in self.terms:
             parts, columns = terms[0][0].shape[-2] // depth, terms[0][0].shape[-1]
@@ -590,50 +626,121 @@
     )(lengths, grad_mixed, input_all, grad_sum, *saved, gain, feed_rows, *head_rows)
 
 
+def square_kernel(count, *refs):
+    terms, extra_ref, out_ref = refs[:count], refs[count], refs[count + 1]
+    total = jnp.zeros((1, 1), jnp.float32)
+    for ref in terms:
+        rows = jnp.sum(ref[...] * ref[...], axis=1, keepdims=True)
+        total = total + jnp.sum(rows, axis=0, keepdims=True)
+    spot = lax.broadcasted_iota(jnp.int32, out_ref.shape, 1)
+    out_ref[...] = extra_ref[...] + jnp.where(spot == 0, total, 0.0)
+
+
+def add_squares(arrays, extra):
+    return pl.pallas_call(
+        partial(square_kernel, len(arrays)),
+        out_shape=jax.ShapeDtypeStruct(extra.shape, jnp.float32),
+    )(*arrays, extra)
+
+
+def stepped(master, first, second, grad, decay):
+    correct_one = 1.0 - BETA_ONE**STEP_COUNT
+    correct_two = 1.0 - BETA_TWO**STEP_COUNT
+    moment_one = BETA_ONE * first + (1.0 - BETA_ONE) * grad
+    moment_two = BETA_TWO * second + (1.0 - BETA_TWO) * grad * grad
+    direction = moment_one / correct_one / (jnp.sqrt(moment_two / correct_two) + ADAM_EPS)
+    return master - LEARN_RATE * (direction + decay * master), moment_one, moment_two
+
+
+def update_kernel(layout, factor_ref, *refs):
+    count = len(layout)
+    olds, refs = refs[: 3 * count], refs[3 * count :]
+    grads, outs = refs[: -3 * count], refs[-3 * count :]
+    factor = factor_ref[0]
+    used = 0
+    for number, entries in enumerate(layout):
+        for lead, widths in enumerate(entries):
+            start = 0
+            for columns in widths:
+                at = (slice(None), slice(start, start + columns))
+                at = (lead,) + at if len(entries) > 1 else at
+                news = stepped(
+                    *(ref[at] for ref in olds[3 * number : 3 * number + 3]),
+                    grads[used][...] * factor,
+                    DECAY_RATE,
+                )
+                for ref, new in zip(outs[3 * number : 3 * number + 3], news):
+                    ref[at] = new
+                start += columns
+                used += 1
+
+
+def entire(array):
+    zeros = (0,) * array.ndim
+    return pl.BlockSpec(array.shape, lambda i: zeros)
+
+
+def update_many(factor, triples, grads):
+    layout = [[[piece.shape[1] for piece in row] for row in rows] for rows in grads]
+    flat = [piece for rows in grads for row in rows for piece in row]
+    olds = [array for triple in triples for array in triple]
+    return pl.pallas_call(
+        partial(update_kernel, layout),
+        out_shape=tuple(jax.ShapeDtypeStruct(array.shape, jnp.float32) for array in olds),
+        grid=(1,),
+        in_specs=[pl.BlockSpec(memory_space=pltpu.SMEM)] + [entire(item) for item in olds + flat],
+        out_specs=tuple(entire(item) for item in olds),
+        compiler_params=pltpu.CompilerParams(vmem_limit_bytes=60 << 20),
+        cost_estimate=pl.CostEstimate(
+            flops=20 * sum(item.size for item in flat),
+            bytes_accessed=28 * sum(item.size for item in flat),
+            transcendentals=sum(item.size for item in flat),
+        ),
+    )(factor.reshape(1), *olds, *flat)
+
+
 def gelu_parts(values):
     below = 0.5 + 0.5 * lax.erf(values * (0.5**0.5))
     density = jnp.exp(-0.5 * values * values) * ((0.5 / jnp.pi) ** 0.5)
     return values * below, below + values * density
 
 
-def softmax_head(queries, keys, alive):
-    raw = lax.dot_general(
-        queries, keys, (((1,), (1,)), ((), ())), preferred_element_type=jnp.float32
-    ) * HEAD ** (-0.5)
-    scores = jnp.where(alive, raw, MASKED_FILL)
+def softmax_head(queries, keys, masking):
+    scores = product_right(queries * HEAD ** (-0.5), keys) + masking
     expo = jnp.exp(scores - jnp.max(scores, axis=-1, keepdims=True))
-    return expo / jnp.sum(expo, axis=-1, keepdims=True)
+    return expo * (1.0 / jnp.sum(expo, axis=-1, keepdims=True))
+
+
+def masking_row(tokens, length):
+    alive = lax.broadcasted_iota(jnp.int32, (1, tokens), 1) < length
+    return jnp.where(alive, 0.0, MASKED_FILL)
 
 
 def attend_kernel(length_ref, query_ref, key_ref, value_ref, context_ref):
-    tokens = query_ref.shape[0]
-    alive = lax.broadcasted_iota(jnp.int32, (tokens, tokens), 1) < length_ref[pl.program_id(0)]
+    masking = masking_row(query_ref.shape[0], length_ref[pl.program_id(0)])
     contexts = []
     for start in (0, HEAD):
         part = slice(start, start + HEAD)
-        attention = softmax_head(query_ref[:, part], key_ref[:, part], alive)
+        attention = softmax_head(query_ref[:, part], key_ref[:, part], masking)
         contexts.append(product(attention.astype(jnp.bfloat16), value_ref[:, part]))
     context_ref[...] = jnp.concatenate(contexts, axis=1).astype(jnp.bfloat16)
 
 
 def attend_back_kernel(length_ref, query_ref, key_ref, value_ref, grad_ref, out_ref):
-    tokens = query_ref.shape[0]
-    alive = lax.broadcasted_iota(jnp.int32, (tokens, tokens), 1) < length_ref[pl.program_id(0)]
+    masking = masking_row(query_ref.shape[0], length_ref[pl.program_id(0)])
     outs = ([], [], [])
     for start in (0, HEAD):
         part = slice(start, start + HEAD)
         queries, keys, values = query_ref[:, part], key_ref[:, part], value_ref[:, part]
         grad = grad_ref[:, part]
-        attention = softmax_head(queries, keys, alive)
+        attention = softmax_head(queries, keys, masking)
         grad_attention = product_right(grad, values)
         grad_scores = attention * (
             grad_attention - jnp.sum(grad_attention * attention, axis=-1, keepdims=True)
         )
-        grad_raw = (grad_scores.astype(jnp.bfloat16).astype(jnp.float32) * HEAD ** (-0.5)).astype(
-            jnp.bfloat16
-        )
-        outs[0].append(product(grad_raw, keys))
-        outs[1].append(product_left(grad_raw, queries))
+        grad_raw = grad_scores.astype(jnp.bfloat16)
+        outs[0].append(product(grad_raw, keys) * HEAD ** (-0.5))
+        outs[1].append(product_left(grad_raw, queries * HEAD ** (-0.5)))
         outs[2].append(product_left(attention.astype(jnp.bfloat16), grad))
     for number, pair in enumerate(outs):
         start = number * (out_ref.shape[1] // 3) + pl.program_id(1) * LANES
@@ -941,15 +1048,24 @@
     )
     sent = head_sum.send()
     grad_table = product_left(pin(grad_logits, sent), heads)
+    def halves(values):
+        high = values.astype(low)
+        return high, (values - high.astype(jnp.float32)).astype(low)
+
+    table_high, table_rest = halves(grad_table)
+    chosen = product(own_first, table_high) + product(own_first, table_rest)
+    table_square = jnp.sum(grad_table * grad_table)
+    present = jnp.sum(own_first.astype(jnp.float32), axis=1, keepdims=True)
     masked_shared = jnp.sum(all_counted * pin(log_totals, sent))
     head_sum.receive()
     for _ in range(1, bits_of(lax.axis_size("wide"))):
         head_sum.step()
     grad_vocab = jnp.sum(grad_logits.astype(jnp.float32), axis=0)
     vocab_pad = -(-vocab_rows // (8 * LANES)) * 8 * LANES
-    all_vocab = share_small(jnp.pad(grad_vocab, (0, vocab_pad - vocab_rows)).reshape(-1, LANES))
+    grad_vocab = jnp.pad(grad_vocab, (0, vocab_pad - vocab_rows)).reshape(-1, LANES)
+    all_vocab = share_small(grad_vocab)
     head_sum.line()
-    grad_head = jnp.concatenate(head_sum.finish(grad_table, all_vocab), axis=1)
+    grad_head = jnp.concatenate(head_sum.finish(grad_table, all_vocab, table_square, chosen), axis=1)
 
     def owners(values):
         return values.reshape(devices, -1, values.shape[1])
@@ -1032,8 +1148,8 @@
     last_away = last_sum.send()
     in_came = in_sum.receive()
     feed_sum.hold(last_away)
-    feed_away = feed_sum.line()
-    in_sum.hold(feed_away)
+    feed_came = feed_sum.line_whole()
+    in_sum.hold(feed_sum.goes)
     in_away = in_sum.send()
     last_sum.receive()
     last_sum.hold(in_away)
@@ -1047,53 +1163,50 @@
     while last_sum.dims[0]:
         last_sum.step()
     sent = last_sum.line()
-    sum_feed_in, sum_dense, sum_feed_out, sum_pooler = feed_sum.finish(sent)
+    sum_feed_in, sum_dense, sum_feed_out, sum_pooler = feed_sum.finish_whole()
     sum_mixed, sum_value, sum_output = in_sum.finish(sent)
     words_left, words_right, sum_small = last_sum.finish()
-    sum_input = jnp.concatenate([sum_mixed, sum_value], axis=1)
 
     def return_more(state):
-        turn, grad_table = state
+        turn, grad_table, table_square = state
         own, mine = picks(turn * ahead)
         back = lax.psum_scatter(
             product(mine, embedded_low), AXES, scatter_dimension=0, tiled=True
         )
-        return turn + 1, grad_table + exact(own.T.astype(jnp.float32), back)
-
-    _, grad_table = lax.while_loop(
-        lambda state: state[0] < rounds, return_more, (jnp.int32(1), grad_table)
-    )
-
-    def halves(values):
-        high = values.astype(low)
-        return high, (values - high.astype(jnp.float32)).astype(low)
-
-    table_high, table_rest = halves(grad_table)
-    chosen = product(own_first, table_high) + product(own_first, table_rest)
-    table_square = jnp.sum(grad_table * grad_table)
-    present = jnp.sum(own_first.astype(jnp.float32), axis=1, keepdims=True)
+        chosen = exact(own.astype(jnp.float32), grad_table)
+        present = jnp.sum(own.astype(jnp.float32), axis=1, keepdims=True)
+        table_square = table_square + jnp.sum(present * back * (back + 2.0 * chosen))
+        return turn + 1, grad_table + exact(own.T.astype(jnp.float32), back), table_square
+
+    _, grad_table, table_square = lax.while_loop(
+        lambda state: state[0] < rounds, return_more, (jnp.int32(1), grad_table, table_square)
+    )
     words_own = jnp.concatenate([words_left, words_right], axis=1)
     table_square = table_square + jnp.sum(present * words_own * (words_own + 2.0 * chosen))
 
     sum_vector = sum_small[:, tokens + 4 : tokens + 4 + vector_count]
-    pieces = [
-        sum_small[:, :tokens],
-        jnp.moveaxis(sum_small[:, tokens : tokens + 4].reshape(depth, 2, 2), 1, 0),
-        sum_input,
-        sum_output,
-        jnp.stack([sum_dense, sum_pooler]),
-        jnp.stack([sum_feed_in, sum_feed_out]),
-    ]
+    sum_position = sum_small[:, :tokens]
+    sum_pair = sum_small[:, tokens : tokens + 4]
+    scalars = jnp.stack([table_square, target_local, pair_local])
+    scalars = add_squares(
+        [
+            sum_small[:, : tokens + 4 + vector_count],
+            sum_mixed,
+            sum_value,
+            sum_output,
+            sum_dense,
+            sum_pooler,
+            sum_feed_in,
+            sum_feed_out,
+            grad_vocab,
+        ],
+        jnp.pad(scalars, (0, LANES - 3))[None],
+    )
+    totals = jnp.sum(share_small(scalars)[:, 0, :3], axis=0)
     vector_flat = depth * vector_count
     vector_pad = -(-vector_flat // LANES) * LANES
-    all_vector = share_small(
-        jnp.pad(sum_vector.reshape(-1), (0, vector_pad - vector_flat)).reshape(-1, LANES)
-    )
-    squares = table_square + sum(
-        (jnp.sum(item * item) for item in pieces + [sum_vector, grad_vocab])
-    )
-    scalars = jnp.stack([squares, target_local, pair_local])
-    totals = jnp.sum(share_small(jnp.pad(scalars, (0, LANES - 3))[None])[:, 0, :3], axis=0)
+    flat_vector = jnp.pad(sum_vector.reshape(-1), (0, vector_pad - vector_flat))
+    all_vector = share_small(pin(flat_vector.reshape(-1, LANES), totals))
     grad_table = grad_table + product_left(
         jnp.concatenate([own_first, own_first], axis=0),
         jnp.concatenate(halves(words_own), axis=0),
@@ -1106,35 +1219,38 @@
             all_vocab.reshape(devices, -1)[:, :vocab_rows].reshape(-1),
         ]
     )
-    pieces = (
-        [grad_table]
-        + pieces
-        + [lax.dynamic_slice_in_dim(grad_vector, me * vector_each, vector_each, 0)]
-    )
+    totals, grad_table = lax.optimization_barrier((totals, grad_table))
     norm = jnp.sqrt(totals[0])
     masked_total = masked_shared - totals[1]
     pair_total_sum = totals[2]
     factor = CLIP_NORM / (norm + 1e-06)
-    correct_one = 1.0 - BETA_ONE**STEP_COUNT
-    correct_two = 1.0 - BETA_TWO**STEP_COUNT
-    updated = []
-    for number in range(8):
-        turned = (lambda item: item.T) if number == 1 else (lambda item: item)
-        master = turned(masters[number])
-        grad = pieces[number] * factor
-        moment_one = BETA_ONE * turned(firsts[number]) + (1.0 - BETA_ONE) * grad
-        moment_two = BETA_TWO * turned(seconds[number]) + (1.0 - BETA_TWO) * grad * grad
-        direction = moment_one / correct_one / (jnp.sqrt(moment_two / correct_two) + ADAM_EPS)
-        decay = DECAY_RATE if number < 7 else 0.0
-        updated.extend(
-            [
-                turned(master - LEARN_RATE * (direction + decay * master)),
-                turned(moment_one),
-                turned(moment_two),
-            ]
-        )
+
+    def straight(number):
+        return masters[number], firsts[number], seconds[number]
+
+    position = tuple(item.T for item in straight(1))
+    many = update_many(
+        factor,
+        [position] + [straight(number) for number in (3, 4, 5, 6)],
+        [
+            [[sum_position]],
+            [[sum_mixed, sum_value]],
+            [[sum_output]],
+            [[sum_dense], [sum_pooler]],
+            [[sum_feed_in], [sum_feed_out]],
+        ],
+    )
+    pair_grad = jnp.moveaxis(sum_pair.reshape(depth, 2, 2), 1, 0)
+    vector_grad = lax.dynamic_slice_in_dim(grad_vector, me * vector_each, vector_each, 0)
+    updated = (
+        stepped(*straight(0), grad_table * factor, DECAY_RATE)
+        + tuple(item.T for item in many[:3])
+        + stepped(*straight(2), pair_grad * factor, DECAY_RATE)
+        + tuple(many[3:])
+        + stepped(*straight(7), vector_grad * factor, 0.0)
+    )
     masked_sums = jnp.stack([masked_total, masked_count])
-    return (masked_sums, pair_total_sum, norm) + tuple(updated)
+    return (masked_sums, pair_total_sum, norm) + updated
 
 
 def solution(mesh):

time: 703 us -> 678 us (0.964)
  waiting for transfers between devices: 139 us -> 128 us
    ppermute x76, waiting for transfers between devices: 100 us -> 89 us  [swap(): lax.ppermute(values, dim[0], [(i, i ^ 1 << dim[1]) for i in range(size)])]
    ppermute x27 -> x24, starting transfers between devices: 51.4 us -> 44 us  [reach(): return lax.ppermute(values, 'narrow', [(z, z ^ step) for z in range(size)])]
    add x12 -> x7, other arithmetic: 16.3 us -> 8.99 us  [cut(): total = part if total is None else total + part]
    ppermute x27 -> x24, waiting for transfers between devices: 28.8 us -> 31 us  [reach(): return lax.ppermute(values, 'narrow', [(z, z ^ step) for z in range(size)])]
    unnamed x412 -> x334, local copies, waits for them, and re-layouts: 20.8 us -> 19.8 us
  transfers between devices with their start and end apart: 108 -> 106, of which waited for: 29 -> 27; matrix products, arithmetic and copies ran while one was open for 31% -> 30% of each run, Pallas kernels for 8% -> 9%
where the time goes in v3:
time: 678 us; the launch traced here: 667 us
  other arithmetic  138 us (20%)
  starting transfers between devices  130 us (19%)
  waiting for transfers between devices  128 us (19%)
  matrix products  94.7 us (14%)
  Pallas kernels  88.3 us (13%)
  local copies, waits for them, and re-layouts  64.3 us (9%)
  between operations  23.3 us (3%)
    ppermute x76, waiting for transfers between devices, swap(): lax.ppermute(values, dim[0], [(i, i ^ 1 << dim[1]) for i in range(size)])  89 us
    ppermute x76, starting transfers between devices, swap(): lax.ppermute(values, dim[0], [(i, i ^ 1 << dim[1]) for i in range(size)])  55.6 us
    ppermute x24, starting transfers between devices, reach(): return lax.ppermute(values, 'narrow', [(z, z ^ step) for z in range(size)])  44 us
    dot_general x13, matrix products, product_left(): lax.dot_general(left, right, (((0,), (0,)), ((), ())), preferred_element_...  38.3 us
    convert_element_type x24, other arithmetic, send(): self.away.append(self.cut(number, fixed).astype(jnp.bfloat16))  37.8 us
    dot_general x13, matrix products, product(): return jnp.dot(left, right, preferred_element_type=jnp.float32)  31.6 us
    ppermute x24, waiting for transfers between devices, reach(): return lax.ppermute(values, 'narrow', [(z, z ^ step) for z in range(size)])  31 us
    pallas_call x1, Pallas kernels, attend_back(): pl.pallas_call(attend_back_kernel, grid_spec=pltpu.PrefetchScalarGridSpec...  22.5 us
  transfers between devices with their start and end apart: 106, of which 27 were waited for; matrix products, arithmetic and copies ran while one was open for 30% of the time, Pallas kernels for 9%

profile of v3, /device:TPU:0, one launch (start us, length us, event | category | flops | bytes accessed | tf_op | source)
XLA Modules:
  0.0 666.9 jit_solution(15799743367434140104)
XLA Ops:
  11.3 7.3 %all-to-all-start = ((s32[32,16,128]{2,1,0:T(8,128)}), s32[32,16,128]{2,1,0:T(8,128)S(1)}, u32[]{:S(2)}, u32[]{:S(2)}) async-start(s32[32,16,128]{2,1,0:T(8,128)} %broadcast_in_dim.129), calls=%async_computation.1 | async-start | bytes 524288 | tf_op jit(solution)/shard_map/all_to_all | solution.py:855
  24.0 2.4 collective-permute-start.8
  35.6 4.9 convert_reduce_fusion.5
  42.4 3.3 collective-permute-start.1
  64.0 13.7 %collective-permute-done.3 = bf16[1,4,96,384]{3,2,1,0:T(8,128)(2,1)S(1)} collective-permute-done((bf16[1,4,96,384]{3,2,1,0:T(8,128)(2,1)S(1)}, bf16[1,4,96,384]{3,2,1,0:T(8,128)(2,1)S(1)}, u32[]{:S(2)}, u32[]{:S(2)}) %collective-permute-start.3) | collective-permute-done | bytes 294944 | tf_op jit(solution)/shard_map/ppermute | solution.py:102
  79.8 5.1 collective-permute-start.22
  84.9 2.4 collective-permute-start.24
  96.5 4.2 collective-permute-start.33
  101.7 2.4 collective-permute-start.35
  130.7 5.6 fusion.29
  137.0 2.3 fusion.44
  140.2 14.1 %collective-permute-done.36 = bf16[1,4,24,2304]{3,2,1,0:T(8,128)(2,1)} collective-permute-done((bf16[1,4,24,2304]{3,2,1,0:T(8,128)(2,1)}, bf16[1,4,24,2304]{3,2,1,0:T(8,128)(2,1)}, u32[]{:S(2)}, u32[]{:S(2)}) %collective-permute-start.36) | collective-permute-done | bytes 442400 | tf_op jit(solution)/shard_map/ppermute | solution.py:102
  155.5 2.5 pad_maximum_fusion.4.refs_4_
  162.2 3.1 add_convert_fusion.query_ref.key_ref.value_ref
  166.0 12.5 %collective-permute-done.38.refs_1_ = bf16[2,4,24,2304]{3,2,1,0:T(8,128)(2,1)S(1)} collective-permute-done((bf16[2,4,24,2304]{3,2,1,0:T(8,128)(2,1)S(1)}, bf16[2,4,24,2304]{3,2,1,0:T(8,128)(2,1)S(1)}, u32[]{:S(2)}, u32[]{:S(2)}) %collective-permute-start.38) | collective-permute-done | bytes 884768 | tf_op jit(solution)/shard_map/ppermute | solution.py:102
  183.3 15.0 %shard_map.487 = bf16[768,768]{1,0:T(8,128)(2,1)S(1)} custom-call(s32[2]{0:T(128)S(1)} %bitcast.688, bf16[768,2304]{1,0:T(8,128)(2,1)S(1)} %add_convert_fusion.query_ref.key_ref.value_ref, bf16[768,2304]{1,0:T(8,128)(2,1)S(1)} %add_convert_fusion.query_ref.key_ref.value_ref, bf16[768,2304]{1,0:T(8,128)(2,1)S(1)} %add_convert_fusion.query_ref.key_ref.value_ref), custom_call_target="tpu_custom_call" | custom-call | flops 1811939328 | bytes 4718592 | tf_op jit(solution)/shard_map/pallas_call | solution.py:763
  199.5 3.2 shard_map.488
  205.2 9.9 %fusion.26 = (f32[768,3072]{1,0:T(8,128)}, bf16[768,3072]{1,0:T(8,128)(2,1)}) fusion(f32[3072]{0:T(1024)S(1)} %slice.507, bf16[768,3072]{1,0:T(8,128)(2,1)S(1)} %bitcast.631, f32[768,768]{1,0:T(8,128)S(1)} %subtract_multiply_fusion.1.normal_one_ref, f32[768]{0:T(1024)S(1)} %copy-done.83, f32[768]{0:T(1024)S(1)} %get-tuple-element.610), kind=kOutput, calls=%fused_computation.46 | convolution fusion | flops 3651600384 | bytes 21252096 | tf_op jit(solution)/shard_map/dot_general | solution.py:30
  215.1 4.3 shard_map.489
  219.5 7.9 %fusion.186 = (f32[768]{0:T(1024)S(1)}, f32[768,768]{1,0:T(8,128)S(1)}) fusion(f32[768]{0:T(1024)S(1)} %copy-done.142, bf16[768,3072]{1,0:T(8,128)(2,1)} %get-tuple-element.308, bf16[768,3072]{1,0:T(8,128)(2,1)S(1)} %bitcast.633, f32[768]{0:T(1024)S(1)} %copy-done.83, f32[768,768]{1,0:T(8,128)S(1)} %subtract_multiply_fusion.1.normal_one_ref, ...), kind=kOutput, calls=%fused_computation.526 | convolution fusion | flops 3626827008 | bytes 14168064 | tf_op jit(solution)/shard_map/dot_general | solution.py:34
  232.8 2.4 collective-permute-start.46
  235.2 4.8 collective-permute-done.44
  240.0 6.4 collective-permute-done.45
  249.1 6.9 %collective-permute-done.47 = bf16[1,4,112,384]{3,2,1,0:T(8,128)(2,1)S(1)} collective-permute-done((bf16[1,4,112,384]{3,2,1,0:T(8,128)(2,1)S(1)}, bf16[1,4,112,384]{3,2,1,0:T(8,128)(2,1)S(1)}, u32[]{:S(2)}, u32[]{:S(2)}) %collective-permute-start.47) | collective-permute-done | bytes 344096 | tf_op jit(solution)/shard_map/ppermute | solution.py:102
  260.3 13.6 %collective-permute-done.49.refs_1_ = bf16[2,4,112,384]{3,2,1,0:T(8,128)(2,1)} collective-permute-done((bf16[2,4,112,384]{3,2,1,0:T(8,128)(2,1)}, bf16[2,4,112,384]{3,2,1,0:T(8,128)(2,1)}, u32[]{:S(2)}, u32[]{:S(2)}) %collective-permute-start.49) | collective-permute-done | bytes 688160 | tf_op jit(solution)/shard_map/ppermute | solution.py:102
  279.0 3.0 shard_map.490
  282.0 5.5 add_reduce_fusion
  287.6 5.5 fusion.21
  294.0 6.7 %all-to-all-start.1 = ((f32[32,28,128]{2,1,0:T(8,128)}), f32[32,28,128]{2,1,0:T(8,128)}, u32[]{:S(2)}, u32[]{:S(2)}) async-start(f32[32,28,128]{2,1,0:T(8,128)} %broadcast_in_dim.235), calls=%async_computation.2 | async-start | bytes 1048576 | tf_op jit(solution)/shard_map/all_to_all | solution.py:355
  310.7 4.4 all-to-all-done.1
  318.7 8.7 %convert_reduce_fusion.1 = (f32[956]{0:T(1024)S(1)}, bf16[3584,956]{0,1:T(8,128)(2,1)S(1)}) fusion(f32[3584]{0:T(1024)} %broadcast_multiply_fusion, s32[3584]{0:T(1024)} %eq.107, s32[956]{0:T(1024)} %iota_add_fusion, f32[3584]{0:T(1024)S(1)} %add_bitcast_fusion, f32[3584,956]{0,1:T(8,128)} %copy-done.30, f32[956]{0:T(1024)} %copy-done.110), kind=kLoop, calls=%fused_computation.38 | loop fusion | flops 30835780 | bytes 20612304 | tf_op jit(solution)/shard_map/reduce_sum | solution.py:1063
  327.4 4.0 fusion.71
  331.5 4.0 fusion.69
  344.6 8.1 %multiply_reduce_fusion = (f32[]{:T(128)}, f32[956,768]{1,0:T(8,128)}) fusion(bf16[3584,956]{0,1:T(8,128)(2,1)S(1)} %get-tuple-element.333, bf16[3584,768]{1,0:T(8,128)(2,1)S(1)} %bitcast.616), kind=kOutput, calls=%fused_computation.66 | convolution fusion | flops 5264271360 | bytes 15294468 | tf_op jit(solution)/shard_map/dot_general | solution.py:40
  354.0 3.5 all-to-all-start.2
  364.9 6.1 collective-permute-done.60
  377.0 2.4 collective-permute-start.62
  383.8 8.5 %collective-permute-done.62 = bf16[112,768]{1,0:T(8,128)(2,1)} collective-permute-done((bf16[112,768]{1,0:T(8,128)(2,1)}, bf16[112,768]{1,0:T(8,128)(2,1)}, u32[]{:S(2)}, u32[]{:S(2)}) %collective-permute-start.62) | collective-permute-done | bytes 172064 | tf_op jit(solution)/shard_map/ppermute | solution.py:153
  398.0 2.5 convolution_add_fusion.2.grad_ref
  400.5 19.5 %shard_map.491 = (bf16[768,768]{1,0:T(8,128)(2,1)}, bf16[768,3072]{1,0:T(8,128)(2,1)}, f32[768,768]{1,0:T(8,128)}, bf16[768,768]{1,0:T(8,128)(2,1)}, bf16[768,768]{1,0:T(8,128)(2,1)}, /*index=5*/f32[32,768]{1,0:T(8,128)}) custom-call(f32[768,768]{1,0:T(8,128)} %convolution_add_fusion.2.grad_ref, f32[768,768]{1,0:T(8,128)} %copy-done.35, ...), custom_call_target="tpu_custom_call" | custom-call | flops 8153726976 | bytes 37748736 | tf_op jit(solution)/shard_map/pallas_call | solution.py:470
  420.1 5.8 fusion.111
  428.0 7.7 %fusion.191 = f32[768,3072]{1,0:T(8,128)S(1)} fusion(bf16[768,768]{1,0:T(8,128)(2,1)S(1)} %copy-done.63, bf16[768,3072]{1,0:T(8,128)(2,1)} %get-tuple-element.308), kind=kOutput, calls=%fused_computation.531 | convolution fusion | flops 3623878656 | bytes 15335424 | tf_op jit(solution)/shard_map/dot_general | solution.py:40
  435.7 3.6 copy-done.33
  451.6 2.2 fusion.38
  455.2 2.3 fusion.37
  463.7 22.5 %shard_map.492.mixed_ref = bf16[768,2304]{1,0:T(8,128)(2,1)S(1)} custom-call(s32[2]{0:T(128)S(1)} %bitcast.689, bf16[768,2304]{1,0:T(8,128)(2,1)S(1)} %add_convert_fusion.query_ref.key_ref.value_ref, bf16[768,2304]{1,0:T(8,128)(2,1)S(1)} %add_convert_fusion.query_ref.key_ref.value_ref, bf16[768,2304]{1,0:T(8,128)(2,1)S(1)} %add_convert_fusion.query_ref.key_ref.value_ref, ...), custom_call_target="tpu_custom_call" | custom-call | flops 4529848320 | bytes 8257536 | tf_op jit(solution)/shard_map/pallas_call | solution.py:786
  486.3 4.0 fusion.61
  490.3 2.8 fusion.60
  509.1 9.6 %shard_map.493 = (bf16[768,768]{1,0:T(8,128)(2,1)S(1)}, f32[768,512]{1,0:T(8,128)S(1)}) custom-call(s32[2]{0:T(128)S(1)} %bitcast.690, bf16[768,2304]{1,0:T(8,128)(2,1)} %copy-done.8, bf16[768,2304]{1,0:T(8,128)(2,1)} %bitcast.622, f32[768,768]{1,0:T(8,128)S(1)} %copy-done.11, f32[768,768]{1,0:T(8,128)} %get-tuple-element.529.normal_ref, ...), custom_call_target="tpu_custom_call" | custom-call | flops 2717908992 | bytes 12976128 | tf_op jit(solution)/shard_map/pallas_call | solution.py:598
  526.6 2.4 fusion.59
  529.0 2.6 fusion.28
  531.6 2.6 fusion.27
  545.6 5.0 all-to-all-start.3
  567.7 8.0 %collective-permute-done.85 = bf16[2,4,96,384]{3,2,1,0:T(8,128)(2,1)S(1)} collective-permute-done((bf16[2,4,96,384]{3,2,1,0:T(8,128)(2,1)S(1)}, bf16[2,4,96,384]{3,2,1,0:T(8,128)(2,1)S(1)}, u32[]{:S(2)}, u32[]{:S(2)}) %collective-permute-start.85) | collective-permute-done | bytes 589856 | tf_op jit(solution)/shard_map/ppermute | solution.py:102
  580.4 2.4 collective-permute-start.98
  582.8 3.3 collective-permute-start.99
  590.9 4.5 collective-permute-done.88
  605.3 7.7 %collective-permute-done.92 = bf16[24,3584]{1,0:T(8,128)(2,1)} collective-permute-done((bf16[24,3584]{1,0:T(8,128)(2,1)}, bf16[24,3584]{1,0:T(8,128)(2,1)}, u32[]{:S(2)}, u32[]{:S(2)}) %collective-permute-start.92) | collective-permute-done | bytes 172064 | tf_op jit(solution)/shard_map/ppermute | solution.py:153
  624.2 5.0 all-to-all-start.4
  629.3 3.2 convolution_add_fusion.1
  632.5 3.8 all-to-all-done.4
  639.1 2.9 all-to-all-start.5
  642.0 7.8 %multiply_subtract_fusion = (f32[956,768]{1,0:T(8,128)}, f32[956,768]{1,0:T(8,128)}, f32[956,768]{1,0:T(8,128)}) fusion(f32[956,768]{1,0:T(8,128)} %param.38, f32[956,768]{1,0:T(8,128)} %convolution_add_fusion.1, f32[]{:T(128)} %div.169, f32[956,768]{1,0:T(8,128)} %param.39, f32[956,768]{1,0:T(8,128)} %param.40), kind=kLoop, calls=%fused_computation.62 | loop fusion | flops 11747328 | bytes 20557828 | tf_op jit(solution)/shard_map/sub | solution.py:652
  651.8 4.4 shard_map.495
  (787 shorter events, 264.9 us)
Async XLA Ops:
  11.3 21.5 %all-to-all-start = ((s32[32,16,128]{2,1,0:T(8,128)}), s32[32,16,128]{2,1,0:T(8,128)S(1)}, u32[]{:S(2)}, u32[]{:S(2)}) async-start(s32[32,16,128]{2,1,0:T(8,128)} %broadcast_in_dim.129), calls=%async_computation.1 | async-start | bytes 524288 | tf_op jit(solution)/shard_map/all_to_all | solution.py:855
  22.2 26.6 %collective-permute-start.7 = (bf16[24,2816]{1,0:T(8,128)(2,1)S(1)}, bf16[24,2816]{1,0:T(8,128)(2,1)S(1)}, u32[]{:S(2)}, u32[]{:S(2)}) collective-permute-start(bf16[24,2816]{1,0:T(8,128)(2,1)S(1)} %constant_dynamic-update-slice_fusion), channel_id=1, source_target_pairs={{0,1},{1,0},{2,3},{3,2},{4,5},{5,4},{6,7},{7,6},{8,9},{9,8},{10,11... | collective-permute-start | bytes 405512 | tf_op jit(solution)/shard_map/ppermute | solution.py:153
  24.0 24.9 %collective-permute-start.8 = (bf16[24,2816]{1,0:T(8,128)(2,1)S(1)}, bf16[24,2816]{1,0:T(8,128)(2,1)S(1)}, u32[]{:S(2)}, u32[]{:S(2)}) collective-permute-start(bf16[24,2816]{1,0:T(8,128)(2,1)S(1)} %constant_dynamic-update-slice_fusion), channel_id=1, source_target_pairs={{0,2},{1,3},{2,0},{3,1},{4,6},{5,7},{6,4},{7,5},{8,10},{9,11},{10,... | collective-permute-start | bytes 405512 | tf_op jit(solution)/shard_map/ppermute | solution.py:153
  26.4 22.5 %collective-permute-start.9 = (bf16[24,2816]{1,0:T(8,128)(2,1)S(1)}, bf16[24,2816]{1,0:T(8,128)(2,1)}, u32[]{:S(2)}, u32[]{:S(2)}) collective-permute-start(bf16[24,2816]{1,0:T(8,128)(2,1)S(1)} %constant_dynamic-update-slice_fusion), channel_id=1, source_target_pairs={{0,3},{1,2},{2,1},{3,0},{4,7},{5,6},{6,5},{7,4},{8,11},{9,10},{10,... | collective-permute-start | bytes 405512 | tf_op jit(solution)/shard_map/ppermute | solution.py:153
  58.6 19.1 %collective-permute-start.12 = (bf16[2,4,24,1408]{3,2,1,0:T(8,128)(2,1)S(1)}, bf16[2,4,24,1408]{3,2,1,0:T(8,128)(2,1)S(1)}, u32[]{:S(2)}, u32[]{:S(2)}) collective-permute-start(bf16[2,4,24,1408]{3,2,1,0:T(8,128)(2,1)S(1)} %pad_maximum_fusion.11.refs_0_), channel_id=1, source_target_pairs={{0,16},{4,20},{8,24},{12,28},{16,0},{20,4},{24,8},{28,12},{1,17},{... | collective-permute-start | bytes 1622024 | tf_op jit(solution)/shard_map/ppermute | solution.py:102
  60.1 18.1 %collective-permute-start.15 = (bf16[2,4,24,1408]{3,2,1,0:T(8,128)(2,1)S(1)}, bf16[2,4,24,1408]{3,2,1,0:T(8,128)(2,1)S(1)}, u32[]{:S(2)}, u32[]{:S(2)}) collective-permute-start(bf16[2,4,24,1408]{3,2,1,0:T(8,128)(2,1)S(1)} %pad_maximum_fusion.12.refs_4_), channel_id=1, source_target_pairs={{0,8},{4,12},{8,0},{12,4},{16,24},{20,28},{24,16},{28,20},{1,9},{5... | collective-permute-start | bytes 1622024 | tf_op jit(solution)/shard_map/ppermute | solution.py:102
  60.8 16.9 %collective-permute-start.3 = (bf16[1,4,96,384]{3,2,1,0:T(8,128)(2,1)S(1)}, bf16[1,4,96,384]{3,2,1,0:T(8,128)(2,1)S(1)}, u32[]{:S(2)}, u32[]{:S(2)}) collective-permute-start(bf16[1,4,96,384]{3,2,1,0:T(8,128)(2,1)S(1)} %maximum_bitcast_fusion.6), channel_id=1, source_target_pairs={{0,8},{4,12},{8,0},{12,4},{16,24},{20,28},{24,16},{28,20},{1,9},{5... | collective-permute-start | bytes 884744 | tf_op jit(solution)/shard_map/ppermute | solution.py:102
  62.7 15.6 %collective-permute-start.4 = (bf16[1,4,96,384]{3,2,1,0:T(8,128)(2,1)S(1)}, bf16[1,4,96,384]{3,2,1,0:T(8,128)(2,1)S(1)}, u32[]{:S(2)}, u32[]{:S(2)}) collective-permute-start(bf16[1,4,96,384]{3,2,1,0:T(8,128)(2,1)S(1)} %maximum_bitcast_fusion.7), channel_id=1, source_target_pairs={{0,16},{4,20},{8,24},{12,28},{16,0},{20,4},{24,8},{28,12},{1,17},{... | collective-permute-start | bytes 884744 | tf_op jit(solution)/shard_map/ppermute | solution.py:102
  63.4 15.7 %collective-permute-start.13 = (bf16[2,4,24,1408]{3,2,1,0:T(8,128)(2,1)S(1)}, bf16[2,4,24,1408]{3,2,1,0:T(8,128)(2,1)S(1)}, u32[]{:S(2)}, u32[]{:S(2)}) collective-permute-start(bf16[2,4,24,1408]{3,2,1,0:T(8,128)(2,1)S(1)} %pad_maximum_fusion.11.refs_0_), channel_id=1, source_target_pairs={{0,4},{4,0},{8,12},{12,8},{16,20},{20,16},{24,28},{28,24},{1,5},{5... | collective-permute-start | bytes 1622024 | tf_op jit(solution)/shard_map/ppermute | solution.py:102
  78.4 15.7 %collective-permute-start.5 = (bf16[2,4,96,384]{3,2,1,0:T(8,128)(2,1)S(1)}, bf16[2,4,96,384]{3,2,1,0:T(8,128)(2,1)S(1)}, u32[]{:S(2)}, u32[]{:S(2)}) collective-permute-start(bf16[2,4,96,384]{3,2,1,0:T(8,128)(2,1)S(1)} %pad_maximum_fusion.9.refs_0_), channel_id=1, source_target_pairs={{0,16},{4,20},{8,24},{12,28},{16,0},{20,4},{24,8},{28,12},{1,17},{... | collective-permute-start | bytes 1769480 | tf_op jit(solution)/shard_map/ppermute | solution.py:102
  79.1 15.5 %collective-permute-start.6 = (bf16[2,4,96,384]{3,2,1,0:T(8,128)(2,1)S(1)}, bf16[2,4,96,384]{3,2,1,0:T(8,128)(2,1)S(1)}, u32[]{:S(2)}, u32[]{:S(2)}) collective-permute-start(bf16[2,4,96,384]{3,2,1,0:T(8,128)(2,1)S(1)} %pad_maximum_fusion.10.refs_4_), channel_id=1, source_target_pairs={{0,8},{4,12},{8,0},{12,4},{16,24},{20,28},{24,16},{28,20},{1,9},{5... | collective-permute-start | bytes 1769480 | tf_op jit(solution)/shard_map/ppermute | solution.py:102
  79.8 21.9 %collective-permute-start.22 = (bf16[24,3840]{1,0:T(8,128)(2,1)S(1)}, bf16[24,3840]{1,0:T(8,128)(2,1)S(1)}, u32[]{:S(2)}, u32[]{:S(2)}) collective-permute-start(bf16[24,3840]{1,0:T(8,128)(2,1)S(1)} %constant_dynamic-update-slice_fusion.2), channel_id=1, source_target_pairs={{0,1},{1,0},{2,3},{3,2},{4,5},{5,4},{6,7},{7,6},{8,9},{9,8},{10,11... | collective-permute-start | bytes 552968 | tf_op jit(solution)/shard_map/ppermute | solution.py:153
  84.9 19.2 %collective-permute-start.23 = (bf16[24,3840]{1,0:T(8,128)(2,1)S(1)}, bf16[24,3840]{1,0:T(8,128)(2,1)}, u32[]{:S(2)}, u32[]{:S(2)}) collective-permute-start(bf16[24,3840]{1,0:T(8,128)(2,1)S(1)} %constant_dynamic-update-slice_fusion.2), channel_id=1, source_target_pairs={{0,2},{1,3},{2,0},{3,1},{4,6},{5,7},{6,4},{7,5},{8,10},{9,11},{10,... | collective-permute-start | bytes 552968 | tf_op jit(solution)/shard_map/ppermute | solution.py:153
  84.9 19.2 %collective-permute-start.24 = (bf16[24,3840]{1,0:T(8,128)(2,1)S(1)}, bf16[24,3840]{1,0:T(8,128)(2,1)}, u32[]{:S(2)}, u32[]{:S(2)}) collective-permute-start(bf16[24,3840]{1,0:T(8,128)(2,1)S(1)} %constant_dynamic-update-slice_fusion.2), channel_id=1, source_target_pairs={{0,3},{1,2},{2,1},{3,0},{4,7},{5,6},{6,5},{7,4},{8,11},{9,10},{10,... | collective-permute-start | bytes 552968 | tf_op jit(solution)/shard_map/ppermute | solution.py:153
  96.5 24.7 %collective-permute-start.33 = (bf16[24,4608]{1,0:T(8,128)(2,1)}, bf16[24,4608]{1,0:T(8,128)(2,1)}, u32[]{:S(2)}, u32[]{:S(2)}) collective-permute-start(bf16[24,4608]{1,0:T(8,128)(2,1)} %constant_dynamic-update-slice_fusion.4), channel_id=1, source_target_pairs={{0,1},{1,0},{2,3},{3,2},{4,5},{5,4},{6,7},{7,6},{8,9},{9,8},{10,11... | collective-permute-start | bytes 663560 | tf_op jit(solution)/shard_map/ppermute | solution.py:153
  100.6 20.5 %collective-permute-start.34 = (bf16[24,4608]{1,0:T(8,128)(2,1)}, bf16[24,4608]{1,0:T(8,128)(2,1)}, u32[]{:S(2)}, u32[]{:S(2)}) collective-permute-start(bf16[24,4608]{1,0:T(8,128)(2,1)} %constant_dynamic-update-slice_fusion.4), channel_id=1, source_target_pairs={{0,2},{1,3},{2,0},{3,1},{4,6},{5,7},{6,4},{7,5},{8,10},{9,11},{10,... | collective-permute-start | bytes 663560 | tf_op jit(solution)/shard_map/ppermute | solution.py:153
  101.7 20.0 %collective-permute-start.35 = (bf16[24,4608]{1,0:T(8,128)(2,1)}, bf16[24,4608]{1,0:T(8,128)(2,1)}, u32[]{:S(2)}, u32[]{:S(2)}) collective-permute-start(bf16[24,4608]{1,0:T(8,128)(2,1)} %constant_dynamic-update-slice_fusion.4), channel_id=1, source_target_pairs={{0,3},{1,2},{2,1},{3,0},{4,7},{5,6},{6,5},{7,4},{8,11},{9,10},{10,... | collective-permute-start | bytes 663560 | tf_op jit(solution)/shard_map/ppermute | solution.py:153
  121.7 43.7 %collective-permute-start.27 = (bf16[2,4,24,1920]{3,2,1,0:T(8,128)(2,1)}, bf16[2,4,24,1920]{3,2,1,0:T(8,128)(2,1)}, u32[]{:S(2)}, u32[]{:S(2)}) collective-permute-start(bf16[2,4,24,1920]{3,2,1,0:T(8,128)(2,1)} %pad_maximum_fusion.5.refs_0_), channel_id=1, source_target_pairs={{0,16},{4,20},{8,24},{12,28},{16,0},{20,4},{24,8},{28,12},{1,17},{... | collective-permute-start | bytes 2211848 | tf_op jit(solution)/shard_map/ppermute | solution.py:102
  126.3 39.1 %collective-permute-start.28 = (bf16[2,4,24,1920]{3,2,1,0:T(8,128)(2,1)}, bf16[2,4,24,1920]{3,2,1,0:T(8,128)(2,1)}, u32[]{:S(2)}, u32[]{:S(2)}) collective-permute-start(bf16[2,4,24,1920]{3,2,1,0:T(8,128)(2,1)} %pad_maximum_fusion.6.refs_4_), channel_id=1, source_target_pairs={{0,8},{4,12},{8,0},{12,4},{16,24},{20,28},{24,16},{28,20},{1,9},{5... | collective-permute-start | bytes 2211848 | tf_op jit(solution)/shard_map/ppermute | solution.py:102
  127.7 26.5 %collective-permute-start.36 = (bf16[1,4,24,2304]{3,2,1,0:T(8,128)(2,1)}, bf16[1,4,24,2304]{3,2,1,0:T(8,128)(2,1)}, u32[]{:S(2)}, u32[]{:S(2)}) collective-permute-start(bf16[1,4,24,2304]{3,2,1,0:T(8,128)(2,1)} %maximum_bitcast_fusion), channel_id=1, source_target_pairs={{0,8},{4,12},{8,0},{12,4},{16,24},{20,28},{24,16},{28,20},{1,9},{5... | collective-permute-start | bytes 1327112 | tf_op jit(solution)/shard_map/ppermute | solution.py:102
  128.3 27.2 %collective-permute-start.37 = (bf16[1,4,24,2304]{3,2,1,0:T(8,128)(2,1)}, bf16[1,4,24,2304]{3,2,1,0:T(8,128)(2,1)}, u32[]{:S(2)}, u32[]{:S(2)}) collective-permute-start(bf16[1,4,24,2304]{3,2,1,0:T(8,128)(2,1)} %maximum_bitcast_fusion.1), channel_id=1, source_target_pairs={{0,16},{4,20},{8,24},{12,28},{16,0},{20,4},{24,8},{28,12},{1,17},{... | collective-permute-start | bytes 1327112 | tf_op jit(solution)/shard_map/ppermute | solution.py:102
  158.0 20.5 %collective-permute-start.38 = (bf16[2,4,24,2304]{3,2,1,0:T(8,128)(2,1)S(1)}, bf16[2,4,24,2304]{3,2,1,0:T(8,128)(2,1)S(1)}, u32[]{:S(2)}, u32[]{:S(2)}) collective-permute-start(bf16[2,4,24,2304]{3,2,1,0:T(8,128)(2,1)S(1)} %pad_maximum_fusion.3.refs_0_), channel_id=1, source_target_pairs={{0,16},{4,20},{8,24},{12,28},{16,0},{20,4},{24,8},{28,12},{1,17},{... | collective-permute-start | bytes 2654216 | tf_op jit(solution)/shard_map/ppermute | solution.py:102
  160.7 37.6 %collective-permute-start.39 = (bf16[2,4,24,2304]{3,2,1,0:T(8,128)(2,1)}, bf16[2,4,24,2304]{3,2,1,0:T(8,128)(2,1)}, u32[]{:S(2)}, u32[]{:S(2)}) collective-permute-start(bf16[2,4,24,2304]{3,2,1,0:T(8,128)(2,1)} %pad_maximum_fusion.4.refs_4_), channel_id=1, source_target_pairs={{0,8},{4,12},{8,0},{12,4},{16,24},{20,28},{24,16},{28,20},{1,9},{5... | collective-permute-start | bytes 2654216 | tf_op jit(solution)/shard_map/ppermute | solution.py:102
  165.4 33.5 %collective-permute-start.29 = (bf16[2,4,24,1920]{3,2,1,0:T(8,128)(2,1)}, bf16[2,4,24,1920]{3,2,1,0:T(8,128)(2,1)}, u32[]{:S(2)}, u32[]{:S(2)}) collective-permute-start(bf16[2,4,24,1920]{3,2,1,0:T(8,128)(2,1)} %pad_maximum_fusion.5.refs_0_), channel_id=1, source_target_pairs={{0,4},{4,0},{8,12},{12,8},{16,20},{20,16},{24,28},{28,24},{1,5},{5... | collective-permute-start | bytes 2211848 | tf_op jit(solution)/shard_map/ppermute | solution.py:102
  165.4 33.5 %collective-permute-start.30 = (bf16[2,4,24,1920]{3,2,1,0:T(8,128)(2,1)}, bf16[2,4,24,1920]{3,2,1,0:T(8,128)(2,1)}, u32[]{:S(2)}, u32[]{:S(2)}) collective-permute-start(bf16[2,4,24,1920]{3,2,1,0:T(8,128)(2,1)} %collective-permute-done.27.refs_1_), channel_id=1, source_target_pairs={{0,4},{4,0},{8,12},{12,8},{16,20},{20,16},{24,28},{28,24},{1,5},{5... | collective-permute-start | bytes 2211848 | tf_op jit(solution)/shard_map/ppermute | solution.py:102
  165.9 33.5 %collective-permute-start.31 = (bf16[2,4,24,1920]{3,2,1,0:T(8,128)(2,1)}, bf16[2,4,24,1920]{3,2,1,0:T(8,128)(2,1)}, u32[]{:S(2)}, u32[]{:S(2)}) collective-permute-start(bf16[2,4,24,1920]{3,2,1,0:T(8,128)(2,1)} %pad_maximum_fusion.6.refs_4_), channel_id=1, source_target_pairs={{0,4},{4,0},{8,12},{12,8},{16,20},{20,16},{24,28},{28,24},{1,5},{5... | collective-permute-start | bytes 2211848 | tf_op jit(solution)/shard_map/ppermute | solution.py:102
  179.4 20.1 %collective-permute-start.32 = (bf16[2,4,24,1920]{3,2,1,0:T(8,128)(2,1)}, bf16[2,4,24,1920]{3,2,1,0:T(8,128)(2,1)}, u32[]{:S(2)}, u32[]{:S(2)}) collective-permute-start(bf16[2,4,24,1920]{3,2,1,0:T(8,128)(2,1)} %collective-permute-done.28.refs_5_), channel_id=1, source_target_pairs={{0,4},{4,0},{8,12},{12,8},{16,20},{20,16},{24,28},{28,24},{1,5},{5... | collective-permute-start | bytes 2211848 | tf_op jit(solution)/shard_map/ppermute | solution.py:102
  198.3 16.8 %collective-permute-start.40 = (bf16[2,4,24,2304]{3,2,1,0:T(8,128)(2,1)S(1)}, bf16[2,4,24,2304]{3,2,1,0:T(8,128)(2,1)S(1)}, u32[]{:S(2)}, u32[]{:S(2)}) collective-permute-start(bf16[2,4,24,2304]{3,2,1,0:T(8,128)(2,1)S(1)} %copy-done.10), channel_id=1, source_target_pairs={{0,4},{4,0},{8,12},{12,8},{16,20},{20,16},{24,28},{28,24},{1,5},{5... | collective-permute-start | bytes 2654216 | tf_op jit(solution)/shard_map/ppermute | solution.py:102
  198.9 16.2 %collective-permute-start.41 = (bf16[2,4,24,2304]{3,2,1,0:T(8,128)(2,1)S(1)}, bf16[2,4,24,2304]{3,2,1,0:T(8,128)(2,1)S(1)}, u32[]{:S(2)}, u32[]{:S(2)}) collective-permute-start(bf16[2,4,24,2304]{3,2,1,0:T(8,128)(2,1)S(1)} %copy-done.16), channel_id=1, source_target_pairs={{0,4},{4,0},{8,12},{12,8},{16,20},{20,16},{24,28},{28,24},{1,5},{5... | collective-permute-start | bytes 2654216 | tf_op jit(solution)/shard_map/ppermute | solution.py:102
  199.0 16.1 %collective-permute-start.42 = (bf16[2,4,24,2304]{3,2,1,0:T(8,128)(2,1)}, bf16[2,4,24,2304]{3,2,1,0:T(8,128)(2,1)S(1)}, u32[]{:S(2)}, u32[]{:S(2)}) collective-permute-start(bf16[2,4,24,2304]{3,2,1,0:T(8,128)(2,1)} %pad_maximum_fusion.4.refs_4_), channel_id=1, source_target_pairs={{0,4},{4,0},{8,12},{12,8},{16,20},{20,16},{24,28},{28,24},{1,5},{5... | collective-permute-start | bytes 2654216 | tf_op jit(solution)/shard_map/ppermute | solution.py:102
  199.4 15.7 %collective-permute-start.43 = (bf16[2,4,24,2304]{3,2,1,0:T(8,128)(2,1)}, bf16[2,4,24,2304]{3,2,1,0:T(8,128)(2,1)S(1)}, u32[]{:S(2)}, u32[]{:S(2)}) collective-permute-start(bf16[2,4,24,2304]{3,2,1,0:T(8,128)(2,1)} %collective-permute-done.39.refs_5_), channel_id=1, source_target_pairs={{0,4},{4,0},{8,12},{12,8},{16,20},{20,16},{24,28},{28,24},{1,5},{5... | collective-permute-start | bytes 2654216 | tf_op jit(solution)/shard_map/ppermute | solution.py:102
  230.8 15.6 %collective-permute-start.45 = (bf16[112,768]{1,0:T(8,128)(2,1)S(1)}, bf16[112,768]{1,0:T(8,128)(2,1)S(1)}, u32[]{:S(2)}, u32[]{:S(2)}) collective-permute-start(bf16[112,768]{1,0:T(8,128)(2,1)S(1)} %add_convert_fusion.2), channel_id=1, source_target_pairs={{0,2},{1,3},{2,0},{3,1},{4,6},{5,7},{6,4},{7,5},{8,10},{9,11},{10,... | collective-permute-start | bytes 516104 | tf_op jit(solution)/shard_map/ppermute | solution.py:153
  258.0 15.9 %collective-permute-start.49 = (bf16[2,4,112,384]{3,2,1,0:T(8,128)(2,1)}, bf16[2,4,112,384]{3,2,1,0:T(8,128)(2,1)}, u32[]{:S(2)}, u32[]{:S(2)}) collective-permute-start(bf16[2,4,112,384]{3,2,1,0:T(8,128)(2,1)} %pad_maximum_fusion.7.refs_0_), channel_id=1, source_target_pairs={{0,16},{4,20},{8,24},{12,28},{16,0},{20,4},{24,8},{28,12},{1,17},{... | collective-permute-start | bytes 2064392 | tf_op jit(solution)/shard_map/ppermute | solution.py:102
  258.5 15.6 %collective-permute-start.52 = (bf16[2,4,112,384]{3,2,1,0:T(8,128)(2,1)}, bf16[2,4,112,384]{3,2,1,0:T(8,128)(2,1)}, u32[]{:S(2)}, u32[]{:S(2)}) collective-permute-start(bf16[2,4,112,384]{3,2,1,0:T(8,128)(2,1)} %pad_maximum_fusion.8.refs_4_), channel_id=1, source_target_pairs={{0,8},{4,12},{8,0},{12,4},{16,24},{20,28},{24,16},{28,20},{1,9},{5... | collective-permute-start | bytes 2064392 | tf_op jit(solution)/shard_map/ppermute | solution.py:102
  259.7 19.2 %collective-permute-start.50 = (bf16[2,4,112,384]{3,2,1,0:T(8,128)(2,1)}, bf16[2,4,112,384]{3,2,1,0:T(8,128)(2,1)}, u32[]{:S(2)}, u32[]{:S(2)}) collective-permute-start(bf16[2,4,112,384]{3,2,1,0:T(8,128)(2,1)} %pad_maximum_fusion.7.refs_0_), channel_id=1, source_target_pairs={{0,4},{4,0},{8,12},{12,8},{16,20},{20,16},{24,28},{28,24},{1,5},{5... | collective-permute-start | bytes 2064392 | tf_op jit(solution)/shard_map/ppermute | solution.py:102
  259.8 19.2 %collective-permute-start.53 = (bf16[2,4,112,384]{3,2,1,0:T(8,128)(2,1)}, bf16[2,4,112,384]{3,2,1,0:T(8,128)(2,1)}, u32[]{:S(2)}, u32[]{:S(2)}) collective-permute-start(bf16[2,4,112,384]{3,2,1,0:T(8,128)(2,1)} %pad_maximum_fusion.8.refs_4_), channel_id=1, source_target_pairs={{0,4},{4,0},{8,12},{12,8},{16,20},{20,16},{24,28},{28,24},{1,5},{5... | collective-permute-start | bytes 2064392 | tf_op jit(solution)/shard_map/ppermute | solution.py:102
  294.0 21.1 %all-to-all-start.1 = ((f32[32,28,128]{2,1,0:T(8,128)}), f32[32,28,128]{2,1,0:T(8,128)}, u32[]{:S(2)}, u32[]{:S(2)}) async-start(f32[32,28,128]{2,1,0:T(8,128)} %broadcast_in_dim.235), calls=%async_computation.2 | async-start | bytes 1048576 | tf_op jit(solution)/shard_map/all_to_all | solution.py:355
  341.1 18.1 %collective-permute-start.59 = (bf16[2,4,112,384]{3,2,1,0:T(8,128)(2,1)}, bf16[2,4,112,384]{3,2,1,0:T(8,128)(2,1)}, u32[]{:S(2)}, u32[]{:S(2)}) collective-permute-start(bf16[2,4,112,384]{3,2,1,0:T(8,128)(2,1)} %fusion.48), channel_id=1, source_target_pairs={{0,8},{4,12},{8,0},{12,4},{16,24},{20,28},{24,16},{28,20},{1,9},{5... | collective-permute-start | bytes 2064392 | tf_op jit(solution)/shard_map/ppermute | solution.py:102
  344.0 18.4 %collective-permute-start.56 = (bf16[2,4,112,384]{3,2,1,0:T(8,128)(2,1)}, bf16[2,4,112,384]{3,2,1,0:T(8,128)(2,1)}, u32[]{:S(2)}, u32[]{:S(2)}) collective-permute-start(bf16[2,4,112,384]{3,2,1,0:T(8,128)(2,1)} %fusion.49), channel_id=1, source_target_pairs={{0,16},{4,20},{8,24},{12,28},{16,0},{20,4},{24,8},{28,12},{1,17},{... | collective-permute-start | bytes 2064392 | tf_op jit(solution)/shard_map/ppermute | solution.py:102
  354.0 28.0 %all-to-all-start.2 = ((f32[32,8,128]{2,1,0:T(8,128)}), f32[32,8,128]{2,1,0:T(8,128)}, u32[]{:S(2)}, u32[]{:S(2)}) async-start(f32[32,8,128]{2,1,0:T(8,128)} %broadcast_in_dim.237), calls=%async_computation.3 | async-start | bytes 262144 | tf_op jit(solution)/shard_map/all_to_all | solution.py:355
  377.0 15.3 %collective-permute-start.62 = (bf16[112,768]{1,0:T(8,128)(2,1)}, bf16[112,768]{1,0:T(8,128)(2,1)}, u32[]{:S(2)}, u32[]{:S(2)}) collective-permute-start(bf16[112,768]{1,0:T(8,128)(2,1)} %get-tuple-element.540), channel_id=1, source_target_pairs={{0,2},{1,3},{2,0},{3,1},{4,6},{5,7},{6,4},{7,5},{8,10},{9,11},{10,... | collective-permute-start | bytes 516104 | tf_op jit(solution)/shard_map/ppermute | solution.py:153
  427.7 23.9 %collective-permute-start.64 = (bf16[2,2,4,24,3072]{4,3,2,1,0:T(8,128)(2,1)}, bf16[2,2,4,24,3072]{4,3,2,1,0:T(8,128)(2,1)}, u32[]{:S(2)}, u32[]{:S(2)}) collective-permute-start(bf16[2,2,4,24,3072]{4,3,2,1,0:T(8,128)(2,1)} %fusion.35), channel_id=1, source_target_pairs={{0,4},{4,0},{8,12},{12,8},{16,20},{20,16},{24,28},{28,24},{1,5},{5... | collective-permute-start | bytes 7077896 | tf_op jit(solution)/shard_map/ppermute | solution.py:102
  441.0 14.1 %collective-permute-start.66 = (bf16[2,2,4,24,3072]{4,3,2,1,0:T(8,128)(2,1)}, bf16[2,2,4,24,3072]{4,3,2,1,0:T(8,128)(2,1)}, u32[]{:S(2)}, u32[]{:S(2)}) collective-permute-start(bf16[2,2,4,24,3072]{4,3,2,1,0:T(8,128)(2,1)} %fusion.36), channel_id=1, source_target_pairs={{0,4},{4,0},{8,12},{12,8},{16,20},{20,16},{24,28},{28,24},{1,5},{5... | collective-permute-start | bytes 7077896 | tf_op jit(solution)/shard_map/ppermute | solution.py:102
  453.9 32.4 %collective-permute-start.68 = (bf16[2,4,24,3072]{3,2,1,0:T(8,128)(2,1)S(1)}, bf16[2,4,24,3072]{3,2,1,0:T(8,128)(2,1)S(1)}, u32[]{:S(2)}, u32[]{:S(2)}) collective-permute-start(bf16[2,4,24,3072]{3,2,1,0:T(8,128)(2,1)S(1)} %fusion.38), channel_id=1, source_target_pairs={{0,16},{4,20},{8,24},{12,28},{16,0},{20,4},{24,8},{28,12},{1,17},{... | collective-permute-start | bytes 3538952 | tf_op jit(solution)/shard_map/ppermute | solution.py:102
  457.4 32.9 %collective-permute-start.70 = (bf16[2,4,24,3072]{3,2,1,0:T(8,128)(2,1)S(1)}, bf16[2,4,24,3072]{3,2,1,0:T(8,128)(2,1)S(1)}, u32[]{:S(2)}, u32[]{:S(2)}) collective-permute-start(bf16[2,4,24,3072]{3,2,1,0:T(8,128)(2,1)S(1)} %fusion.37), channel_id=1, source_target_pairs={{0,8},{4,12},{8,0},{12,4},{16,24},{20,28},{24,16},{28,20},{1,9},{5... | collective-permute-start | bytes 3538952 | tf_op jit(solution)/shard_map/ppermute | solution.py:102
  499.5 27.1 %collective-permute-start.76 = (bf16[2,2,4,24,1536]{4,3,2,1,0:T(8,128)(2,1)}, bf16[2,2,4,24,1536]{4,3,2,1,0:T(8,128)(2,1)}, u32[]{:S(2)}, u32[]{:S(2)}) collective-permute-start(bf16[2,2,4,24,1536]{4,3,2,1,0:T(8,128)(2,1)} %fusion.50), channel_id=1, source_target_pairs={{0,4},{4,0},{8,12},{12,8},{16,20},{20,16},{24,28},{28,24},{1,5},{5... | collective-permute-start | bytes 3538952 | tf_op jit(solution)/shard_map/ppermute | solution.py:102
  499.6 19.2 %collective-permute-start.77 = (bf16[2,2,4,24,768]{4,3,2,1,0:T(8,128)(2,1)}, bf16[2,2,4,24,768]{4,3,2,1,0:T(8,128)(2,1)S(1)}, u32[]{:S(2)}, u32[]{:S(2)}) collective-permute-start(bf16[2,2,4,24,768]{4,3,2,1,0:T(8,128)(2,1)} %fusion.82), channel_id=1, source_target_pairs={{0,4},{4,0},{8,12},{12,8},{16,20},{20,16},{24,28},{28,24},{1,5},{5... | collective-permute-start | bytes 1769480 | tf_op jit(solution)/shard_map/ppermute | solution.py:102
  502.8 17.2 %collective-permute-start.78 = (bf16[2,2,4,24,768]{4,3,2,1,0:T(8,128)(2,1)}, bf16[2,2,4,24,768]{4,3,2,1,0:T(8,128)(2,1)}, u32[]{:S(2)}, u32[]{:S(2)}) collective-permute-start(bf16[2,2,4,24,768]{4,3,2,1,0:T(8,128)(2,1)} %fusion.83), channel_id=1, source_target_pairs={{0,4},{4,0},{8,12},{12,8},{16,20},{20,16},{24,28},{28,24},{1,5},{5... | collective-permute-start | bytes 1769480 | tf_op jit(solution)/shard_map/ppermute | solution.py:102
  503.0 23.6 %collective-permute-start.72 = (bf16[4,24,3072]{2,1,0:T(8,128)(2,1)}, bf16[4,24,3072]{2,1,0:T(8,128)(2,1)}, u32[]{:S(2)}, u32[]{:S(2)}) collective-permute-start(bf16[4,24,3072]{2,1,0:T(8,128)(2,1)} %fusion.61), channel_id=1, source_target_pairs={{0,8},{4,12},{8,0},{12,4},{16,24},{20,28},{24,16},{28,20},{1,9},{5... | collective-permute-start | bytes 1769480 | tf_op jit(solution)/shard_map/ppermute | solution.py:102
  504.3 22.3 %collective-permute-start.74 = (bf16[4,24,3072]{2,1,0:T(8,128)(2,1)}, bf16[4,24,3072]{2,1,0:T(8,128)(2,1)}, u32[]{:S(2)}, u32[]{:S(2)}) collective-permute-start(bf16[4,24,3072]{2,1,0:T(8,128)(2,1)} %fusion.60), channel_id=1, source_target_pairs={{0,16},{4,20},{8,24},{12,28},{16,0},{20,4},{24,8},{28,12},{1,17},{... | collective-permute-start | bytes 1769480 | tf_op jit(solution)/shard_map/ppermute | solution.py:102
  524.6 26.0 %collective-permute-start.83 = (bf16[2,4,24,768]{3,2,1,0:T(8,128)(2,1)}, bf16[2,4,24,768]{3,2,1,0:T(8,128)(2,1)}, u32[]{:S(2)}, u32[]{:S(2)}) collective-permute-start(bf16[2,4,24,768]{3,2,1,0:T(8,128)(2,1)} %fusion.91), channel_id=1, source_target_pairs={{0,8},{4,12},{8,0},{12,4},{16,24},{20,28},{24,16},{28,20},{1,9},{5... | collective-permute-start | bytes 884744 | tf_op jit(solution)/shard_map/ppermute | solution.py:102
  525.9 24.8 %collective-permute-start.84 = (bf16[2,4,24,768]{3,2,1,0:T(8,128)(2,1)}, bf16[2,4,24,768]{3,2,1,0:T(8,128)(2,1)}, u32[]{:S(2)}, u32[]{:S(2)}) collective-permute-start(bf16[2,4,24,768]{3,2,1,0:T(8,128)(2,1)} %fusion.90), channel_id=1, source_target_pairs={{0,8},{4,12},{8,0},{12,4},{16,24},{20,28},{24,16},{28,20},{1,9},{5... | collective-permute-start | bytes 884744 | tf_op jit(solution)/shard_map/ppermute | solution.py:102
  534.2 16.5 %collective-permute-start.82 = (bf16[2,4,24,1536]{3,2,1,0:T(8,128)(2,1)}, bf16[2,4,24,1536]{3,2,1,0:T(8,128)(2,1)}, u32[]{:S(2)}, u32[]{:S(2)}) collective-permute-start(bf16[2,4,24,1536]{3,2,1,0:T(8,128)(2,1)} %fusion.59), channel_id=1, source_target_pairs={{0,16},{4,20},{8,24},{12,28},{16,0},{20,4},{24,8},{28,12},{1,17},{... | collective-permute-start | bytes 1769480 | tf_op jit(solution)/shard_map/ppermute | solution.py:102
  535.6 21.8 %collective-permute-start.79 = (bf16[2,2,4,96,384]{4,3,2,1,0:T(8,128)(2,1)S(1)}, bf16[2,2,4,96,384]{4,3,2,1,0:T(8,128)(2,1)}, u32[]{:S(2)}, u32[]{:S(2)}) collective-permute-start(bf16[2,2,4,96,384]{4,3,2,1,0:T(8,128)(2,1)S(1)} %fusion.51), channel_id=1, source_target_pairs={{0,4},{4,0},{8,12},{12,8},{16,20},{20,16},{24,28},{28,24},{1,5},{5... | collective-permute-start | bytes 3538952 | tf_op jit(solution)/shard_map/ppermute | solution.py:102
  536.9 20.5 %collective-permute-start.80 = (bf16[2,2,4,96,384]{4,3,2,1,0:T(8,128)(2,1)}, bf16[2,2,4,96,384]{4,3,2,1,0:T(8,128)(2,1)}, u32[]{:S(2)}, u32[]{:S(2)}) collective-permute-start(bf16[2,2,4,96,384]{4,3,2,1,0:T(8,128)(2,1)} %fusion.52), channel_id=1, source_target_pairs={{0,4},{4,0},{8,12},{12,8},{16,20},{20,16},{24,28},{28,24},{1,5},{5... | collective-permute-start | bytes 3538952 | tf_op jit(solution)/shard_map/ppermute | solution.py:102
  545.6 58.0 %all-to-all-start.3 = ((bf16[4,24,7680]{2,1,0:T(8,128)(2,1)}), bf16[4,24,7680]{2,1,0:T(8,128)(2,1)S(1)}, u32[]{:S(2)}, u32[]{:S(2)}) async-start(bf16[4,24,7680]{2,1,0:T(8,128)(2,1)} %pad_maximum_fusion), calls=%async_computation.4 | async-start | bytes 2949120 | tf_op jit(solution)/shard_map/all_to_all | solution.py:157
  558.9 16.8 %collective-permute-start.85 = (bf16[2,4,96,384]{3,2,1,0:T(8,128)(2,1)S(1)}, bf16[2,4,96,384]{3,2,1,0:T(8,128)(2,1)S(1)}, u32[]{:S(2)}, u32[]{:S(2)}) collective-permute-start(bf16[2,4,96,384]{3,2,1,0:T(8,128)(2,1)S(1)} %fusion.54), channel_id=1, source_target_pairs={{0,16},{4,20},{8,24},{12,28},{16,0},{20,4},{24,8},{28,12},{1,17},{... | collective-permute-start | bytes 1769480 | tf_op jit(solution)/shard_map/ppermute | solution.py:102
  561.8 24.3 %collective-permute-start.87 = (bf16[2,4,96,384]{3,2,1,0:T(8,128)(2,1)S(1)}, bf16[2,4,96,384]{3,2,1,0:T(8,128)(2,1)S(1)}, u32[]{:S(2)}, u32[]{:S(2)}) collective-permute-start(bf16[2,4,96,384]{3,2,1,0:T(8,128)(2,1)S(1)} %fusion.53), channel_id=1, source_target_pairs={{0,8},{4,12},{8,0},{12,4},{16,24},{20,28},{24,16},{28,20},{1,9},{5... | collective-permute-start | bytes 1769480 | tf_op jit(solution)/shard_map/ppermute | solution.py:102
  562.6 20.2 %collective-permute-start.89 = (bf16[2,4,24,512]{3,2,1,0:T(8,128)(2,1)S(1)}, bf16[2,4,24,512]{3,2,1,0:T(8,128)(2,1)S(1)}, u32[]{:S(2)}, u32[]{:S(2)}) collective-permute-start(bf16[2,4,24,512]{3,2,1,0:T(8,128)(2,1)S(1)} %fusion.100), channel_id=1, source_target_pairs={{0,8},{4,12},{8,0},{12,4},{16,24},{20,28},{24,16},{28,20},{1,9},{5... | collective-permute-start | bytes 589832 | tf_op jit(solution)/shard_map/ppermute | solution.py:102
  578.3 22.8 %collective-permute-start.97 = (bf16[24,3072]{1,0:T(8,128)(2,1)S(1)}, bf16[24,3072]{1,0:T(8,128)(2,1)S(1)}, u32[]{:S(2)}, u32[]{:S(2)}) collective-permute-start(bf16[24,3072]{1,0:T(8,128)(2,1)S(1)} %get-tuple-element.544), channel_id=1, source_target_pairs={{0,1},{1,0},{2,3},{3,2},{4,5},{5,4},{6,7},{7,6},{8,9},{9,8},{10,11... | collective-permute-start | bytes 442376 | tf_op jit(solution)/shard_map/ppermute | solution.py:153
  580.4 21.7 %collective-permute-start.98 = (bf16[24,3072]{1,0:T(8,128)(2,1)S(1)}, bf16[24,3072]{1,0:T(8,128)(2,1)S(1)}, u32[]{:S(2)}, u32[]{:S(2)}) collective-permute-start(bf16[24,3072]{1,0:T(8,128)(2,1)S(1)} %get-tuple-element.543), channel_id=1, source_target_pairs={{0,2},{1,3},{2,0},{3,1},{4,6},{5,7},{6,4},{7,5},{8,10},{9,11},{10,... | collective-permute-start | bytes 442376 | tf_op jit(solution)/shard_map/ppermute | solution.py:153
  582.8 19.3 %collective-permute-start.99 = (bf16[24,3072]{1,0:T(8,128)(2,1)S(1)}, bf16[24,3072]{1,0:T(8,128)(2,1)S(1)}, u32[]{:S(2)}, u32[]{:S(2)}) collective-permute-start(bf16[24,3072]{1,0:T(8,128)(2,1)S(1)} %get-tuple-element.542), channel_id=1, source_target_pairs={{0,3},{1,2},{2,1},{3,0},{4,7},{5,6},{6,5},{7,4},{8,11},{9,10},{10,... | collective-permute-start | bytes 442376 | tf_op jit(solution)/shard_map/ppermute | solution.py:153
  599.1 13.9 %collective-permute-start.92 = (bf16[24,3584]{1,0:T(8,128)(2,1)}, bf16[24,3584]{1,0:T(8,128)(2,1)}, u32[]{:S(2)}, u32[]{:S(2)}) collective-permute-start(bf16[24,3584]{1,0:T(8,128)(2,1)} %get-tuple-element.537), channel_id=1, source_target_pairs={{0,2},{1,3},{2,0},{3,1},{4,6},{5,7},{6,4},{7,5},{8,10},{9,11},{10,... | collective-permute-start | bytes 516104 | tf_op jit(solution)/shard_map/ppermute | solution.py:153
  639.1 18.3 %all-to-all-start.5 = ((f32[32,4,128]{2,1,0:T(4,128)}), f32[32,4,128]{2,1,0:T(4,128)S(1)}, u32[]{:S(2)}, u32[]{:S(2)}) async-start(f32[32,4,128]{2,1,0:T(4,128)} %broadcast_in_dim.250), calls=%async_computation.6 | async-start | bytes 131072 | tf_op jit(solution)/shard_map/all_to_all | solution.py:355
  (201 other events, 1437.4 us)

commit v4 on v3

--- a/solution.py
+++ b/solution.py
@@ -1165,7 +1165,8 @@
     sent = last_sum.line()
     sum_feed_in, sum_dense, sum_feed_out, sum_pooler = feed_sum.finish_whole()
     sum_mixed, sum_value, sum_output = in_sum.finish(sent)
-    words_left, words_right, sum_small = last_sum.finish()
+    vocab_flat = pin(all_vocab, sent).reshape(devices, -1)[:, :vocab_rows].reshape(-1)
+    words_left, words_right, sum_small = last_sum.finish(vocab_flat)
 
     def return_more(state):
         turn, grad_table, table_square = state
@@ -1216,7 +1217,7 @@
             all_vector.reshape(devices, -1)[:, :vector_flat]
             .reshape(devices * depth, vector_count)
             .T.reshape(-1),
-            all_vocab.reshape(devices, -1)[:, :vocab_rows].reshape(-1),
+            vocab_flat,
         ]
     )
     totals, grad_table = lax.optimization_barrier((totals, grad_table))

time: 678 us -> 676 us (level)
    unnamed x334 -> x332, local copies, waits for them, and re-layouts: 19.8 us -> 21.6 us
  transfers between devices with their start and end apart: 106 -> 106, of which waited for: 27 -> 28; matrix products, arithmetic and copies ran while one was open for 30% -> 30% of each run, Pallas kernels for 9% -> 9%
where the time goes in v4:
time: 676 us; the launch traced here: 664 us
  other arithmetic  136 us (20%)
  starting transfers between devices  129 us (19%)
  waiting for transfers between devices  128 us (19%)
  matrix products  94.7 us (14%)
  Pallas kernels  89.2 us (13%)
  local copies, waits for them, and re-layouts  63.6 us (9%)
  between operations  23.3 us (3%)
    ppermute x76, waiting for transfers between devices, swap(): lax.ppermute(values, dim[0], [(i, i ^ 1 << dim[1]) for i in range(size)])  91.5 us
    ppermute x76, starting transfers between devices, swap(): lax.ppermute(values, dim[0], [(i, i ^ 1 << dim[1]) for i in range(size)])  55.1 us
    ppermute x24, starting transfers between devices, reach(): return lax.ppermute(values, 'narrow', [(z, z ^ step) for z in range(size)])  43 us
    dot_general x13, matrix products, product_left(): lax.dot_general(left, right, (((0,), (0,)), ((), ())), preferred_element_...  38.3 us
    convert_element_type x24, other arithmetic, send(): self.away.append(self.cut(number, fixed).astype(jnp.bfloat16))  35.1 us
    dot_general x13, matrix products, product(): return jnp.dot(left, right, preferred_element_type=jnp.float32)  31.6 us
    ppermute x24, waiting for transfers between devices, reach(): return lax.ppermute(values, 'narrow', [(z, z ^ step) for z in range(size)])  28 us
    pallas_call x1, Pallas kernels, attend_back(): pl.pallas_call(attend_back_kernel, grid_spec=pltpu.PrefetchScalarGridSpec...  22.5 us
  transfers between devices with their start and end apart: 106, of which 28 were waited for; matrix products, arithmetic and copies ran while one was open for 30% of the time, Pallas kernels for 9%

profile of v4, /device:TPU:0, one launch (start us, length us, event | category | flops | bytes accessed | tf_op | source)
XLA Modules:
  0.0 664.2 jit_solution(7185554785510264206)
XLA Ops:
  11.3 7.3 %all-to-all-start = ((s32[32,16,128]{2,1,0:T(8,128)}), s32[32,16,128]{2,1,0:T(8,128)S(1)}, u32[]{:S(2)}, u32[]{:S(2)}) async-start(s32[32,16,128]{2,1,0:T(8,128)} %broadcast_in_dim.129), calls=%async_computation.1 | async-start | bytes 524288 | tf_op jit(solution)/shard_map/all_to_all | solution.py:855
  24.0 2.4 collective-permute-start.8
  35.6 4.9 convert_reduce_fusion.5
  42.4 3.3 collective-permute-start.1
  64.0 13.6 %collective-permute-done.3 = bf16[1,4,96,384]{3,2,1,0:T(8,128)(2,1)S(1)} collective-permute-done((bf16[1,4,96,384]{3,2,1,0:T(8,128)(2,1)S(1)}, bf16[1,4,96,384]{3,2,1,0:T(8,128)(2,1)S(1)}, u32[]{:S(2)}, u32[]{:S(2)}) %collective-permute-start.3) | collective-permute-done | bytes 294944 | tf_op jit(solution)/shard_map/ppermute | solution.py:102
  79.8 5.1 collective-permute-start.22
  84.9 2.4 collective-permute-start.24
  96.4 4.2 collective-permute-start.33
  101.7 2.4 collective-permute-start.35
  130.6 5.6 fusion.29
  137.0 2.3 fusion.44
  140.1 14.1 %collective-permute-done.36 = bf16[1,4,24,2304]{3,2,1,0:T(8,128)(2,1)} collective-permute-done((bf16[1,4,24,2304]{3,2,1,0:T(8,128)(2,1)}, bf16[1,4,24,2304]{3,2,1,0:T(8,128)(2,1)}, u32[]{:S(2)}, u32[]{:S(2)}) %collective-permute-start.36) | collective-permute-done | bytes 442400 | tf_op jit(solution)/shard_map/ppermute | solution.py:102
  155.5 2.5 pad_maximum_fusion.4.refs_4_
  162.2 3.1 add_convert_fusion.query_ref.key_ref.value_ref
  166.0 12.5 %collective-permute-done.38.refs_1_ = bf16[2,4,24,2304]{3,2,1,0:T(8,128)(2,1)S(1)} collective-permute-done((bf16[2,4,24,2304]{3,2,1,0:T(8,128)(2,1)S(1)}, bf16[2,4,24,2304]{3,2,1,0:T(8,128)(2,1)S(1)}, u32[]{:S(2)}, u32[]{:S(2)}) %collective-permute-start.38) | collective-permute-done | bytes 884768 | tf_op jit(solution)/shard_map/ppermute | solution.py:102
  183.2 15.0 %shard_map.487 = bf16[768,768]{1,0:T(8,128)(2,1)S(1)} custom-call(s32[2]{0:T(128)S(1)} %bitcast.688, bf16[768,2304]{1,0:T(8,128)(2,1)S(1)} %add_convert_fusion.query_ref.key_ref.value_ref, bf16[768,2304]{1,0:T(8,128)(2,1)S(1)} %add_convert_fusion.query_ref.key_ref.value_ref, bf16[768,2304]{1,0:T(8,128)(2,1)S(1)} %add_convert_fusion.query_ref.key_ref.value_ref), custom_call_target="tpu_custom_call" | custom-call | flops 1811939328 | bytes 4718592 | tf_op jit(solution)/shard_map/pallas_call | solution.py:763
  199.5 3.2 shard_map.488
  205.2 9.9 %fusion.26 = (f32[768,3072]{1,0:T(8,128)}, bf16[768,3072]{1,0:T(8,128)(2,1)}) fusion(f32[3072]{0:T(1024)S(1)} %slice.507, bf16[768,3072]{1,0:T(8,128)(2,1)S(1)} %bitcast.631, f32[768,768]{1,0:T(8,128)S(1)} %subtract_multiply_fusion.1.normal_one_ref, f32[768]{0:T(1024)S(1)} %copy-done.82, f32[768]{0:T(1024)S(1)} %get-tuple-element.612), kind=kOutput, calls=%fused_computation.46 | convolution fusion | flops 3651600384 | bytes 21252096 | tf_op jit(solution)/shard_map/dot_general | solution.py:30
  215.1 4.3 shard_map.489
  219.4 7.9 %fusion.186 = (f32[768]{0:T(1024)S(1)}, f32[768,768]{1,0:T(8,128)S(1)}) fusion(f32[768]{0:T(1024)S(1)} %copy-done.141, bf16[768,3072]{1,0:T(8,128)(2,1)} %get-tuple-element.309, bf16[768,3072]{1,0:T(8,128)(2,1)S(1)} %bitcast.633, f32[768]{0:T(1024)S(1)} %copy-done.82, f32[768,768]{1,0:T(8,128)S(1)} %subtract_multiply_fusion.1.normal_one_ref, ...), kind=kOutput, calls=%fused_computation.526 | convolution fusion | flops 3626827008 | bytes 14168064 | tf_op jit(solution)/shard_map/dot_general | solution.py:34
  232.8 2.4 collective-permute-start.46
  235.1 4.8 collective-permute-done.44
  239.9 6.4 collective-permute-done.45
  249.1 6.9 %collective-permute-done.47 = bf16[1,4,112,384]{3,2,1,0:T(8,128)(2,1)S(1)} collective-permute-done((bf16[1,4,112,384]{3,2,1,0:T(8,128)(2,1)S(1)}, bf16[1,4,112,384]{3,2,1,0:T(8,128)(2,1)S(1)}, u32[]{:S(2)}, u32[]{:S(2)}) %collective-permute-start.47) | collective-permute-done | bytes 344096 | tf_op jit(solution)/shard_map/ppermute | solution.py:102
  260.2 13.6 %collective-permute-done.49.refs_1_ = bf16[2,4,112,384]{3,2,1,0:T(8,128)(2,1)} collective-permute-done((bf16[2,4,112,384]{3,2,1,0:T(8,128)(2,1)}, bf16[2,4,112,384]{3,2,1,0:T(8,128)(2,1)}, u32[]{:S(2)}, u32[]{:S(2)}) %collective-permute-start.49) | collective-permute-done | bytes 688160 | tf_op jit(solution)/shard_map/ppermute | solution.py:102
  279.0 3.0 shard_map.490
  282.0 5.5 add_reduce_fusion
  287.6 5.5 fusion.21
  294.0 6.7 %all-to-all-start.1 = ((f32[32,28,128]{2,1,0:T(8,128)}), f32[32,28,128]{2,1,0:T(8,128)}, u32[]{:S(2)}, u32[]{:S(2)}) async-start(f32[32,28,128]{2,1,0:T(8,128)} %broadcast_in_dim.235), calls=%async_computation.2 | async-start | bytes 1048576 | tf_op jit(solution)/shard_map/all_to_all | solution.py:355
  310.7 4.4 all-to-all-done.1
  318.6 8.7 %convert_reduce_fusion.1 = (f32[956]{0:T(1024)S(1)}, bf16[3584,956]{0,1:T(8,128)(2,1)S(1)}) fusion(f32[3584]{0:T(1024)} %broadcast_multiply_fusion, s32[3584]{0:T(1024)} %eq.107, s32[956]{0:T(1024)} %iota_add_fusion, f32[3584]{0:T(1024)S(1)} %add_bitcast_fusion, f32[3584,956]{0,1:T(8,128)} %copy-done.27, f32[956]{0:T(1024)} %copy-done.109), kind=kLoop, calls=%fused_computation.38 | loop fusion | flops 30835780 | bytes 20612304 | tf_op jit(solution)/shard_map/reduce_sum | solution.py:1063
  327.4 4.0 fusion.71
  331.4 4.0 fusion.69
  344.5 8.2 %multiply_reduce_fusion = (f32[]{:T(128)}, f32[956,768]{1,0:T(8,128)}) fusion(bf16[3584,956]{0,1:T(8,128)(2,1)S(1)} %get-tuple-element.334, bf16[3584,768]{1,0:T(8,128)(2,1)S(1)} %bitcast.616), kind=kOutput, calls=%fused_computation.66 | convolution fusion | flops 5264271360 | bytes 15294468 | tf_op jit(solution)/shard_map/dot_general | solution.py:40
  353.9 3.4 all-to-all-start.2
  364.8 6.0 collective-permute-done.60
  376.9 2.4 collective-permute-start.62
  383.7 8.5 %collective-permute-done.62 = bf16[112,768]{1,0:T(8,128)(2,1)} collective-permute-done((bf16[112,768]{1,0:T(8,128)(2,1)}, bf16[112,768]{1,0:T(8,128)(2,1)}, u32[]{:S(2)}, u32[]{:S(2)}) %collective-permute-start.62) | collective-permute-done | bytes 172064 | tf_op jit(solution)/shard_map/ppermute | solution.py:153
  397.9 2.5 convolution_add_fusion.2.grad_ref
  400.4 19.5 %shard_map.491 = (bf16[768,768]{1,0:T(8,128)(2,1)}, bf16[768,3072]{1,0:T(8,128)(2,1)}, f32[768,768]{1,0:T(8,128)}, bf16[768,768]{1,0:T(8,128)(2,1)}, bf16[768,768]{1,0:T(8,128)(2,1)}, /*index=5*/f32[32,768]{1,0:T(8,128)}) custom-call(f32[768,768]{1,0:T(8,128)} %convolution_add_fusion.2.grad_ref, f32[768,768]{1,0:T(8,128)} %copy-done.32, ...), custom_call_target="tpu_custom_call" | custom-call | flops 8153726976 | bytes 37748736 | tf_op jit(solution)/shard_map/pallas_call | solution.py:470
  420.0 5.8 fusion.111
  427.9 7.7 %fusion.191 = f32[768,3072]{1,0:T(8,128)S(1)} fusion(bf16[768,768]{1,0:T(8,128)(2,1)S(1)} %copy-done.62, bf16[768,3072]{1,0:T(8,128)(2,1)} %get-tuple-element.309), kind=kOutput, calls=%fused_computation.531 | convolution fusion | flops 3623878656 | bytes 15335424 | tf_op jit(solution)/shard_map/dot_general | solution.py:40
  435.6 3.6 copy-done.30
  451.5 2.2 fusion.38
  455.1 2.2 fusion.37
  462.8 22.5 %shard_map.492.mixed_ref = bf16[768,2304]{1,0:T(8,128)(2,1)S(1)} custom-call(s32[2]{0:T(128)S(1)} %bitcast.689, bf16[768,2304]{1,0:T(8,128)(2,1)S(1)} %add_convert_fusion.query_ref.key_ref.value_ref, bf16[768,2304]{1,0:T(8,128)(2,1)S(1)} %add_convert_fusion.query_ref.key_ref.value_ref, bf16[768,2304]{1,0:T(8,128)(2,1)S(1)} %add_convert_fusion.query_ref.key_ref.value_ref, ...), custom_call_target="tpu_custom_call" | custom-call | flops 4529848320 | bytes 8257536 | tf_op jit(solution)/shard_map/pallas_call | solution.py:786
  485.3 4.0 fusion.61
  490.4 2.4 fusion.60
  504.0 10.6 %shard_map.493 = (bf16[768,768]{1,0:T(8,128)(2,1)}, f32[768,512]{1,0:T(8,128)S(1)}) custom-call(s32[2]{0:T(128)S(1)} %bitcast.690, bf16[768,2304]{1,0:T(8,128)(2,1)} %copy-done.8, bf16[768,2304]{1,0:T(8,128)(2,1)} %bitcast.622, f32[768,768]{1,0:T(8,128)S(1)} %copy-done.11, f32[768,768]{1,0:T(8,128)} %get-tuple-element.531.normal_ref, ...), custom_call_target="tpu_custom_call" | custom-call | flops 2717908992 | bytes 12976128 | tf_op jit(solution)/shard_map/pallas_call | solution.py:598
  524.5 2.6 fusion.28
  527.1 2.6 fusion.27
  540.9 4.8 all-to-all-start.3
  563.0 8.1 %collective-permute-done.85 = bf16[2,4,96,384]{3,2,1,0:T(8,128)(2,1)S(1)} collective-permute-done((bf16[2,4,96,384]{3,2,1,0:T(8,128)(2,1)S(1)}, bf16[2,4,96,384]{3,2,1,0:T(8,128)(2,1)S(1)}, u32[]{:S(2)}, u32[]{:S(2)}) %collective-permute-start.85) | collective-permute-done | bytes 589856 | tf_op jit(solution)/shard_map/ppermute | solution.py:102
  576.4 2.4 collective-permute-start.98
  578.7 2.3 collective-permute-start.99
  585.9 4.9 collective-permute-done.88
  595.1 2.4 collective-permute-start.92
  604.6 4.8 collective-permute-done.92
  620.5 5.9 all-to-all-start.4
  626.5 3.2 convolution_add_fusion.1
  629.7 3.8 all-to-all-done.4
  636.3 2.9 all-to-all-start.5
  639.2 7.8 %multiply_subtract_fusion = (f32[956,768]{1,0:T(8,128)}, f32[956,768]{1,0:T(8,128)}, f32[956,768]{1,0:T(8,128)}) fusion(f32[956,768]{1,0:T(8,128)} %param.38, f32[956,768]{1,0:T(8,128)} %convolution_add_fusion.1, f32[]{:T(128)} %div.169, f32[956,768]{1,0:T(8,128)} %param.39, f32[956,768]{1,0:T(8,128)} %param.40), kind=kLoop, calls=%fused_computation.62 | loop fusion | flops 11747328 | bytes 20557828 | tf_op jit(solution)/shard_map/sub | solution.py:652
  649.0 4.4 shard_map.495
  (785 shorter events, 264.3 us)
Async XLA Ops:
  11.3 21.5 %all-to-all-start = ((s32[32,16,128]{2,1,0:T(8,128)}), s32[32,16,128]{2,1,0:T(8,128)S(1)}, u32[]{:S(2)}, u32[]{:S(2)}) async-start(s32[32,16,128]{2,1,0:T(8,128)} %broadcast_in_dim.129), calls=%async_computation.1 | async-start | bytes 524288 | tf_op jit(solution)/shard_map/all_to_all | solution.py:855
  22.2 26.6 %collective-permute-start.7 = (bf16[24,2816]{1,0:T(8,128)(2,1)S(1)}, bf16[24,2816]{1,0:T(8,128)(2,1)S(1)}, u32[]{:S(2)}, u32[]{:S(2)}) collective-permute-start(bf16[24,2816]{1,0:T(8,128)(2,1)S(1)} %constant_dynamic-update-slice_fusion), channel_id=1, source_target_pairs={{0,1},{1,0},{2,3},{3,2},{4,5},{5,4},{6,7},{7,6},{8,9},{9,8},{10,11... | collective-permute-start | bytes 405512 | tf_op jit(solution)/shard_map/ppermute | solution.py:153
  24.0 24.9 %collective-permute-start.8 = (bf16[24,2816]{1,0:T(8,128)(2,1)S(1)}, bf16[24,2816]{1,0:T(8,128)(2,1)S(1)}, u32[]{:S(2)}, u32[]{:S(2)}) collective-permute-start(bf16[24,2816]{1,0:T(8,128)(2,1)S(1)} %constant_dynamic-update-slice_fusion), channel_id=1, source_target_pairs={{0,2},{1,3},{2,0},{3,1},{4,6},{5,7},{6,4},{7,5},{8,10},{9,11},{10,... | collective-permute-start | bytes 405512 | tf_op jit(solution)/shard_map/ppermute | solution.py:153
  26.4 22.5 %collective-permute-start.9 = (bf16[24,2816]{1,0:T(8,128)(2,1)S(1)}, bf16[24,2816]{1,0:T(8,128)(2,1)}, u32[]{:S(2)}, u32[]{:S(2)}) collective-permute-start(bf16[24,2816]{1,0:T(8,128)(2,1)S(1)} %constant_dynamic-update-slice_fusion), channel_id=1, source_target_pairs={{0,3},{1,2},{2,1},{3,0},{4,7},{5,6},{6,5},{7,4},{8,11},{9,10},{10,... | collective-permute-start | bytes 405512 | tf_op jit(solution)/shard_map/ppermute | solution.py:153
  58.6 19.1 %collective-permute-start.12 = (bf16[2,4,24,1408]{3,2,1,0:T(8,128)(2,1)S(1)}, bf16[2,4,24,1408]{3,2,1,0:T(8,128)(2,1)S(1)}, u32[]{:S(2)}, u32[]{:S(2)}) collective-permute-start(bf16[2,4,24,1408]{3,2,1,0:T(8,128)(2,1)S(1)} %pad_maximum_fusion.11.refs_0_), channel_id=1, source_target_pairs={{0,16},{4,20},{8,24},{12,28},{16,0},{20,4},{24,8},{28,12},{1,17},{... | collective-permute-start | bytes 1622024 | tf_op jit(solution)/shard_map/ppermute | solution.py:102
  60.1 18.1 %collective-permute-start.15 = (bf16[2,4,24,1408]{3,2,1,0:T(8,128)(2,1)S(1)}, bf16[2,4,24,1408]{3,2,1,0:T(8,128)(2,1)S(1)}, u32[]{:S(2)}, u32[]{:S(2)}) collective-permute-start(bf16[2,4,24,1408]{3,2,1,0:T(8,128)(2,1)S(1)} %pad_maximum_fusion.12.refs_4_), channel_id=1, source_target_pairs={{0,8},{4,12},{8,0},{12,4},{16,24},{20,28},{24,16},{28,20},{1,9},{5... | collective-permute-start | bytes 1622024 | tf_op jit(solution)/shard_map/ppermute | solution.py:102
  60.7 16.9 %collective-permute-start.3 = (bf16[1,4,96,384]{3,2,1,0:T(8,128)(2,1)S(1)}, bf16[1,4,96,384]{3,2,1,0:T(8,128)(2,1)S(1)}, u32[]{:S(2)}, u32[]{:S(2)}) collective-permute-start(bf16[1,4,96,384]{3,2,1,0:T(8,128)(2,1)S(1)} %maximum_bitcast_fusion.6), channel_id=1, source_target_pairs={{0,8},{4,12},{8,0},{12,4},{16,24},{20,28},{24,16},{28,20},{1,9},{5... | collective-permute-start | bytes 884744 | tf_op jit(solution)/shard_map/ppermute | solution.py:102
  62.7 15.6 %collective-permute-start.4 = (bf16[1,4,96,384]{3,2,1,0:T(8,128)(2,1)S(1)}, bf16[1,4,96,384]{3,2,1,0:T(8,128)(2,1)S(1)}, u32[]{:S(2)}, u32[]{:S(2)}) collective-permute-start(bf16[1,4,96,384]{3,2,1,0:T(8,128)(2,1)S(1)} %maximum_bitcast_fusion.7), channel_id=1, source_target_pairs={{0,16},{4,20},{8,24},{12,28},{16,0},{20,4},{24,8},{28,12},{1,17},{... | collective-permute-start | bytes 884744 | tf_op jit(solution)/shard_map/ppermute | solution.py:102
  63.3 15.7 %collective-permute-start.13 = (bf16[2,4,24,1408]{3,2,1,0:T(8,128)(2,1)S(1)}, bf16[2,4,24,1408]{3,2,1,0:T(8,128)(2,1)S(1)}, u32[]{:S(2)}, u32[]{:S(2)}) collective-permute-start(bf16[2,4,24,1408]{3,2,1,0:T(8,128)(2,1)S(1)} %pad_maximum_fusion.11.refs_0_), channel_id=1, source_target_pairs={{0,4},{4,0},{8,12},{12,8},{16,20},{20,16},{24,28},{28,24},{1,5},{5... | collective-permute-start | bytes 1622024 | tf_op jit(solution)/shard_map/ppermute | solution.py:102
  78.4 15.7 %collective-permute-start.5 = (bf16[2,4,96,384]{3,2,1,0:T(8,128)(2,1)S(1)}, bf16[2,4,96,384]{3,2,1,0:T(8,128)(2,1)S(1)}, u32[]{:S(2)}, u32[]{:S(2)}) collective-permute-start(bf16[2,4,96,384]{3,2,1,0:T(8,128)(2,1)S(1)} %pad_maximum_fusion.9.refs_0_), channel_id=1, source_target_pairs={{0,16},{4,20},{8,24},{12,28},{16,0},{20,4},{24,8},{28,12},{1,17},{... | collective-permute-start | bytes 1769480 | tf_op jit(solution)/shard_map/ppermute | solution.py:102
  79.1 15.5 %collective-permute-start.6 = (bf16[2,4,96,384]{3,2,1,0:T(8,128)(2,1)S(1)}, bf16[2,4,96,384]{3,2,1,0:T(8,128)(2,1)S(1)}, u32[]{:S(2)}, u32[]{:S(2)}) collective-permute-start(bf16[2,4,96,384]{3,2,1,0:T(8,128)(2,1)S(1)} %pad_maximum_fusion.10.refs_4_), channel_id=1, source_target_pairs={{0,8},{4,12},{8,0},{12,4},{16,24},{20,28},{24,16},{28,20},{1,9},{5... | collective-permute-start | bytes 1769480 | tf_op jit(solution)/shard_map/ppermute | solution.py:102
  79.8 21.9 %collective-permute-start.22 = (bf16[24,3840]{1,0:T(8,128)(2,1)S(1)}, bf16[24,3840]{1,0:T(8,128)(2,1)S(1)}, u32[]{:S(2)}, u32[]{:S(2)}) collective-permute-start(bf16[24,3840]{1,0:T(8,128)(2,1)S(1)} %constant_dynamic-update-slice_fusion.2), channel_id=1, source_target_pairs={{0,1},{1,0},{2,3},{3,2},{4,5},{5,4},{6,7},{7,6},{8,9},{9,8},{10,11... | collective-permute-start | bytes 552968 | tf_op jit(solution)/shard_map/ppermute | solution.py:153
  84.9 19.2 %collective-permute-start.23 = (bf16[24,3840]{1,0:T(8,128)(2,1)S(1)}, bf16[24,3840]{1,0:T(8,128)(2,1)}, u32[]{:S(2)}, u32[]{:S(2)}) collective-permute-start(bf16[24,3840]{1,0:T(8,128)(2,1)S(1)} %constant_dynamic-update-slice_fusion.2), channel_id=1, source_target_pairs={{0,2},{1,3},{2,0},{3,1},{4,6},{5,7},{6,4},{7,5},{8,10},{9,11},{10,... | collective-permute-start | bytes 552968 | tf_op jit(solution)/shard_map/ppermute | solution.py:153
  84.9 19.2 %collective-permute-start.24 = (bf16[24,3840]{1,0:T(8,128)(2,1)S(1)}, bf16[24,3840]{1,0:T(8,128)(2,1)}, u32[]{:S(2)}, u32[]{:S(2)}) collective-permute-start(bf16[24,3840]{1,0:T(8,128)(2,1)S(1)} %constant_dynamic-update-slice_fusion.2), channel_id=1, source_target_pairs={{0,3},{1,2},{2,1},{3,0},{4,7},{5,6},{6,5},{7,4},{8,11},{9,10},{10,... | collective-permute-start | bytes 552968 | tf_op jit(solution)/shard_map/ppermute | solution.py:153
  96.4 24.7 %collective-permute-start.33 = (bf16[24,4608]{1,0:T(8,128)(2,1)}, bf16[24,4608]{1,0:T(8,128)(2,1)}, u32[]{:S(2)}, u32[]{:S(2)}) collective-permute-start(bf16[24,4608]{1,0:T(8,128)(2,1)} %constant_dynamic-update-slice_fusion.4), channel_id=1, source_target_pairs={{0,1},{1,0},{2,3},{3,2},{4,5},{5,4},{6,7},{7,6},{8,9},{9,8},{10,11... | collective-permute-start | bytes 663560 | tf_op jit(solution)/shard_map/ppermute | solution.py:153
  100.6 20.5 %collective-permute-start.34 = (bf16[24,4608]{1,0:T(8,128)(2,1)}, bf16[24,4608]{1,0:T(8,128)(2,1)}, u32[]{:S(2)}, u32[]{:S(2)}) collective-permute-start(bf16[24,4608]{1,0:T(8,128)(2,1)} %constant_dynamic-update-slice_fusion.4), channel_id=1, source_target_pairs={{0,2},{1,3},{2,0},{3,1},{4,6},{5,7},{6,4},{7,5},{8,10},{9,11},{10,... | collective-permute-start | bytes 663560 | tf_op jit(solution)/shard_map/ppermute | solution.py:153
  101.7 20.0 %collective-permute-start.35 = (bf16[24,4608]{1,0:T(8,128)(2,1)}, bf16[24,4608]{1,0:T(8,128)(2,1)}, u32[]{:S(2)}, u32[]{:S(2)}) collective-permute-start(bf16[24,4608]{1,0:T(8,128)(2,1)} %constant_dynamic-update-slice_fusion.4), channel_id=1, source_target_pairs={{0,3},{1,2},{2,1},{3,0},{4,7},{5,6},{6,5},{7,4},{8,11},{9,10},{10,... | collective-permute-start | bytes 663560 | tf_op jit(solution)/shard_map/ppermute | solution.py:153
  121.6 43.7 %collective-permute-start.27 = (bf16[2,4,24,1920]{3,2,1,0:T(8,128)(2,1)}, bf16[2,4,24,1920]{3,2,1,0:T(8,128)(2,1)}, u32[]{:S(2)}, u32[]{:S(2)}) collective-permute-start(bf16[2,4,24,1920]{3,2,1,0:T(8,128)(2,1)} %pad_maximum_fusion.5.refs_0_), channel_id=1, source_target_pairs={{0,16},{4,20},{8,24},{12,28},{16,0},{20,4},{24,8},{28,12},{1,17},{... | collective-permute-start | bytes 2211848 | tf_op jit(solution)/shard_map/ppermute | solution.py:102
  126.2 39.1 %collective-permute-start.28 = (bf16[2,4,24,1920]{3,2,1,0:T(8,128)(2,1)}, bf16[2,4,24,1920]{3,2,1,0:T(8,128)(2,1)}, u32[]{:S(2)}, u32[]{:S(2)}) collective-permute-start(bf16[2,4,24,1920]{3,2,1,0:T(8,128)(2,1)} %pad_maximum_fusion.6.refs_4_), channel_id=1, source_target_pairs={{0,8},{4,12},{8,0},{12,4},{16,24},{20,28},{24,16},{28,20},{1,9},{5... | collective-permute-start | bytes 2211848 | tf_op jit(solution)/shard_map/ppermute | solution.py:102
  127.7 26.5 %collective-permute-start.36 = (bf16[1,4,24,2304]{3,2,1,0:T(8,128)(2,1)}, bf16[1,4,24,2304]{3,2,1,0:T(8,128)(2,1)}, u32[]{:S(2)}, u32[]{:S(2)}) collective-permute-start(bf16[1,4,24,2304]{3,2,1,0:T(8,128)(2,1)} %maximum_bitcast_fusion), channel_id=1, source_target_pairs={{0,8},{4,12},{8,0},{12,4},{16,24},{20,28},{24,16},{28,20},{1,9},{5... | collective-permute-start | bytes 1327112 | tf_op jit(solution)/shard_map/ppermute | solution.py:102
  128.3 27.2 %collective-permute-start.37 = (bf16[1,4,24,2304]{3,2,1,0:T(8,128)(2,1)}, bf16[1,4,24,2304]{3,2,1,0:T(8,128)(2,1)}, u32[]{:S(2)}, u32[]{:S(2)}) collective-permute-start(bf16[1,4,24,2304]{3,2,1,0:T(8,128)(2,1)} %maximum_bitcast_fusion.1), channel_id=1, source_target_pairs={{0,16},{4,20},{8,24},{12,28},{16,0},{20,4},{24,8},{28,12},{1,17},{... | collective-permute-start | bytes 1327112 | tf_op jit(solution)/shard_map/ppermute | solution.py:102
  158.0 20.5 %collective-permute-start.38 = (bf16[2,4,24,2304]{3,2,1,0:T(8,128)(2,1)S(1)}, bf16[2,4,24,2304]{3,2,1,0:T(8,128)(2,1)S(1)}, u32[]{:S(2)}, u32[]{:S(2)}) collective-permute-start(bf16[2,4,24,2304]{3,2,1,0:T(8,128)(2,1)S(1)} %pad_maximum_fusion.3.refs_0_), channel_id=1, source_target_pairs={{0,16},{4,20},{8,24},{12,28},{16,0},{20,4},{24,8},{28,12},{1,17},{... | collective-permute-start | bytes 2654216 | tf_op jit(solution)/shard_map/ppermute | solution.py:102
  160.7 37.6 %collective-permute-start.39 = (bf16[2,4,24,2304]{3,2,1,0:T(8,128)(2,1)}, bf16[2,4,24,2304]{3,2,1,0:T(8,128)(2,1)}, u32[]{:S(2)}, u32[]{:S(2)}) collective-permute-start(bf16[2,4,24,2304]{3,2,1,0:T(8,128)(2,1)} %pad_maximum_fusion.4.refs_4_), channel_id=1, source_target_pairs={{0,8},{4,12},{8,0},{12,4},{16,24},{20,28},{24,16},{28,20},{1,9},{5... | collective-permute-start | bytes 2654216 | tf_op jit(solution)/shard_map/ppermute | solution.py:102
  165.3 33.5 %collective-permute-start.29 = (bf16[2,4,24,1920]{3,2,1,0:T(8,128)(2,1)}, bf16[2,4,24,1920]{3,2,1,0:T(8,128)(2,1)}, u32[]{:S(2)}, u32[]{:S(2)}) collective-permute-start(bf16[2,4,24,1920]{3,2,1,0:T(8,128)(2,1)} %pad_maximum_fusion.5.refs_0_), channel_id=1, source_target_pairs={{0,4},{4,0},{8,12},{12,8},{16,20},{20,16},{24,28},{28,24},{1,5},{5... | collective-permute-start | bytes 2211848 | tf_op jit(solution)/shard_map/ppermute | solution.py:102
  165.4 33.5 %collective-permute-start.30 = (bf16[2,4,24,1920]{3,2,1,0:T(8,128)(2,1)}, bf16[2,4,24,1920]{3,2,1,0:T(8,128)(2,1)}, u32[]{:S(2)}, u32[]{:S(2)}) collective-permute-start(bf16[2,4,24,1920]{3,2,1,0:T(8,128)(2,1)} %collective-permute-done.27.refs_1_), channel_id=1, source_target_pairs={{0,4},{4,0},{8,12},{12,8},{16,20},{20,16},{24,28},{28,24},{1,5},{5... | collective-permute-start | bytes 2211848 | tf_op jit(solution)/shard_map/ppermute | solution.py:102
  165.9 33.5 %collective-permute-start.31 = (bf16[2,4,24,1920]{3,2,1,0:T(8,128)(2,1)}, bf16[2,4,24,1920]{3,2,1,0:T(8,128)(2,1)}, u32[]{:S(2)}, u32[]{:S(2)}) collective-permute-start(bf16[2,4,24,1920]{3,2,1,0:T(8,128)(2,1)} %pad_maximum_fusion.6.refs_4_), channel_id=1, source_target_pairs={{0,4},{4,0},{8,12},{12,8},{16,20},{20,16},{24,28},{28,24},{1,5},{5... | collective-permute-start | bytes 2211848 | tf_op jit(solution)/shard_map/ppermute | solution.py:102
  179.4 20.1 %collective-permute-start.32 = (bf16[2,4,24,1920]{3,2,1,0:T(8,128)(2,1)}, bf16[2,4,24,1920]{3,2,1,0:T(8,128)(2,1)}, u32[]{:S(2)}, u32[]{:S(2)}) collective-permute-start(bf16[2,4,24,1920]{3,2,1,0:T(8,128)(2,1)} %collective-permute-done.28.refs_5_), channel_id=1, source_target_pairs={{0,4},{4,0},{8,12},{12,8},{16,20},{20,16},{24,28},{28,24},{1,5},{5... | collective-permute-start | bytes 2211848 | tf_op jit(solution)/shard_map/ppermute | solution.py:102
  198.3 16.8 %collective-permute-start.40 = (bf16[2,4,24,2304]{3,2,1,0:T(8,128)(2,1)S(1)}, bf16[2,4,24,2304]{3,2,1,0:T(8,128)(2,1)S(1)}, u32[]{:S(2)}, u32[]{:S(2)}) collective-permute-start(bf16[2,4,24,2304]{3,2,1,0:T(8,128)(2,1)S(1)} %copy-done.10), channel_id=1, source_target_pairs={{0,4},{4,0},{8,12},{12,8},{16,20},{20,16},{24,28},{28,24},{1,5},{5... | collective-permute-start | bytes 2654216 | tf_op jit(solution)/shard_map/ppermute | solution.py:102
  198.8 16.2 %collective-permute-start.41 = (bf16[2,4,24,2304]{3,2,1,0:T(8,128)(2,1)S(1)}, bf16[2,4,24,2304]{3,2,1,0:T(8,128)(2,1)S(1)}, u32[]{:S(2)}, u32[]{:S(2)}) collective-permute-start(bf16[2,4,24,2304]{3,2,1,0:T(8,128)(2,1)S(1)} %copy-done.15), channel_id=1, source_target_pairs={{0,4},{4,0},{8,12},{12,8},{16,20},{20,16},{24,28},{28,24},{1,5},{5... | collective-permute-start | bytes 2654216 | tf_op jit(solution)/shard_map/ppermute | solution.py:102
  198.9 16.1 %collective-permute-start.42 = (bf16[2,4,24,2304]{3,2,1,0:T(8,128)(2,1)}, bf16[2,4,24,2304]{3,2,1,0:T(8,128)(2,1)S(1)}, u32[]{:S(2)}, u32[]{:S(2)}) collective-permute-start(bf16[2,4,24,2304]{3,2,1,0:T(8,128)(2,1)} %pad_maximum_fusion.4.refs_4_), channel_id=1, source_target_pairs={{0,4},{4,0},{8,12},{12,8},{16,20},{20,16},{24,28},{28,24},{1,5},{5... | collective-permute-start | bytes 2654216 | tf_op jit(solution)/shard_map/ppermute | solution.py:102
  199.4 15.7 %collective-permute-start.43 = (bf16[2,4,24,2304]{3,2,1,0:T(8,128)(2,1)}, bf16[2,4,24,2304]{3,2,1,0:T(8,128)(2,1)S(1)}, u32[]{:S(2)}, u32[]{:S(2)}) collective-permute-start(bf16[2,4,24,2304]{3,2,1,0:T(8,128)(2,1)} %collective-permute-done.39.refs_5_), channel_id=1, source_target_pairs={{0,4},{4,0},{8,12},{12,8},{16,20},{20,16},{24,28},{28,24},{1,5},{5... | collective-permute-start | bytes 2654216 | tf_op jit(solution)/shard_map/ppermute | solution.py:102
  230.8 15.6 %collective-permute-start.45 = (bf16[112,768]{1,0:T(8,128)(2,1)S(1)}, bf16[112,768]{1,0:T(8,128)(2,1)S(1)}, u32[]{:S(2)}, u32[]{:S(2)}) collective-permute-start(bf16[112,768]{1,0:T(8,128)(2,1)S(1)} %add_convert_fusion.2), channel_id=1, source_target_pairs={{0,2},{1,3},{2,0},{3,1},{4,6},{5,7},{6,4},{7,5},{8,10},{9,11},{10,... | collective-permute-start | bytes 516104 | tf_op jit(solution)/shard_map/ppermute | solution.py:153
  257.9 15.9 %collective-permute-start.49 = (bf16[2,4,112,384]{3,2,1,0:T(8,128)(2,1)}, bf16[2,4,112,384]{3,2,1,0:T(8,128)(2,1)}, u32[]{:S(2)}, u32[]{:S(2)}) collective-permute-start(bf16[2,4,112,384]{3,2,1,0:T(8,128)(2,1)} %pad_maximum_fusion.7.refs_0_), channel_id=1, source_target_pairs={{0,16},{4,20},{8,24},{12,28},{16,0},{20,4},{24,8},{28,12},{1,17},{... | collective-permute-start | bytes 2064392 | tf_op jit(solution)/shard_map/ppermute | solution.py:102
  258.5 15.6 %collective-permute-start.52 = (bf16[2,4,112,384]{3,2,1,0:T(8,128)(2,1)}, bf16[2,4,112,384]{3,2,1,0:T(8,128)(2,1)}, u32[]{:S(2)}, u32[]{:S(2)}) collective-permute-start(bf16[2,4,112,384]{3,2,1,0:T(8,128)(2,1)} %pad_maximum_fusion.8.refs_4_), channel_id=1, source_target_pairs={{0,8},{4,12},{8,0},{12,4},{16,24},{20,28},{24,16},{28,20},{1,9},{5... | collective-permute-start | bytes 2064392 | tf_op jit(solution)/shard_map/ppermute | solution.py:102
  259.7 19.3 %collective-permute-start.50 = (bf16[2,4,112,384]{3,2,1,0:T(8,128)(2,1)}, bf16[2,4,112,384]{3,2,1,0:T(8,128)(2,1)}, u32[]{:S(2)}, u32[]{:S(2)}) collective-permute-start(bf16[2,4,112,384]{3,2,1,0:T(8,128)(2,1)} %pad_maximum_fusion.7.refs_0_), channel_id=1, source_target_pairs={{0,4},{4,0},{8,12},{12,8},{16,20},{20,16},{24,28},{28,24},{1,5},{5... | collective-permute-start | bytes 2064392 | tf_op jit(solution)/shard_map/ppermute | solution.py:102
  259.7 19.3 %collective-permute-start.53 = (bf16[2,4,112,384]{3,2,1,0:T(8,128)(2,1)}, bf16[2,4,112,384]{3,2,1,0:T(8,128)(2,1)}, u32[]{:S(2)}, u32[]{:S(2)}) collective-permute-start(bf16[2,4,112,384]{3,2,1,0:T(8,128)(2,1)} %pad_maximum_fusion.8.refs_4_), channel_id=1, source_target_pairs={{0,4},{4,0},{8,12},{12,8},{16,20},{20,16},{24,28},{28,24},{1,5},{5... | collective-permute-start | bytes 2064392 | tf_op jit(solution)/shard_map/ppermute | solution.py:102
  294.0 21.1 %all-to-all-start.1 = ((f32[32,28,128]{2,1,0:T(8,128)}), f32[32,28,128]{2,1,0:T(8,128)}, u32[]{:S(2)}, u32[]{:S(2)}) async-start(f32[32,28,128]{2,1,0:T(8,128)} %broadcast_in_dim.235), calls=%async_computation.2 | async-start | bytes 1048576 | tf_op jit(solution)/shard_map/all_to_all | solution.py:355
  341.1 18.1 %collective-permute-start.59 = (bf16[2,4,112,384]{3,2,1,0:T(8,128)(2,1)}, bf16[2,4,112,384]{3,2,1,0:T(8,128)(2,1)}, u32[]{:S(2)}, u32[]{:S(2)}) collective-permute-start(bf16[2,4,112,384]{3,2,1,0:T(8,128)(2,1)} %fusion.48), channel_id=1, source_target_pairs={{0,8},{4,12},{8,0},{12,4},{16,24},{20,28},{24,16},{28,20},{1,9},{5... | collective-permute-start | bytes 2064392 | tf_op jit(solution)/shard_map/ppermute | solution.py:102
  343.9 18.4 %collective-permute-start.56 = (bf16[2,4,112,384]{3,2,1,0:T(8,128)(2,1)}, bf16[2,4,112,384]{3,2,1,0:T(8,128)(2,1)}, u32[]{:S(2)}, u32[]{:S(2)}) collective-permute-start(bf16[2,4,112,384]{3,2,1,0:T(8,128)(2,1)} %fusion.49), channel_id=1, source_target_pairs={{0,16},{4,20},{8,24},{12,28},{16,0},{20,4},{24,8},{28,12},{1,17},{... | collective-permute-start | bytes 2064392 | tf_op jit(solution)/shard_map/ppermute | solution.py:102
  353.9 28.0 %all-to-all-start.2 = ((f32[32,8,128]{2,1,0:T(8,128)}), f32[32,8,128]{2,1,0:T(8,128)}, u32[]{:S(2)}, u32[]{:S(2)}) async-start(f32[32,8,128]{2,1,0:T(8,128)} %broadcast_in_dim.237), calls=%async_computation.3 | async-start | bytes 262144 | tf_op jit(solution)/shard_map/all_to_all | solution.py:355
  376.9 15.3 %collective-permute-start.62 = (bf16[112,768]{1,0:T(8,128)(2,1)}, bf16[112,768]{1,0:T(8,128)(2,1)}, u32[]{:S(2)}, u32[]{:S(2)}) collective-permute-start(bf16[112,768]{1,0:T(8,128)(2,1)} %get-tuple-element.542), channel_id=1, source_target_pairs={{0,2},{1,3},{2,0},{3,1},{4,6},{5,7},{6,4},{7,5},{8,10},{9,11},{10,... | collective-permute-start | bytes 516104 | tf_op jit(solution)/shard_map/ppermute | solution.py:153
  427.6 23.9 %collective-permute-start.64 = (bf16[2,2,4,24,3072]{4,3,2,1,0:T(8,128)(2,1)}, bf16[2,2,4,24,3072]{4,3,2,1,0:T(8,128)(2,1)}, u32[]{:S(2)}, u32[]{:S(2)}) collective-permute-start(bf16[2,2,4,24,3072]{4,3,2,1,0:T(8,128)(2,1)} %fusion.35), channel_id=1, source_target_pairs={{0,4},{4,0},{8,12},{12,8},{16,20},{20,16},{24,28},{28,24},{1,5},{5... | collective-permute-start | bytes 7077896 | tf_op jit(solution)/shard_map/ppermute | solution.py:102
  440.9 14.1 %collective-permute-start.66 = (bf16[2,2,4,24,3072]{4,3,2,1,0:T(8,128)(2,1)}, bf16[2,2,4,24,3072]{4,3,2,1,0:T(8,128)(2,1)}, u32[]{:S(2)}, u32[]{:S(2)}) collective-permute-start(bf16[2,2,4,24,3072]{4,3,2,1,0:T(8,128)(2,1)} %fusion.36), channel_id=1, source_target_pairs={{0,4},{4,0},{8,12},{12,8},{16,20},{20,16},{24,28},{28,24},{1,5},{5... | collective-permute-start | bytes 7077896 | tf_op jit(solution)/shard_map/ppermute | solution.py:102
  453.8 31.5 %collective-permute-start.68 = (bf16[2,4,24,3072]{3,2,1,0:T(8,128)(2,1)S(1)}, bf16[2,4,24,3072]{3,2,1,0:T(8,128)(2,1)S(1)}, u32[]{:S(2)}, u32[]{:S(2)}) collective-permute-start(bf16[2,4,24,3072]{3,2,1,0:T(8,128)(2,1)S(1)} %fusion.38), channel_id=1, source_target_pairs={{0,16},{4,20},{8,24},{12,28},{16,0},{20,4},{24,8},{28,12},{1,17},{... | collective-permute-start | bytes 3538952 | tf_op jit(solution)/shard_map/ppermute | solution.py:102
  457.3 32.0 %collective-permute-start.70 = (bf16[2,4,24,3072]{3,2,1,0:T(8,128)(2,1)S(1)}, bf16[2,4,24,3072]{3,2,1,0:T(8,128)(2,1)S(1)}, u32[]{:S(2)}, u32[]{:S(2)}) collective-permute-start(bf16[2,4,24,3072]{3,2,1,0:T(8,128)(2,1)S(1)} %fusion.37), channel_id=1, source_target_pairs={{0,8},{4,12},{8,0},{12,4},{16,24},{20,28},{24,16},{28,20},{1,9},{5... | collective-permute-start | bytes 3538952 | tf_op jit(solution)/shard_map/ppermute | solution.py:102
  496.3 27.0 %collective-permute-start.76 = (bf16[2,2,4,24,1536]{4,3,2,1,0:T(8,128)(2,1)S(1)}, bf16[2,2,4,24,1536]{4,3,2,1,0:T(8,128)(2,1)S(1)}, u32[]{:S(2)}, u32[]{:S(2)}) collective-permute-start(bf16[2,2,4,24,1536]{4,3,2,1,0:T(8,128)(2,1)S(1)} %fusion.50), channel_id=1, source_target_pairs={{0,4},{4,0},{8,12},{12,8},{16,20},{20,16},{24,28},{28,24},{1,5},{5... | collective-permute-start | bytes 3538952 | tf_op jit(solution)/shard_map/ppermute | solution.py:102
  496.4 18.1 %collective-permute-start.77 = (bf16[2,2,4,24,768]{4,3,2,1,0:T(8,128)(2,1)S(1)}, bf16[2,2,4,24,768]{4,3,2,1,0:T(8,128)(2,1)S(1)}, u32[]{:S(2)}, u32[]{:S(2)}) collective-permute-start(bf16[2,2,4,24,768]{4,3,2,1,0:T(8,128)(2,1)S(1)} %fusion.82), channel_id=1, source_target_pairs={{0,4},{4,0},{8,12},{12,8},{16,20},{20,16},{24,28},{28,24},{1,5},{5... | collective-permute-start | bytes 1769480 | tf_op jit(solution)/shard_map/ppermute | solution.py:102
  501.0 14.8 %collective-permute-start.78 = (bf16[2,2,4,24,768]{4,3,2,1,0:T(8,128)(2,1)}, bf16[2,2,4,24,768]{4,3,2,1,0:T(8,128)(2,1)S(1)}, u32[]{:S(2)}, u32[]{:S(2)}) collective-permute-start(bf16[2,2,4,24,768]{4,3,2,1,0:T(8,128)(2,1)} %fusion.83), channel_id=1, source_target_pairs={{0,4},{4,0},{8,12},{12,8},{16,20},{20,16},{24,28},{28,24},{1,5},{5... | collective-permute-start | bytes 1769480 | tf_op jit(solution)/shard_map/ppermute | solution.py:102
  501.2 22.2 %collective-permute-start.72 = (bf16[4,24,3072]{2,1,0:T(8,128)(2,1)}, bf16[4,24,3072]{2,1,0:T(8,128)(2,1)}, u32[]{:S(2)}, u32[]{:S(2)}) collective-permute-start(bf16[4,24,3072]{2,1,0:T(8,128)(2,1)} %fusion.61), channel_id=1, source_target_pairs={{0,8},{4,12},{8,0},{12,4},{16,24},{20,28},{24,16},{28,20},{1,9},{5... | collective-permute-start | bytes 1769480 | tf_op jit(solution)/shard_map/ppermute | solution.py:102
  502.5 20.9 %collective-permute-start.74 = (bf16[4,24,3072]{2,1,0:T(8,128)(2,1)}, bf16[4,24,3072]{2,1,0:T(8,128)(2,1)}, u32[]{:S(2)}, u32[]{:S(2)}) collective-permute-start(bf16[4,24,3072]{2,1,0:T(8,128)(2,1)} %fusion.60), channel_id=1, source_target_pairs={{0,16},{4,20},{8,24},{12,28},{16,0},{20,4},{24,8},{28,12},{1,17},{... | collective-permute-start | bytes 1769480 | tf_op jit(solution)/shard_map/ppermute | solution.py:102
  521.3 24.5 %collective-permute-start.83 = (bf16[2,4,24,768]{3,2,1,0:T(8,128)(2,1)}, bf16[2,4,24,768]{3,2,1,0:T(8,128)(2,1)}, u32[]{:S(2)}, u32[]{:S(2)}) collective-permute-start(bf16[2,4,24,768]{3,2,1,0:T(8,128)(2,1)} %fusion.91), channel_id=1, source_target_pairs={{0,8},{4,12},{8,0},{12,4},{16,24},{20,28},{24,16},{28,20},{1,9},{5... | collective-permute-start | bytes 884744 | tf_op jit(solution)/shard_map/ppermute | solution.py:102
  522.0 23.9 %collective-permute-start.84 = (bf16[2,4,24,768]{3,2,1,0:T(8,128)(2,1)}, bf16[2,4,24,768]{3,2,1,0:T(8,128)(2,1)}, u32[]{:S(2)}, u32[]{:S(2)}) collective-permute-start(bf16[2,4,24,768]{3,2,1,0:T(8,128)(2,1)} %fusion.90), channel_id=1, source_target_pairs={{0,8},{4,12},{8,0},{12,4},{16,24},{20,28},{24,16},{28,20},{1,9},{5... | collective-permute-start | bytes 884744 | tf_op jit(solution)/shard_map/ppermute | solution.py:102
  529.8 16.1 %collective-permute-start.82 = (bf16[2,4,24,1536]{3,2,1,0:T(8,128)(2,1)}, bf16[2,4,24,1536]{3,2,1,0:T(8,128)(2,1)}, u32[]{:S(2)}, u32[]{:S(2)}) collective-permute-start(bf16[2,4,24,1536]{3,2,1,0:T(8,128)(2,1)} %fusion.59), channel_id=1, source_target_pairs={{0,16},{4,20},{8,24},{12,28},{16,0},{20,4},{24,8},{28,12},{1,17},{... | collective-permute-start | bytes 1769480 | tf_op jit(solution)/shard_map/ppermute | solution.py:102
  531.8 20.7 %collective-permute-start.79 = (bf16[2,2,4,96,384]{4,3,2,1,0:T(8,128)(2,1)}, bf16[2,2,4,96,384]{4,3,2,1,0:T(8,128)(2,1)}, u32[]{:S(2)}, u32[]{:S(2)}) collective-permute-start(bf16[2,2,4,96,384]{4,3,2,1,0:T(8,128)(2,1)} %fusion.51), channel_id=1, source_target_pairs={{0,4},{4,0},{8,12},{12,8},{16,20},{20,16},{24,28},{28,24},{1,5},{5... | collective-permute-start | bytes 3538952 | tf_op jit(solution)/shard_map/ppermute | solution.py:102
  533.0 19.5 %collective-permute-start.80 = (bf16[2,2,4,96,384]{4,3,2,1,0:T(8,128)(2,1)}, bf16[2,2,4,96,384]{4,3,2,1,0:T(8,128)(2,1)}, u32[]{:S(2)}, u32[]{:S(2)}) collective-permute-start(bf16[2,2,4,96,384]{4,3,2,1,0:T(8,128)(2,1)} %fusion.52), channel_id=1, source_target_pairs={{0,4},{4,0},{8,12},{12,8},{16,20},{20,16},{24,28},{28,24},{1,5},{5... | collective-permute-start | bytes 3538952 | tf_op jit(solution)/shard_map/ppermute | solution.py:102
  540.9 61.8 %all-to-all-start.3 = ((bf16[4,24,7680]{2,1,0:T(8,128)(2,1)}), bf16[4,24,7680]{2,1,0:T(8,128)(2,1)S(1)}, u32[]{:S(2)}, u32[]{:S(2)}) async-start(bf16[4,24,7680]{2,1,0:T(8,128)(2,1)} %pad_maximum_fusion), calls=%async_computation.4 | async-start | bytes 2949120 | tf_op jit(solution)/shard_map/all_to_all | solution.py:157
  554.1 17.0 %collective-permute-start.85 = (bf16[2,4,96,384]{3,2,1,0:T(8,128)(2,1)S(1)}, bf16[2,4,96,384]{3,2,1,0:T(8,128)(2,1)S(1)}, u32[]{:S(2)}, u32[]{:S(2)}) collective-permute-start(bf16[2,4,96,384]{3,2,1,0:T(8,128)(2,1)S(1)} %fusion.54), channel_id=1, source_target_pairs={{0,16},{4,20},{8,24},{12,28},{16,0},{20,4},{24,8},{28,12},{1,17},{... | collective-permute-start | bytes 1769480 | tf_op jit(solution)/shard_map/ppermute | solution.py:102
  557.0 24.1 %collective-permute-start.87 = (bf16[2,4,96,384]{3,2,1,0:T(8,128)(2,1)S(1)}, bf16[2,4,96,384]{3,2,1,0:T(8,128)(2,1)S(1)}, u32[]{:S(2)}, u32[]{:S(2)}) collective-permute-start(bf16[2,4,96,384]{3,2,1,0:T(8,128)(2,1)S(1)} %fusion.53), channel_id=1, source_target_pairs={{0,8},{4,12},{8,0},{12,4},{16,24},{20,28},{24,16},{28,20},{1,9},{5... | collective-permute-start | bytes 1769480 | tf_op jit(solution)/shard_map/ppermute | solution.py:102
  558.4 20.3 %collective-permute-start.89 = (bf16[2,4,24,512]{3,2,1,0:T(8,128)(2,1)S(1)}, bf16[2,4,24,512]{3,2,1,0:T(8,128)(2,1)S(1)}, u32[]{:S(2)}, u32[]{:S(2)}) collective-permute-start(bf16[2,4,24,512]{3,2,1,0:T(8,128)(2,1)S(1)} %fusion.100), channel_id=1, source_target_pairs={{0,8},{4,12},{8,0},{12,4},{16,24},{20,28},{24,16},{28,20},{1,9},{5... | collective-permute-start | bytes 589832 | tf_op jit(solution)/shard_map/ppermute | solution.py:102
  574.3 24.9 %collective-permute-start.97 = (bf16[24,3072]{1,0:T(8,128)(2,1)}, bf16[24,3072]{1,0:T(8,128)(2,1)S(1)}, u32[]{:S(2)}, u32[]{:S(2)}) collective-permute-start(bf16[24,3072]{1,0:T(8,128)(2,1)} %get-tuple-element.546), channel_id=1, source_target_pairs={{0,1},{1,0},{2,3},{3,2},{4,5},{5,4},{6,7},{7,6},{8,9},{9,8},{10,11... | collective-permute-start | bytes 442376 | tf_op jit(solution)/shard_map/ppermute | solution.py:153
  576.4 23.9 %collective-permute-start.98 = (bf16[24,3072]{1,0:T(8,128)(2,1)}, bf16[24,3072]{1,0:T(8,128)(2,1)}, u32[]{:S(2)}, u32[]{:S(2)}) collective-permute-start(bf16[24,3072]{1,0:T(8,128)(2,1)} %get-tuple-element.545), channel_id=1, source_target_pairs={{0,2},{1,3},{2,0},{3,1},{4,6},{5,7},{6,4},{7,5},{8,10},{9,11},{10,... | collective-permute-start | bytes 442376 | tf_op jit(solution)/shard_map/ppermute | solution.py:153
  578.7 21.5 %collective-permute-start.99 = (bf16[24,3072]{1,0:T(8,128)(2,1)}, bf16[24,3072]{1,0:T(8,128)(2,1)}, u32[]{:S(2)}, u32[]{:S(2)}) collective-permute-start(bf16[24,3072]{1,0:T(8,128)(2,1)} %get-tuple-element.544), channel_id=1, source_target_pairs={{0,3},{1,2},{2,1},{3,0},{4,7},{5,6},{6,5},{7,4},{8,11},{9,10},{10,... | collective-permute-start | bytes 442376 | tf_op jit(solution)/shard_map/ppermute | solution.py:153
  595.1 14.3 %collective-permute-start.92 = (bf16[24,3584]{1,0:T(8,128)(2,1)}, bf16[24,3584]{1,0:T(8,128)(2,1)}, u32[]{:S(2)}, u32[]{:S(2)}) collective-permute-start(bf16[24,3584]{1,0:T(8,128)(2,1)} %get-tuple-element.539), channel_id=1, source_target_pairs={{0,2},{1,3},{2,0},{3,1},{4,6},{5,7},{6,4},{7,5},{8,10},{9,11},{10,... | collective-permute-start | bytes 516104 | tf_op jit(solution)/shard_map/ppermute | solution.py:153
  636.3 18.3 %all-to-all-start.5 = ((f32[32,4,128]{2,1,0:T(4,128)}), f32[32,4,128]{2,1,0:T(4,128)S(1)}, u32[]{:S(2)}, u32[]{:S(2)}) async-start(f32[32,4,128]{2,1,0:T(4,128)} %broadcast_in_dim.250), calls=%async_computation.6 | async-start | bytes 131072 | tf_op jit(solution)/shard_map/all_to_all | solution.py:355
  (200 other events, 1475.7 us)
